TPU v7x, 32 devices: a whole 2x2x4 slice. The times are simulated.
32 devices in a mesh: pole: 2 (over y), row: 4 (over x, core), col: 4 (over z).
Axes of the slice: x: 2, y: 2, z: 4, core: 2. Of those that a mesh axis runs over, the one named last changes fastest.
Arguments:
- green_top: bfloat16 [4096, 2048], P(('pole', 'col'), 'row'), parts along dimension 0, may hold values from -6 to 6
- factor_cols: bfloat16 [1024, 2048], P(('pole', 'row', 'col')), parts along dimension 0, may hold values from -0.1875 to 0.1875
- fill_blocks: int32 [4, 8], replicated, may hold values from 0 to 1, as said below
- diag_inverse: float32 [1024, 128], P(('pole', 'row')), parts along dimension 0, may hold values from -6 to 6
Outputs:
- green_cols: float32 [1024, 2048], P(('pole', 'row'), 'col'), parts along dimension 0
- green_diag: float32 [1024, 128], P(('pole', 'row')), parts along dimension 0
There are 2 independent parts, one for each index of `pole`. A program takes and returns all parts, laid end to end along the dimension named above; an argument that names none is the same for every part. Nothing has to cross between parts.
Inputs may be any that keep to these rules, and one draw needn't show every extreme that they name: `fill_blocks`: in every row, each aligned run of 8 // 4 blocks holds exactly half ones.
All inputs are finite; a program needn't handle non-finite values.
Results may differ from a plain program's by a relative error of at most 0.0003.
Values may be sent and summed in bfloat16 or wider, within the bound.
No kernel may reach another device: no remote copies, remote signals or barrier semaphores. Data moves between devices by JAX's collectives and lax.ppermute only.
A program may use at most 64 MiB of HBM per device.

v0:
```python
import jax
import jax.numpy as jnp
from jax import lax
from jax.sharding import PartitionSpec as P


def per_device(green_top, factor_cols, fill_blocks, diag_inverse):
    row_index = lax.axis_index("row")
    col_index = lax.axis_index("col")
    row_count = lax.axis_size("row")
    col_count = lax.axis_size("col")
    local_rows = factor_cols.shape[0]
    order = factor_cols.shape[1]
    block_cols = order // fill_blocks.shape[1]
    width_col = order // col_count
    width_row = order // row_count
    fill_row = lax.dynamic_index_in_dim(fill_blocks, row_index, 0, keepdims=False)
    fill_line = jnp.repeat(fill_row, block_cols)
    masked = factor_cols * fill_line.astype(jnp.bfloat16)[None, :]
    pieces = lax.all_to_all(masked, "row", split_axis=1, concat_axis=0, tiled=True)
    stacked = lax.all_gather(pieces, "col", axis=0, tiled=True)
    panel_rows = stacked.reshape(col_count, row_count, local_rows, width_row)
    panel_rows = panel_rows.transpose(1, 0, 2, 3).reshape(
        row_count * col_count * local_rows, width_row
    )
    panel_own = lax.all_to_all(masked, "col", split_axis=1, concat_axis=0, tiled=True)
    solved = -lax.psum_scatter(
        lax.dot_general(
            panel_rows, green_top, (((1,), (1,)), ((), ())), preferred_element_type=jnp.float32
        ),
        "row",
        scatter_dimension=0,
        tiled=True,
    )
    fill_cols = lax.dynamic_slice_in_dim(fill_line, col_index * width_col, width_col, 0)
    green_cols = solved * fill_cols.astype(jnp.float32)[None, :]
    partial_value = lax.dot_general(
        solved,
        panel_own.astype(jnp.float32),
        (((1,), (1,)), ((), ())),
        precision=lax.Precision.HIGHEST,
        preferred_element_type=jnp.float32,
    )
    total = lax.psum(partial_value, "col")
    return (green_cols, diag_inverse - total)


def solution(mesh):
    placed = (
        P(("pole", "col"), "row"),
        P(("pole", "row", "col"), None),
        P(),
        P(("pole", "row"), None),
    )
    return jax.shard_map(
        per_device,
        mesh=mesh,
        in_specs=placed,
        out_specs=(P(("pole", "row"), "col"), P(("pole", "row"), None)),
        check_vma=False,
    )
```

profile of v0, /device:TPU:0, one launch (start us, length us, event | category | flops | bytes accessed | tf_op | source)
XLA Modules:
  0.0 107.5 jit_solution(14876294678615729144)
XLA Ops:
  7.2 0.0 copy-start
  7.2 0.0 reduce-scatter.2.cloned.1.call-start
  7.2 0.7 dynamic-slice_bitcast_fusion
  8.0 0.1 broadcast_bitcast_fusion
  8.1 0.9 broadcast_multiply_fusion
  9.0 0.7 copy.16
  9.6 8.8 %all_to_all.35 = bf16[32,4,512]{2,0,1:T(8,128)(2,1)S(1)} all-to-all(bf16[32,4,512]{2,0,1:T(8,128)(2,1)} %bitcast.21), channel_id=1, replica_groups=mesh['pole'=2,'row'=4,'col'=4] {'row'}, dimensions={1} | all-to-all | bytes 262144 | tf_op jit(solution)/shard_map/all_to_all | solution.py:20
  18.5 16.2 %all_gather.3 = bf16[512,512]{1,0:T(8,128)(2,1)S(1)} all-gather(bf16[128,512]{1,0:T(8,128)(2,1)S(1)} %bitcast.25), channel_id=1, replica_groups=mesh['pole'=2,'row'=4,'col'=4] {'col'}, dimensions={0}, use_global_device_ids=true | all-gather | bytes 655360 | tf_op jit(solution)/shard_map/all_gather | solution.py:21
  34.7 0.0 copy-done
  34.7 1.4 %fusion.2 = f32[512,512]{1,0:T(8,128)} fusion(bf16[512,512]{1,0:T(8,128)(2,1)S(1)} %bitcast.23, bf16[512,512]{1,0:T(8,128)(2,1)S(1)} %copy-done), kind=kOutput, calls=%fused_computation.8 | convolution fusion | flops 268435456 | bytes 2097152 | tf_op jit(solution)/shard_map/dot_general | solution.py:28
  36.1 0.0 reduce-scatter.2.cloned.1.call-update
  36.2 5.4 %all-to-all-start.1 = ((bf16[32,4,512]{2,0,1:T(8,128)(2,1)}), bf16[32,4,512]{2,0,1:T(8,128)(2,1)S(1)}, u32[]{:S(2)}, u32[]{:S(2)}) async-start(bf16[32,4,512]{2,0,1:T(8,128)(2,1)} %bitcast.21), calls=%async_computation.2 | async-start | bytes 262144 | tf_op jit(solution)/shard_map/all_to_all | solution.py:26
  41.6 0.0 all-reduce.2.cloned.1.call-start
  41.6 0.1 dynamic-slice_convert_fusion
  41.6 5.8 %all-to-all-done.1 = bf16[32,4,512]{2,0,1:T(8,128)(2,1)S(1)} async-done(((bf16[32,4,512]{2,0,1:T(8,128)(2,1)}), bf16[32,4,512]{2,0,1:T(8,128)(2,1)S(1)}, u32[]{:S(2)}, u32[]{:S(2)}) %all-to-all-start.1) | async-done | bytes 131104 | tf_op jit(solution)/shard_map/all_to_all | solution.py:26
  47.5 14.7 %reduce-scatter.2.cloned.1.call-done = f32[128,512]{1,0:T(8,128)} async-done(((f32[512,512]{1,0:T(8,128)}), f32[128,512]{1,0:T(8,128)}) %reduce-scatter.2.cloned.1.call-update) | async-done | bytes 262160 | tf_op jit(solution)/shard_map/reduce_scatter | solution.py:27
  62.2 0.0 copy-start.1
  62.2 1.9 %fusion = f32[128,128]{1,0:T(8,128)} fusion(bf16[128,512]{1,0:T(8,128)(2,1)S(1)} %bitcast.24, f32[128,512]{1,0:T(8,128)} %reduce-scatter.2.cloned.1.call-done), kind=kOutput, calls=%fused_computation | convolution fusion | flops 100728832 | bytes 458752 | tf_op jit(solution)/shard_map/dot_general | solution.py:37
  64.1 0.0 all-reduce.2.cloned.1.call-update
  64.1 0.0 copy-done.1
  64.1 0.0 copy-start.2
  64.1 0.7 negate_multiply_fusion
  64.9 34.3 %all-reduce.2.cloned.1.call-done = f32[128,128]{1,0:T(8,128)} async-done(((f32[128,128]{1,0:T(8,128)}), f32[128,128]{1,0:T(8,128)}) %all-reduce.2.cloned.1.call-update) | async-done | bytes 65552 | tf_op jit(solution)/shard_map/psum | solution.py:44
  99.2 0.0 copy-done.2
  99.2 1.5 %sub.3 = f32[128,128]{1,0:T(8,128)} subtract(f32[128,128]{1,0:T(8,128)S(1)} %copy-done.2, f32[128,128]{1,0:T(8,128)} %all-reduce.2.cloned.1.call-done) | non-fusion elementwise | flops 16384 | bytes 196608 | tf_op jit(solution)/shard_map/sub | solution.py:45
  (3 shorter events, 0.1 us)
Async XLA Ops:
  7.2 27.5 %copy-start = (bf16[512,512]{1,0:T(8,128)(2,1)S(1)}, bf16[512,512]{1,0:T(8,128)(2,1)}, u32[]{:S(2)}) copy-start(bf16[512,512]{1,0:T(8,128)(2,1)} %param.4) | copy-start | bytes 1572868
  7.2 55.0 %reduce-scatter.2.cloned.1.call-start = ((), (), s32[]{:S(2)}) async-start(), calls=%async_computation.3 | async-start | bytes 1310720 | tf_op jit(solution)/shard_map/reduce_scatter | solution.py:27
  36.2 11.3 %all-to-all-start.1 = ((bf16[32,4,512]{2,0,1:T(8,128)(2,1)}), bf16[32,4,512]{2,0,1:T(8,128)(2,1)S(1)}, u32[]{:S(2)}, u32[]{:S(2)}) async-start(bf16[32,4,512]{2,0,1:T(8,128)(2,1)} %bitcast.21), calls=%async_computation.2 | async-start | bytes 262144 | tf_op jit(solution)/shard_map/all_to_all | solution.py:26
  41.6 57.6 %all-reduce.2.cloned.1.call-start = ((), (), s32[]{:S(2)}) async-start(), calls=%async_computation.4 | async-start | bytes 131072 | tf_op jit(solution)/shard_map/psum | solution.py:44
  62.2 2.0 %copy-start.1 = (f32[128,512]{1,0:T(8,128)S(1)}, f32[128,512]{1,0:T(8,128)}, u32[]{:S(2)}) copy-start(f32[128,512]{1,0:T(8,128)} %reduce-scatter.2.cloned.1.call-done) | copy-start | bytes 786436
  64.1 35.0 %copy-start.2 = (f32[128,128]{1,0:T(8,128)S(1)}, f32[128,128]{1,0:T(8,128)}, u32[]{:S(2)}) copy-start(f32[128,128]{1,0:T(8,128)} %param.7) | copy-start | bytes 196612
Sparse Core Ops, SparseCore 0:
  36.3 25.8 reduce-scatter.1
  65.2 33.9 all-reduce.1
where the time goes:
time: 108 us; the launch traced here: 107 us
  waiting for transfers between devices  54.8 us (51%)
  blocking collectives  25 us (23%)
  between operations  14.1 us (13%)
  starting transfers between devices  5.44 us (5%)
  matrix products  3.37 us (3%)
  other arithmetic  3.21 us (3%)
  local copies, waits for them, and re-layouts  1.54 us (1%)
    psum x1, waiting for transfers between devices, per_device(): total = lax.psum(partial_value, 'col')  34.3 us
    all_gather x1, blocking collectives, per_device(): stacked = lax.all_gather(pieces, 'col', axis=0, tiled=True)  16.2 us
    reduce_scatter x1, waiting for transfers between devices, per_device(): lax.psum_scatter(lax.dot_general(panel_rows, green_top, (((1,), (1,)), ((...  14.7 us
    all_to_all x1, blocking collectives, per_device(): lax.all_to_all(masked, 'row', split_axis=1, concat_axis=0, tiled=True)  8.84 us
    all_to_all x1, waiting for transfers between devices, per_device(): lax.all_to_all(masked, 'col', split_axis=1, concat_axis=0, tiled=True)  5.84 us
    all_to_all x1, starting transfers between devices, per_device(): lax.all_to_all(masked, 'col', split_axis=1, concat_axis=0, tiled=True)  5.4 us
  transfers between devices with their start and end apart: 3, of which 3 were waited for; matrix products, arithmetic and copies ran while one was open for 1% of the time, Pallas kernels for 0%

commit v1 on v0

v1 whole, which is shorter than its diff:
```python
import jax
import jax.numpy as jnp
from jax import lax
from jax.sharding import PartitionSpec as P


def partner(value, axis, step):
    size = lax.axis_size(axis)
    return lax.ppermute(value, axis, [(a, a ^ step) for a in range(size)])


def filled(line, count):
    rank = jnp.cumsum(line) - 1
    place = jnp.arange(line.shape[0])
    return [jnp.sum(jnp.where((line == 1) & (rank == p), place, 0)) for p in range(count)]


def cut(value, rows, row_size, cols, col_size):
    return jnp.concatenate(
        [
            jnp.concatenate(
                [
                    lax.dynamic_slice(
                        value, (r * row_size, c * col_size), (row_size, col_size)
                    )
                    for c in cols
                ],
                axis=1,
            )
            for r in rows
        ],
        axis=0,
    )


def per_device(green_top, factor_cols, fill_blocks, diag_inverse):
    row_index = lax.axis_index("row")
    col_index = lax.axis_index("col")
    row_count = lax.axis_size("row")
    col_count = lax.axis_size("col")
    local_rows, order = factor_cols.shape
    blocks = fill_blocks.shape[1]
    size = order // blocks
    group = blocks // col_count
    half = group // 2
    chunk = blocks // row_count
    exact = chunk % group == 0
    kept = chunk // 2 if exact else chunk

    def fill_of(k, start, count):
        return lax.dynamic_slice(fill_blocks, (k, start), (1, count))[0]

    def chosen(k, part):
        if exact:
            return filled(fill_of(k, part * chunk, chunk), kept)
        return list(range(kept))

    fill_line = jnp.repeat(fill_of(row_index, 0, blocks), size)
    masked = factor_cols * fill_line.astype(jnp.bfloat16)[None, :]
    picks = [[part * chunk + b for b in chosen(row_index, part)] for part in range(row_count)]
    own_factor = jnp.concatenate(
        [
            lax.dynamic_slice(masked, (0, b * size), (local_rows, size))
            for pick in picks
            for b in pick
        ],
        axis=1,
    )
    factor_parts = {t: partner(own_factor, "col", t) for t in range(1, col_count)}
    factor_parts[0] = own_factor

    green_parts = {}
    for s in range(row_count):
        k = row_index ^ s
        rows = filled(fill_of(k, col_index * group, group), half)
        green_parts[s] = cut(green_top, rows, size, chosen(k, row_index), size)
    for s in range(1, row_count):
        green_parts[s] = partner(green_parts[s], "row", s)

    factor = jnp.zeros((col_count * local_rows, own_factor.shape[1]), jnp.bfloat16)
    for t in range(col_count):
        factor = lax.dynamic_update_slice(
            factor, factor_parts[t], ((col_index ^ t) * local_rows, 0)
        )
    width = kept * size
    solved = 0.0
    for s in range(row_count):
        part = lax.dynamic_slice(
            factor, (0, (row_index ^ s) * width), (factor.shape[0], width)
        )
        solved = solved - lax.dot_general(
            part, green_parts[s], (((1,), (1,)), ((), ())), preferred_element_type=jnp.float32
        )
    fill_own = fill_of(row_index, col_index * group, group)
    rows = filled(fill_own, half)
    if exact:
        places = [col_index * half + p for p in range(half)]
    else:
        places = [col_index * group + r for r in rows]
    factor_rows = jnp.concatenate(
        [
            lax.dynamic_slice(factor, (0, b * size), (factor.shape[0], size))
            for b in places
        ],
        axis=1,
    )
    partial_value = lax.dot_general(
        solved,
        factor_rows.astype(jnp.float32),
        (((1,), (1,)), ((), ())),
        precision=lax.Precision.HIGHEST,
        preferred_element_type=jnp.float32,
    )
    rank = jnp.cumsum(fill_own) - 1
    green_cols = jnp.concatenate(
        [
            sum(
                jnp.where((fill_own[b] == 1) & (rank[b] == p), 1.0, 0.0)
                * solved[:, p * size : (p + 1) * size]
                for p in range(half)
            )
            for b in range(group)
        ],
        axis=1,
    )
    sums = [partial_value] + [partner(partial_value, "col", t) for t in range(1, col_count)]
    while len(sums) > 1:
        sums = [a + b for a, b in zip(sums[::2], sums[1::2])]
    return (green_cols, diag_inverse - sums[0])


def solution(mesh):
    placed = (
        P(("pole", "col"), "row"),
        P(("pole", "row", "col"), None),
        P(),
        P(("pole", "row"), None),
    )
    return jax.shard_map(
        per_device,
        mesh=mesh,
        in_specs=placed,
        out_specs=(P(("pole", "row"), "col"), P(("pole", "row"), None)),
        check_vma=False,
    )
```

time: 108 us -> 48.3 us (0.45)
  waiting for transfers between devices: 54.8 us -> 10.1 us
  blocking collectives: 25 us -> 0 us
  starting transfers between devices: 5.44 us -> 12.1 us
  other arithmetic: 3.21 us -> 9.6 us
  between operations: 14.1 us -> 11.5 us
  matrix products: 3.37 us -> 1.03 us
  local copies, waits for them, and re-layouts: 1.54 us -> 3.63 us
    psum x1 -> x0, waiting for transfers between devices: 34.3 us -> none  [per_device(): total = lax.psum(partial_value, 'col')]
    all_gather x1 -> x0, blocking collectives: 16.2 us -> none  [per_device(): stacked = lax.all_gather(pieces, 'col', axis=0, tiled=True)]
    reduce_scatter x1 -> x0, waiting for transfers between devices: 14.7 us -> none  [per_device(): lax.psum_scatter(lax.dot_general(panel_rows, green_top, (((1,), (1,)), ((...]
    ppermute x0 -> x9, starting transfers between devices: none -> 12.1 us  [partner(): return lax.ppermute(value, axis, [(a, a ^ step) for a in range(size)])]
    ppermute x0 -> x9, waiting for transfers between devices: none -> 10.1 us  [partner(): return lax.ppermute(value, axis, [(a, a ^ step) for a in range(size)])]
    all_to_all x1 -> x0, blocking collectives: 8.84 us -> none  [per_device(): lax.all_to_all(masked, 'row', split_axis=1, concat_axis=0, tiled=True)]
    all_to_all x1 -> x0, waiting for transfers between devices: 5.84 us -> none  [per_device(): lax.all_to_all(masked, 'col', split_axis=1, concat_axis=0, tiled=True)]
    all_to_all x1 -> x0, starting transfers between devices: 5.4 us -> none  [per_device(): lax.all_to_all(masked, 'col', split_axis=1, concat_axis=0, tiled=True)]
  transfers between devices with their start and end apart: 3 -> 9, of which waited for: 3 -> 3; matrix products, arithmetic and copies ran while one was open for 1% -> 17% of each run, Pallas kernels for 0% -> 0%
where the time goes in v1:
time: 48.3 us; the launch traced here: 48 us
  starting transfers between devices  12.1 us (25%)
  between operations  11.5 us (24%)
  waiting for transfers between devices  10.1 us (21%)
  other arithmetic  9.6 us (20%)
  local copies, waits for them, and re-layouts  3.63 us (8%)
  matrix products  1.03 us (2%)
    ppermute x9, starting transfers between devices, partner(): return lax.ppermute(value, axis, [(a, a ^ step) for a in range(size)])  12.1 us
    ppermute x9, waiting for transfers between devices, partner(): return lax.ppermute(value, axis, [(a, a ^ step) for a in range(size)])  10.1 us
    reduce_sum x6, other arithmetic, filled(): jnp.sum(jnp.where((line == 1) & (rank == p), place, 0))  3.96 us
    another operation x12, other arithmetic  2.1 us
    eq x12, other arithmetic, filled(): line == 1  1.44 us
    dynamic_slice x1, local copies, waits for them, and re-layouts, fill_of(): return lax.dynamic_slice(fill_blocks, (k, start), (1, count))[0]  1.21 us
    unnamed x20, local copies, waits for them, and re-layouts  1.21 us
  transfers between devices with their start and end apart: 9, of which 3 were waited for; matrix products, arithmetic and copies ran while one was open for 17% of the time, Pallas kernels for 0%

profile of v1, /device:TPU:0, one launch (start us, length us, event | category | flops | bytes accessed | tf_op | source)
XLA Modules:
  0.0 48.0 jit_solution(10592511785809268183)
XLA Ops:
  0.7 1.2 %fusion.45 = (s32[1,2]{1,0:T(1,128)S(1)}, s32[1,2]{1,0:T(1,128)S(1)}, s32[1,2]{1,0:T(1,128)S(1)}, s32[1,2]{1,0:T(1,128)S(1)}, s32[1,2]{1,0:T(1,128)S(1)}, /*inde...) fusion(s32[4,8]{1,0:T(4,128)} %param.6, ...), kind=kLoop, calls=%fused_computation.91 | loop fusion | bytes 216 | tf_op jit(solution)/shard_map/dynamic_slice | solution.py:51
  2.5 0.2 reduce-window.110
  2.7 0.6 %fusion.32 = (s32[]{:T(128)}, s32[]{:T(128)}) fusion(pred[2]{0:T(512)(128)(4,1)S(1)} %compare_reduce_fusion.11, s32[2,1]{0,1:T(1,128)S(1)} %reduce-window.109, pred[2]{0:T(512)(128)(4,1)S(1)} %compare_reduce_fusion.10, s32[2,1]{0,1:T(1,128)S(1)} %reduce-window.110), kind=kLoop, calls=%fused_computation.74 | loop fusion | flops 18 | bytes 28 | tf_op jit(solution)/shard_map/reduce_sum | solution.py:15
  4.4 0.2 reduce-window.111
  4.6 0.2 reduce-window.112
  4.7 0.7 %fusion.34 = (s32[]{:T(128)}, s32[]{:T(128)}) fusion(pred[2]{0:T(512)(128)(4,1)S(1)} %compare_reduce_fusion.9, s32[2,1]{0,1:T(1,128)S(1)} %reduce-window.111, pred[2]{0:T(512)(128)(4,1)S(1)} %compare_reduce_fusion.8, s32[2,1]{0,1:T(1,128)S(1)} %reduce-window.112), kind=kLoop, calls=%fused_computation.76 | loop fusion | flops 18 | bytes 28 | tf_op jit(solution)/shard_map/reduce_sum | solution.py:15
  7.5 0.7 %fusion.31 = bf16[8]{0:T(256)(128)(2,1)S(1)} fusion(s32[4,8]{1,0:T(4,128)} %param.6, s32[]{:T(128)S(6)} %select_n.148), kind=kLoop, calls=%fused_computation.73 | loop fusion | flops 8 | bytes 52 | tf_op jit(solution)/shard_map/convert_element_type | solution.py:59
  8.4 3.1 %collective-permute-start = (bf16[32,1024]{1,0:T(8,128)(2,1)S(1)}, bf16[32,1024]{1,0:T(8,128)(2,1)S(1)}, u32[]{:S(2)}, u32[]{:S(2)}) collective-permute-start(bf16[32,1024]{1,0:T(8,128)(2,1)S(1)} %get-tuple-element.11), channel_id=1, source_target_pairs={{0,1},{1,0},{2,3},{3,2},{4,5},{5,4},{6,7},{7,6},{8,9},{9,8},{10,11... | collective-permute-start | bytes 196616 | tf_op jit(solution)/shard_map/ppermute | solution.py:9
  11.5 2.6 %collective-permute-start.1 = (bf16[32,1024]{1,0:T(8,128)(2,1)S(1)}, bf16[32,1024]{1,0:T(8,128)(2,1)S(1)}, u32[]{:S(2)}, u32[]{:S(2)}) collective-permute-start(bf16[32,1024]{1,0:T(8,128)(2,1)S(1)} %get-tuple-element.11), channel_id=1, source_target_pairs={{0,2},{1,3},{2,0},{3,1},{4,6},{5,7},{6,4},{7,5},{8,10},{9,11},{10,... | collective-permute-start | bytes 196616 | tf_op jit(solution)/shard_map/ppermute | solution.py:9
  14.5 0.2 reduce-window.116
  14.7 0.2 reduce-window.117
  14.9 0.6 %fusion.40 = (s32[]{:T(128)}, s32[]{:T(128)}) fusion(pred[2]{0:T(512)(128)(4,1)S(1)} %compare_reduce_fusion.3, s32[2,1]{0,1:T(1,128)S(1)} %reduce-window.116, pred[2]{0:T(512)(128)(4,1)S(1)} %compare_reduce_fusion.2, s32[2,1]{0,1:T(1,128)S(1)} %reduce-window.117), kind=kLoop, calls=%fused_computation.82 | loop fusion | flops 18 | bytes 28 | tf_op jit(solution)/shard_map/reduce_sum | solution.py:15
  17.3 0.2 reduce-window.118
  17.6 0.6 %fusion.42 = (s32[]{:T(128)}, s32[]{:T(128)}) fusion(pred[2]{0:T(512)(128)(4,1)S(1)} %compare_reduce_fusion.1, s32[2,1]{0,1:T(1,128)S(1)} %reduce-window.118, pred[2]{0:T(512)(128)(4,1)S(1)} %compare_reduce_fusion, s32[2,1]{0,1:T(1,128)S(1)} %reduce-window.119), kind=kLoop, calls=%fused_computation.84 | loop fusion | flops 18 | bytes 28 | tf_op jit(solution)/shard_map/reduce_sum | solution.py:15
  20.3 0.6 %fusion.38 = (s32[]{:T(128)}, s32[]{:T(128)}) fusion(pred[2]{0:T(512)(128)(4,1)S(1)} %compare_reduce_fusion.5, s32[2,1]{0,1:T(1,128)S(1)} %reduce-window.114, pred[2]{0:T(512)(128)(4,1)S(1)} %compare_reduce_fusion.4, s32[2,1]{0,1:T(1,128)S(1)} %reduce-window.115), kind=kLoop, calls=%fused_computation.80 | loop fusion | flops 18 | bytes 28 | tf_op jit(solution)/shard_map/reduce_sum | solution.py:15
  22.4 1.8 %collective-permute-start.4 = (bf16[256,256]{1,0:T(8,128)(2,1)S(1)}, bf16[256,256]{1,0:T(8,128)(2,1)S(1)}, u32[]{:S(2)}, u32[]{:S(2)}) collective-permute-start(bf16[256,256]{1,0:T(8,128)(2,1)S(1)} %get-tuple-element.4), channel_id=1, source_target_pairs={{0,8},{4,12},{8,0},{12,4},{1,9},{5,13},{9,1},{13,5},{2,10},{6,14},... | collective-permute-start | bytes 393224 | tf_op jit(solution)/shard_map/ppermute | solution.py:9
  25.0 0.6 %fusion.36 = (s32[]{:T(128)}, s32[]{:T(128)}) fusion(pred[2]{0:T(512)(128)(4,1)S(1)} %compare_reduce_fusion.7, s32[2,1]{0,1:T(1,128)S(1)} %reduce-window.108, pred[2]{0:T(512)(128)(4,1)S(1)} %compare_reduce_fusion.6, s32[2,1]{0,1:T(1,128)S(1)} %reduce-window.113), kind=kLoop, calls=%fused_computation.78 | loop fusion | flops 18 | bytes 28 | tf_op jit(solution)/shard_map/reduce_sum | solution.py:15
  27.0 0.5 %fusion.46 = (s32[1,1]{0,1:T(1,128)}, s32[1,1]{0,1:T(1,128)}) fusion(s32[1,2]{0,1:T(2,128)S(1)} %copy.30), kind=kLoop, calls=%fused_computation.92 | loop fusion | bytes 16 | tf_op jit(solution)/shard_map/slice | solution.py:118
  28.8 0.6 %fusion.47 = (s32[1,1]{0,1:T(1,128)}, s32[1,1]{0,1:T(1,128)}) fusion(s32[2,1]{0,1:T(1,128)S(1)} %broadcast_add_fusion), kind=kLoop, calls=%fused_computation.93 | loop fusion | bytes 16 | tf_op jit(solution)/shard_map/slice | solution.py:118
  31.0 0.2 fusion.10
  31.2 0.2 fusion.8
  31.4 4.9 %collective-permute-done.5 = bf16[256,256]{1,0:T(8,128)(2,1)S(1)} collective-permute-done((bf16[256,256]{1,0:T(8,128)(2,1)S(1)}, bf16[256,256]{1,0:T(8,128)(2,1)S(1)}, u32[]{:S(2)}, u32[]{:S(2)}) %collective-permute-start.5) | collective-permute-done | bytes 131104 | tf_op jit(solution)/shard_map/ppermute | solution.py:9
  36.2 0.2 fusion.6
  36.4 0.2 broadcast_multiply_fusion.2
  36.7 0.2 fusion.4
  36.9 0.7 %collective-permute-start.6 = (f32[128,128]{1,0:T(8,128)S(1)}, f32[128,128]{1,0:T(8,128)S(1)}, u32[]{:S(2)}, u32[]{:S(2)}) collective-permute-start(f32[128,128]{1,0:T(8,128)S(1)} %fusion.4), channel_id=1, source_target_pairs={{0,1},{1,0},{2,3},{3,2},{4,5},{5,4},{6,7},{7,6},{8,9},{9,8},{10,11... | collective-permute-start | bytes 196616 | tf_op jit(solution)/shard_map/ppermute | solution.py:9
  37.7 3.5 %collective-permute-start.7 = (f32[128,128]{1,0:T(8,128)S(1)}, f32[128,128]{1,0:T(8,128)S(1)}, u32[]{:S(2)}, u32[]{:S(2)}) collective-permute-start(f32[128,128]{1,0:T(8,128)S(1)} %fusion.4), channel_id=1, source_target_pairs={{0,2},{1,3},{2,0},{3,1},{4,6},{5,7},{6,4},{7,5},{8,10},{9,11},{10,... | collective-permute-start | bytes 196616 | tf_op jit(solution)/shard_map/ppermute | solution.py:9
  41.2 0.2 collective-permute-start.8
  41.4 0.7 %pad_maximum_fusion = f32[128,512]{1,0:T(8,128)} fusion(f32[128,256]{1,0:T(8,128)S(1)} %get-tuple-element.6, f32[128,256]{1,0:T(8,128)S(1)} %get-tuple-element.5), kind=kLoop, calls=%fused_computation.4 | loop fusion | flops 65536 | bytes 524288 | tf_op jit(solution)/shard_map/concatenate | solution.py:115
  42.1 3.1 %collective-permute-done.7 = f32[128,128]{1,0:T(8,128)S(1)} collective-permute-done((f32[128,128]{1,0:T(8,128)S(1)}, f32[128,128]{1,0:T(8,128)S(1)}, u32[]{:S(2)}, u32[]{:S(2)}) %collective-permute-start.7) | collective-permute-done | bytes 65568 | tf_op jit(solution)/shard_map/ppermute | solution.py:9
  45.2 2.1 %collective-permute-done.8 = f32[128,128]{1,0:T(8,128)S(1)} collective-permute-done((f32[128,128]{1,0:T(8,128)S(1)}, f32[128,128]{1,0:T(8,128)S(1)}, u32[]{:S(2)}, u32[]{:S(2)}) %collective-permute-start.8) | collective-permute-done | bytes 65568 | tf_op jit(solution)/shard_map/ppermute | solution.py:9
  47.3 0.6 %add_subtract_fusion = f32[128,128]{1,0:T(8,128)} fusion(f32[128,128]{1,0:T(8,128)S(1)} %copy-done.2, f32[128,128]{1,0:T(8,128)S(1)} %collective-permute-done.7, f32[128,128]{1,0:T(8,128)S(1)} %collective-permute-done.8, f32[128,128]{1,0:T(8,128)S(1)} %fusion.4, f32[128,128]{1,0:T(8,128)S(1)} %collective-permute-done.6), kind=kLoop, calls=%fused_computation.7 | loop fusion | flops 65536 | bytes 393216 | tf_op jit(solution)/shard_map/sub | solution.py:129
  (56 shorter events, 4.1 us)
Async XLA Ops:
  0.6 7.7 %copy-start.1 = (bf16[32,2048]{1,0:T(8,128)(2,1)S(1)}, bf16[32,2048]{1,0:T(8,128)(2,1)}, u32[]{:S(2)}) copy-start(bf16[32,2048]{1,0:T(8,128)(2,1)} %param.5) | copy-start | bytes 393220
  6.1 16.2 %copy-start = (bf16[512,512]{1,0:T(8,128)(2,1)S(1)}, bf16[512,512]{1,0:T(8,128)(2,1)}, u32[]{:S(2)}) copy-start(bf16[512,512]{1,0:T(8,128)(2,1)} %param.4) | copy-start | bytes 1572868
  8.4 22.3 %collective-permute-start = (bf16[32,1024]{1,0:T(8,128)(2,1)S(1)}, bf16[32,1024]{1,0:T(8,128)(2,1)S(1)}, u32[]{:S(2)}, u32[]{:S(2)}) collective-permute-start(bf16[32,1024]{1,0:T(8,128)(2,1)S(1)} %get-tuple-element.11), channel_id=1, source_target_pairs={{0,1},{1,0},{2,3},{3,2},{4,5},{5,4},{6,7},{7,6},{8,9},{9,8},{10,11... | collective-permute-start | bytes 196616 | tf_op jit(solution)/shard_map/ppermute | solution.py:9
  11.5 19.4 %collective-permute-start.1 = (bf16[32,1024]{1,0:T(8,128)(2,1)S(1)}, bf16[32,1024]{1,0:T(8,128)(2,1)S(1)}, u32[]{:S(2)}, u32[]{:S(2)}) collective-permute-start(bf16[32,1024]{1,0:T(8,128)(2,1)S(1)} %get-tuple-element.11), channel_id=1, source_target_pairs={{0,2},{1,3},{2,0},{3,1},{4,6},{5,7},{6,4},{7,5},{8,10},{9,11},{10,... | collective-permute-start | bytes 196616 | tf_op jit(solution)/shard_map/ppermute | solution.py:9
  14.1 16.8 %collective-permute-start.2 = (bf16[32,1024]{1,0:T(8,128)(2,1)S(1)}, bf16[32,1024]{1,0:T(8,128)(2,1)S(1)}, u32[]{:S(2)}, u32[]{:S(2)}) collective-permute-start(bf16[32,1024]{1,0:T(8,128)(2,1)S(1)} %get-tuple-element.11), channel_id=1, source_target_pairs={{0,3},{1,2},{2,1},{3,0},{4,7},{5,6},{6,5},{7,4},{8,11},{9,10},{10,... | collective-permute-start | bytes 196616 | tf_op jit(solution)/shard_map/ppermute | solution.py:9
  22.4 8.6 %collective-permute-start.3 = (bf16[256,256]{1,0:T(8,128)(2,1)S(1)}, bf16[256,256]{1,0:T(8,128)(2,1)S(1)}, u32[]{:S(2)}, u32[]{:S(2)}) collective-permute-start(bf16[256,256]{1,0:T(8,128)(2,1)S(1)} %get-tuple-element.2), channel_id=1, source_target_pairs={{0,4},{4,0},{8,12},{12,8},{1,5},{5,1},{9,13},{13,9},{2,6},{6,2},{1... | collective-permute-start | bytes 393224 | tf_op jit(solution)/shard_map/ppermute | solution.py:9
  22.4 8.7 %collective-permute-start.4 = (bf16[256,256]{1,0:T(8,128)(2,1)S(1)}, bf16[256,256]{1,0:T(8,128)(2,1)S(1)}, u32[]{:S(2)}, u32[]{:S(2)}) collective-permute-start(bf16[256,256]{1,0:T(8,128)(2,1)S(1)} %get-tuple-element.4), channel_id=1, source_target_pairs={{0,8},{4,12},{8,0},{12,4},{1,9},{5,13},{9,1},{13,5},{2,10},{6,14},... | collective-permute-start | bytes 393224 | tf_op jit(solution)/shard_map/ppermute | solution.py:9
  30.7 5.5 %collective-permute-start.5 = (bf16[256,256]{1,0:T(8,128)(2,1)S(1)}, bf16[256,256]{1,0:T(8,128)(2,1)S(1)}, u32[]{:S(2)}, u32[]{:S(2)}) collective-permute-start(bf16[256,256]{1,0:T(8,128)(2,1)S(1)} %get-tuple-element.3), channel_id=1, source_target_pairs={{0,12},{4,8},{8,4},{12,0},{1,13},{5,9},{9,5},{13,1},{2,14},{6,10},... | collective-permute-start | bytes 393224 | tf_op jit(solution)/shard_map/ppermute | solution.py:9
  36.9 5.2 %collective-permute-start.6 = (f32[128,128]{1,0:T(8,128)S(1)}, f32[128,128]{1,0:T(8,128)S(1)}, u32[]{:S(2)}, u32[]{:S(2)}) collective-permute-start(f32[128,128]{1,0:T(8,128)S(1)} %fusion.4), channel_id=1, source_target_pairs={{0,1},{1,0},{2,3},{3,2},{4,5},{5,4},{6,7},{7,6},{8,9},{9,8},{10,11... | collective-permute-start | bytes 196616 | tf_op jit(solution)/shard_map/ppermute | solution.py:9
  37.7 7.6 %collective-permute-start.7 = (f32[128,128]{1,0:T(8,128)S(1)}, f32[128,128]{1,0:T(8,128)S(1)}, u32[]{:S(2)}, u32[]{:S(2)}) collective-permute-start(f32[128,128]{1,0:T(8,128)S(1)} %fusion.4), channel_id=1, source_target_pairs={{0,2},{1,3},{2,0},{3,1},{4,6},{5,7},{6,4},{7,5},{8,10},{9,11},{10,... | collective-permute-start | bytes 196616 | tf_op jit(solution)/shard_map/ppermute | solution.py:9
  41.2 6.2 %collective-permute-start.8 = (f32[128,128]{1,0:T(8,128)S(1)}, f32[128,128]{1,0:T(8,128)S(1)}, u32[]{:S(2)}, u32[]{:S(2)}) collective-permute-start(f32[128,128]{1,0:T(8,128)S(1)} %fusion.4), channel_id=1, source_target_pairs={{0,3},{1,2},{2,1},{3,0},{4,7},{5,6},{6,5},{7,4},{8,11},{9,10},{10,... | collective-permute-start | bytes 196616 | tf_op jit(solution)/shard_map/ppermute | solution.py:9
  41.4 6.0 %copy-start.2 = (f32[128,128]{1,0:T(8,128)S(1)}, f32[128,128]{1,0:T(8,128)}, u32[]{:S(2)}) copy-start(f32[128,128]{1,0:T(8,128)} %param.7) | copy-start | bytes 196612

commit v2 on v1

--- a/solution.py
+++ b/solution.py
@@ -1,6 +1,8 @@
 import jax
 import jax.numpy as jnp
 from jax import lax
+from jax.experimental import pallas as pl
+from jax.experimental.pallas import tpu as pltpu
 from jax.sharding import PartitionSpec as P
 
 
@@ -33,7 +35,7 @@
     )
 
 
-def per_device(green_top, factor_cols, fill_blocks, diag_inverse):
+def wide_device(green_top, factor_cols, fill_blocks, diag_inverse):
     row_index = lax.axis_index("row")
     col_index = lax.axis_index("col")
     row_count = lax.axis_size("row")
@@ -129,6 +131,145 @@
     return (green_cols, diag_inverse - sums[0])
 
 
+def pack_kernel(row_count, col_count, fill, green, factor, *refs):
+    outs, sems = refs[:-1], refs[-1]
+    own_factor, mask = outs[0], outs[1]
+    greens = outs[2:]
+    row_index = lax.axis_index("row")
+    col_index = lax.axis_index("col")
+    blocks = fill.shape[1]
+    size = factor.shape[1] // blocks
+    group = blocks // col_count
+    half = group // 2
+    chunk = blocks // row_count
+    kept = chunk // 2
+
+    def places(k, start, count, wanted):
+        found = [0] * wanted
+        rank = 0
+        for b in range(count):
+            one = fill[k, start + b]
+            for p in range(wanted):
+                found[p] = jnp.where((one == 1) & (rank == p), b, found[p])
+            rank = rank + one
+        return found
+
+    copies = []
+
+    def copy(source, target):
+        one = pltpu.make_async_copy(source, target, sems.at[len(copies)])
+        one.start()
+        copies.append(one)
+
+    for part in range(row_count):
+        for p, b in enumerate(places(row_index, part * chunk, chunk, kept)):
+            copy(
+                factor.at[:, pl.ds(pl.multiple_of((part * chunk + b) * size, size), size)],
+                own_factor.at[:, pl.ds((part * kept + p) * size, size)],
+            )
+    for s in range(row_count):
+        k = row_index ^ s
+        rows = places(k, col_index * group, group, half)
+        cols = places(k, row_index * chunk, chunk, kept)
+        for p, r in enumerate(rows):
+            for q, c in enumerate(cols):
+                copy(
+                    green.at[
+                        pl.ds(pl.multiple_of(r * size, size), size),
+                        pl.ds(pl.multiple_of(c * size, size), size),
+                    ],
+                    greens[s].at[pl.ds(p * size, size), pl.ds(q * size, size)],
+                )
+        if s == 0:
+            for p, r in enumerate(rows):
+                for b in range(group):
+                    mask[p : p + 1, b * size : (b + 1) * size] = jnp.full(
+                        (1, size), jnp.where(r == b, 1.0, 0.0), jnp.float32
+                    )
+    for one in copies:
+        one.wait()
+
+
+def pack(green_top, factor_cols, fill_blocks):
+    row_count = lax.axis_size("row")
+    col_count = lax.axis_size("col")
+    local_rows, order = factor_cols.shape
+    blocks = fill_blocks.shape[1]
+    size = order // blocks
+    group = blocks // col_count
+    half = group // 2
+    kept = blocks // row_count // 2
+    shapes = [
+        pltpu.VMEM((local_rows, row_count * kept * size), jnp.bfloat16),
+        pltpu.VMEM((half, group * size), jnp.float32),
+    ] + [pltpu.VMEM((half * size, kept * size), jnp.bfloat16)] * row_count
+    return pl.pallas_call(
+        lambda *refs: pack_kernel(row_count, col_count, *refs),
+        out_shape=shapes,
+        in_specs=[
+            pl.BlockSpec(memory_space=pltpu.SMEM),
+            pl.BlockSpec(memory_space=pltpu.HBM),
+            pl.BlockSpec(memory_space=pltpu.HBM),
+        ],
+        out_specs=[pl.BlockSpec(memory_space=pltpu.VMEM)] * len(shapes),
+        scratch_shapes=[
+            pltpu.SemaphoreType.DMA((row_count * kept + row_count * half * kept,))
+        ],
+        name="pack",
+    )(fill_blocks, green_top, factor_cols)
+
+
+def per_device(green_top, factor_cols, fill_blocks, diag_inverse):
+    row_count = lax.axis_size("row")
+    col_count = lax.axis_size("col")
+    blocks = fill_blocks.shape[1]
+    chunk = blocks // row_count
+    group = blocks // col_count
+    if chunk % group or green_top.size > 1 << 20:
+        return wide_device(green_top, factor_cols, fill_blocks, diag_inverse)
+    row_index = lax.axis_index("row")
+    col_index = lax.axis_index("col")
+    local_rows, order = factor_cols.shape
+    size = order // blocks
+    half = group // 2
+    width = chunk // 2 * size
+
+    own_factor, mask, *greens = pack(green_top, factor_cols, fill_blocks)
+    factors = [own_factor] + [partner(own_factor, "col", t) for t in range(1, col_count)]
+    greens = greens[:1] + [partner(greens[s], "row", s) for s in range(1, row_count)]
+    factor = jnp.zeros((col_count * local_rows, own_factor.shape[1]), jnp.bfloat16)
+    for t in range(col_count):
+        factor = lax.dynamic_update_slice(
+            factor, factors[t], ((col_index ^ t) * local_rows, 0)
+        )
+    solved = 0.0
+    for s in range(row_count):
+        part = lax.dynamic_slice(
+            factor, (0, (row_index ^ s) * width), (factor.shape[0], width)
+        )
+        solved = solved - lax.dot_general(
+            part, greens[s], (((1,), (1,)), ((), ())), preferred_element_type=jnp.float32
+        )
+    factor_rows = lax.dynamic_slice(
+        factor, (0, col_index * half * size), (factor.shape[0], half * size)
+    )
+    partial_value = lax.dot_general(
+        solved,
+        factor_rows.astype(jnp.float32),
+        (((1,), (1,)), ((), ())),
+        precision=lax.Precision.HIGHEST,
+        preferred_element_type=jnp.float32,
+    )
+    green_cols = sum(
+        mask[p : p + 1] * jnp.tile(solved[:, p * size : (p + 1) * size], (1, group))
+        for p in range(half)
+    )
+    sums = [partial_value] + [partner(partial_value, "col", t) for t in range(1, col_count)]
+    while len(sums) > 1:
+        sums = [a + b for a, b in zip(sums[::2], sums[1::2])]
+    return (green_cols, diag_inverse - sums[0])
+
+
 def solution(mesh):
     placed = (
         P(("pole", "col"), "row"),

time: 48.3 us -> 28.7 us (0.59)
  between operations: 11.5 us -> 0.75 us
  other arithmetic: 9.6 us -> 1.38 us
  local copies, waits for them, and re-layouts: 3.63 us -> 0.17 us
  Pallas kernels: 0 us -> 1.94 us
  waiting for transfers between devices: 10.1 us -> 11.2 us
    reduce_sum x6 -> x0, other arithmetic: 3.96 us -> none  [filled(): jnp.sum(jnp.where((line == 1) & (rank == p), place, 0))]
    another operation x12 -> x0, other arithmetic: 2.1 us -> none
    pallas_call x0 -> x1, Pallas kernels: none -> 1.94 us  [pack(): pl.pallas_call(lambda *refs: pack_kernel(row_count, col_count, *refs), ou...]
    eq x12 -> x0, other arithmetic: 1.44 us -> none  [filled(): line == 1]
    dynamic_slice x3 -> x0, local copies, waits for them, and re-layouts: 1.28 us -> none  [the longest x1 1.21 us: fill_of(): return lax.dynamic_slice(fill_blocks, (k, start), (1, count))[0]]
    unnamed x20 -> x3, local copies, waits for them, and re-layouts: 1.21 us -> 0.03 us
    slice x2 -> x0, local copies, waits for them, and re-layouts: 1.1 us -> none  [the longest x1 0.58 us: per_device(): rank[b] == p]
    ppermute x9, waiting for transfers between devices: 10.1 us -> 11.2 us  [partner(): return lax.ppermute(value, axis, [(a, a ^ step) for a in range(size)])]
  transfers between devices with their start and end apart: 9 -> 9, of which waited for: 3 -> 5; matrix products, arithmetic and copies ran while one was open for 17% -> 4% of each run, Pallas kernels for 0% -> 0%
where the time goes in v2:
time: 28.7 us; the launch traced here: 28.5 us
  starting transfers between devices  12.1 us (42%)
  waiting for transfers between devices  11.2 us (39%)
  Pallas kernels  1.94 us (7%)
  other arithmetic  1.38 us (5%)
  matrix products  1.01 us (4%)
  between operations  0.75 us (3%)
    ppermute x9, starting transfers between devices, partner(): return lax.ppermute(value, axis, [(a, a ^ step) for a in range(size)])  12.1 us
    ppermute x9, waiting for transfers between devices, partner(): return lax.ppermute(value, axis, [(a, a ^ step) for a in range(size)])  11.2 us
    pallas_call x1, Pallas kernels, pack(): pl.pallas_call(lambda *refs: pack_kernel(row_count, col_count, *refs), ou...  1.94 us
    dot_general x4, matrix products, per_device(): lax.dot_general(part, greens[s], (((1,), (1,)), ((), ())), preferred_elem...  0.77 us
    mul x1, other arithmetic, per_device(): mask[p:p + 1] * jnp.tile(solved[:, p * size:(p + 1) * size], (1, group))  0.73 us
    sub x1, other arithmetic, per_device(): return (green_cols, diag_inverse - sums[0])  0.65 us
  transfers between devices with their start and end apart: 9, of which 5 were waited for; matrix products, arithmetic and copies ran while one was open for 4% of the time, Pallas kernels for 0%

profile of v2, /device:TPU:0, one launch (start us, length us, event | category | flops | bytes accessed | tf_op | source)
XLA Modules:
  0.0 28.5 jit_solution(15434656119153402632)
XLA Ops:
  0.6 1.9 %pack.1 = (bf16[32,1024]{1,0:T(8,128)(2,1)S(1)}, f32[1,512]{1,0:T(1,128)S(1)}, bf16[256,256]{1,0:T(8,128)(2,1)S(1)}, bf16[256,256]{1,0:T(8,128)(2,1)S(1)}, bf16[...) custom-call(s32[4,8]{1,0:T(4,128)} %refs_0_.1, bf16[512,512]{1,0:T(8,128)(2,1)} %refs_1_.1, bf16[32,2048]{1,0:T(8,128)(2,1)} %refs_2_.1), custom_call_target="tpu_custom_call" | custom-call | tf_op jit(solution)/shard_map/pack/pallas_call | solution.py:206
  2.6 3.1 %collective-permute-start = (bf16[32,1024]{1,0:T(8,128)(2,1)S(1)}, bf16[32,1024]{1,0:T(8,128)(2,1)S(1)}, u32[]{:S(2)}, u32[]{:S(2)}) collective-permute-start(bf16[32,1024]{1,0:T(8,128)(2,1)S(1)} %get-tuple-element.9), channel_id=1, source_target_pairs={{0,1},{1,0},{2,3},{3,2},{4,5},{5,4},{6,7},{7,6},{8,9},{9,8},{10,11... | collective-permute-start | bytes 196616 | tf_op jit(solution)/shard_map/ppermute | solution.py:11
  5.7 2.6 %collective-permute-start.1 = (bf16[32,1024]{1,0:T(8,128)(2,1)S(1)}, bf16[32,1024]{1,0:T(8,128)(2,1)S(1)}, u32[]{:S(2)}, u32[]{:S(2)}) collective-permute-start(bf16[32,1024]{1,0:T(8,128)(2,1)S(1)} %get-tuple-element.9), channel_id=1, source_target_pairs={{0,2},{1,3},{2,0},{3,1},{4,6},{5,7},{6,4},{7,5},{8,10},{9,11},{10,... | collective-permute-start | bytes 196616 | tf_op jit(solution)/shard_map/ppermute | solution.py:11
  8.3 0.0 collective-permute-start.2
  8.3 0.0 collective-permute-start.3
  8.3 1.7 %collective-permute-start.4 = (bf16[256,256]{1,0:T(8,128)(2,1)S(1)}, bf16[256,256]{1,0:T(8,128)(2,1)S(1)}, u32[]{:S(2)}, u32[]{:S(2)}) collective-permute-start(bf16[256,256]{1,0:T(8,128)(2,1)S(1)} %get-tuple-element.12), channel_id=1, source_target_pairs={{0,8},{4,12},{8,0},{12,4},{1,9},{5,13},{9,1},{13,5},{2,10},{6,14},... | collective-permute-start | bytes 393224 | tf_op jit(solution)/shard_map/ppermute | solution.py:11
  10.0 0.0 collective-permute-done
  10.0 0.2 collective-permute-start.5
  10.3 2.7 %collective-permute-done.1 = bf16[32,1024]{1,0:T(8,128)(2,1)S(1)} collective-permute-done((bf16[32,1024]{1,0:T(8,128)(2,1)S(1)}, bf16[32,1024]{1,0:T(8,128)(2,1)S(1)}, u32[]{:S(2)}, u32[]{:S(2)}) %collective-permute-start.1) | collective-permute-done | bytes 65568 | tf_op jit(solution)/shard_map/ppermute | solution.py:11
  13.0 1.4 %collective-permute-done.2 = bf16[32,1024]{1,0:T(8,128)(2,1)S(1)} collective-permute-done((bf16[32,1024]{1,0:T(8,128)(2,1)S(1)}, bf16[32,1024]{1,0:T(8,128)(2,1)S(1)}, u32[]{:S(2)}, u32[]{:S(2)}) %collective-permute-start.2) | collective-permute-done | bytes 65568 | tf_op jit(solution)/shard_map/ppermute | solution.py:11
  14.4 0.0 collective-permute-done.3
  14.4 0.2 fusion.9
  14.6 0.0 collective-permute-done.4
  14.6 0.2 fusion.7
  14.8 1.8 %collective-permute-done.5 = bf16[256,256]{1,0:T(8,128)(2,1)S(1)} collective-permute-done((bf16[256,256]{1,0:T(8,128)(2,1)S(1)}, bf16[256,256]{1,0:T(8,128)(2,1)S(1)}, u32[]{:S(2)}, u32[]{:S(2)}) %collective-permute-start.5) | collective-permute-done | bytes 131104 | tf_op jit(solution)/shard_map/ppermute | solution.py:11
  16.6 0.2 fusion.5
  16.8 0.2 fusion.2
  17.0 0.2 fusion.3
  17.2 1.0 %collective-permute-start.6 = (f32[128,128]{1,0:T(8,128)S(1)}, f32[128,128]{1,0:T(8,128)S(1)}, u32[]{:S(2)}, u32[]{:S(2)}) collective-permute-start(f32[128,128]{1,0:T(8,128)S(1)} %fusion.3), channel_id=1, source_target_pairs={{0,1},{1,0},{2,3},{3,2},{4,5},{5,4},{6,7},{7,6},{8,9},{9,8},{10,11... | collective-permute-start | bytes 196616 | tf_op jit(solution)/shard_map/ppermute | solution.py:11
  18.2 3.5 %collective-permute-start.7 = (f32[128,128]{1,0:T(8,128)S(1)}, f32[128,128]{1,0:T(8,128)S(1)}, u32[]{:S(2)}, u32[]{:S(2)}) collective-permute-start(f32[128,128]{1,0:T(8,128)S(1)} %fusion.3), channel_id=1, source_target_pairs={{0,2},{1,3},{2,0},{3,1},{4,6},{5,7},{6,4},{7,5},{8,10},{9,11},{10,... | collective-permute-start | bytes 196616 | tf_op jit(solution)/shard_map/ppermute | solution.py:11
  21.7 0.0 collective-permute-start.8
  21.7 0.1 tile.4
  21.8 0.0 copy-start
  21.8 0.7 %broadcast_multiply_fusion = f32[128,512]{1,0:T(8,128)} fusion(f32[128,512]{1,0:T(8,128)S(1)} %bitcast.9, f32[512]{0:T(512)S(1)} %bitcast.8), kind=kLoop, calls=%fused_computation.4 | loop fusion | flops 65536 | bytes 526336 | tf_op jit(solution)/shard_map/mul | solution.py:264
  22.6 0.0 collective-permute-done.6
  22.6 3.2 %collective-permute-done.7 = f32[128,128]{1,0:T(8,128)S(1)} collective-permute-done((f32[128,128]{1,0:T(8,128)S(1)}, f32[128,128]{1,0:T(8,128)S(1)}, u32[]{:S(2)}, u32[]{:S(2)}) %collective-permute-start.7) | collective-permute-done | bytes 65568 | tf_op jit(solution)/shard_map/ppermute | solution.py:11
  25.8 2.1 %collective-permute-done.8 = f32[128,128]{1,0:T(8,128)S(1)} collective-permute-done((f32[128,128]{1,0:T(8,128)S(1)}, f32[128,128]{1,0:T(8,128)S(1)}, u32[]{:S(2)}, u32[]{:S(2)}) %collective-permute-start.8) | collective-permute-done | bytes 65568 | tf_op jit(solution)/shard_map/ppermute | solution.py:11
  27.9 0.0 copy-done
  27.9 0.6 %add_subtract_fusion = f32[128,128]{1,0:T(8,128)} fusion(f32[128,128]{1,0:T(8,128)S(1)} %copy-done, f32[128,128]{1,0:T(8,128)S(1)} %collective-permute-done.7, f32[128,128]{1,0:T(8,128)S(1)} %collective-permute-done.8, f32[128,128]{1,0:T(8,128)S(1)} %fusion.3, f32[128,128]{1,0:T(8,128)S(1)} %collective-permute-done.6), kind=kLoop, calls=%fused_computation.5 | loop fusion | flops 65536 | bytes 393216 | tf_op jit(solution)/shard_map/sub | solution.py:270
  (6 shorter events, 0.1 us)
Async XLA Ops:
  2.6 7.4 %collective-permute-start = (bf16[32,1024]{1,0:T(8,128)(2,1)S(1)}, bf16[32,1024]{1,0:T(8,128)(2,1)S(1)}, u32[]{:S(2)}, u32[]{:S(2)}) collective-permute-start(bf16[32,1024]{1,0:T(8,128)(2,1)S(1)} %get-tuple-element.9), channel_id=1, source_target_pairs={{0,1},{1,0},{2,3},{3,2},{4,5},{5,4},{6,7},{7,6},{8,9},{9,8},{10,11... | collective-permute-start | bytes 196616 | tf_op jit(solution)/shard_map/ppermute | solution.py:11
  5.7 7.3 %collective-permute-start.1 = (bf16[32,1024]{1,0:T(8,128)(2,1)S(1)}, bf16[32,1024]{1,0:T(8,128)(2,1)S(1)}, u32[]{:S(2)}, u32[]{:S(2)}) collective-permute-start(bf16[32,1024]{1,0:T(8,128)(2,1)S(1)} %get-tuple-element.9), channel_id=1, source_target_pairs={{0,2},{1,3},{2,0},{3,1},{4,6},{5,7},{6,4},{7,5},{8,10},{9,11},{10,... | collective-permute-start | bytes 196616 | tf_op jit(solution)/shard_map/ppermute | solution.py:11
  8.3 6.1 %collective-permute-start.2 = (bf16[32,1024]{1,0:T(8,128)(2,1)S(1)}, bf16[32,1024]{1,0:T(8,128)(2,1)S(1)}, u32[]{:S(2)}, u32[]{:S(2)}) collective-permute-start(bf16[32,1024]{1,0:T(8,128)(2,1)S(1)} %get-tuple-element.9), channel_id=1, source_target_pairs={{0,3},{1,2},{2,1},{3,0},{4,7},{5,6},{6,5},{7,4},{8,11},{9,10},{10,... | collective-permute-start | bytes 196616 | tf_op jit(solution)/shard_map/ppermute | solution.py:11
  8.3 6.1 %collective-permute-start.3 = (bf16[256,256]{1,0:T(8,128)(2,1)S(1)}, bf16[256,256]{1,0:T(8,128)(2,1)S(1)}, u32[]{:S(2)}, u32[]{:S(2)}) collective-permute-start(bf16[256,256]{1,0:T(8,128)(2,1)S(1)} %get-tuple-element.11), channel_id=1, source_target_pairs={{0,4},{4,0},{8,12},{12,8},{1,5},{5,1},{9,13},{13,9},{2,6},{6,2},{1... | collective-permute-start | bytes 393224 | tf_op jit(solution)/shard_map/ppermute | solution.py:11
  8.3 6.3 %collective-permute-start.4 = (bf16[256,256]{1,0:T(8,128)(2,1)S(1)}, bf16[256,256]{1,0:T(8,128)(2,1)S(1)}, u32[]{:S(2)}, u32[]{:S(2)}) collective-permute-start(bf16[256,256]{1,0:T(8,128)(2,1)S(1)} %get-tuple-element.12), channel_id=1, source_target_pairs={{0,8},{4,12},{8,0},{12,4},{1,9},{5,13},{9,1},{13,5},{2,10},{6,14},... | collective-permute-start | bytes 393224 | tf_op jit(solution)/shard_map/ppermute | solution.py:11
  10.0 6.6 %collective-permute-start.5 = (bf16[256,256]{1,0:T(8,128)(2,1)S(1)}, bf16[256,256]{1,0:T(8,128)(2,1)S(1)}, u32[]{:S(2)}, u32[]{:S(2)}) collective-permute-start(bf16[256,256]{1,0:T(8,128)(2,1)S(1)} %get-tuple-element.13), channel_id=1, source_target_pairs={{0,12},{4,8},{8,4},{12,0},{1,13},{5,9},{9,5},{13,1},{2,14},{6,10},... | collective-permute-start | bytes 393224 | tf_op jit(solution)/shard_map/ppermute | solution.py:11
  17.2 5.3 %collective-permute-start.6 = (f32[128,128]{1,0:T(8,128)S(1)}, f32[128,128]{1,0:T(8,128)S(1)}, u32[]{:S(2)}, u32[]{:S(2)}) collective-permute-start(f32[128,128]{1,0:T(8,128)S(1)} %fusion.3), channel_id=1, source_target_pairs={{0,1},{1,0},{2,3},{3,2},{4,5},{5,4},{6,7},{7,6},{8,9},{9,8},{10,11... | collective-permute-start | bytes 196616 | tf_op jit(solution)/shard_map/ppermute | solution.py:11
  18.2 7.6 %collective-permute-start.7 = (f32[128,128]{1,0:T(8,128)S(1)}, f32[128,128]{1,0:T(8,128)S(1)}, u32[]{:S(2)}, u32[]{:S(2)}) collective-permute-start(f32[128,128]{1,0:T(8,128)S(1)} %fusion.3), channel_id=1, source_target_pairs={{0,2},{1,3},{2,0},{3,1},{4,6},{5,7},{6,4},{7,5},{8,10},{9,11},{10,... | collective-permute-start | bytes 196616 | tf_op jit(solution)/shard_map/ppermute | solution.py:11
  21.7 6.2 %collective-permute-start.8 = (f32[128,128]{1,0:T(8,128)S(1)}, f32[128,128]{1,0:T(8,128)S(1)}, u32[]{:S(2)}, u32[]{:S(2)}) collective-permute-start(f32[128,128]{1,0:T(8,128)S(1)} %fusion.3), channel_id=1, source_target_pairs={{0,3},{1,2},{2,1},{3,0},{4,7},{5,6},{6,5},{7,4},{8,11},{9,10},{10,... | collective-permute-start | bytes 196616 | tf_op jit(solution)/shard_map/ppermute | solution.py:11
  21.8 6.0 %copy-start = (f32[128,128]{1,0:T(8,128)S(1)}, f32[128,128]{1,0:T(8,128)}, u32[]{:S(2)}) copy-start(f32[128,128]{1,0:T(8,128)} %param.7) | copy-start | bytes 196612

commit v3 on v1

--- a/solution.py
+++ b/solution.py
@@ -1,6 +1,8 @@
 import jax
 import jax.numpy as jnp
 from jax import lax
+from jax.experimental import pallas as pl
+from jax.experimental.pallas import tpu as pltpu
 from jax.sharding import PartitionSpec as P
 
 
@@ -33,7 +35,7 @@
     )
 
 
-def per_device(green_top, factor_cols, fill_blocks, diag_inverse):
+def wide_device(green_top, factor_cols, fill_blocks, diag_inverse):
     row_index = lax.axis_index("row")
     col_index = lax.axis_index("col")
     row_count = lax.axis_size("row")
@@ -129,6 +131,175 @@
     return (green_cols, diag_inverse - sums[0])
 
 
+def places(fill, k, start, count, wanted):
+    found = [0] * wanted
+    rank = 0
+    for b in range(count):
+        one = fill[k, start + b]
+        for p in range(wanted):
+            found[p] = jnp.where((one == 1) & (rank == p), b, found[p])
+        rank = rank + one
+    return found
+
+
+def block(at, size):
+    return pl.ds(pl.multiple_of(at * size, size), size)
+
+
+def pack_kernel(
+    row_count, col_count, fill_in, green_in, factor_in, own_factor, mask, *refs
+):
+    greens, (fill, green, factor, sems) = refs[:row_count], refs[row_count:]
+    copies = [
+        pltpu.make_async_copy(source, target, sems.at[n])
+        for n, (source, target) in enumerate(
+            [(fill_in, fill), (factor_in, factor), (green_in, green)]
+        )
+    ]
+    for one in copies:
+        one.start()
+    row_index = lax.axis_index("row")
+    col_index = lax.axis_index("col")
+    blocks = fill.shape[1]
+    size = factor.shape[1] // blocks
+    group = blocks // col_count
+    half = group // 2
+    chunk = blocks // row_count
+    kept = chunk // 2
+    copies[0].wait()
+    chosen = [
+        (
+            places(fill, row_index ^ s, col_index * group, group, half),
+            places(fill, row_index ^ s, row_index * chunk, chunk, kept),
+        )
+        for s in range(row_count)
+    ]
+    own = [
+        part * chunk + b
+        for part in range(row_count)
+        for b in places(fill, row_index, part * chunk, chunk, kept)
+    ]
+    for p, r in enumerate(chosen[0][0]):
+        for b in range(group):
+            mask[p : p + 1, b * size : (b + 1) * size] = jnp.full(
+                (1, size), jnp.where(r == b, 1.0, 0.0), jnp.float32
+            )
+    copies[1].wait()
+    for p, b in enumerate(own):
+        own_factor[:, p * size : (p + 1) * size] = factor[:, block(b, size)]
+    copies[2].wait()
+    for s, (rows, cols) in enumerate(chosen):
+        for p, r in enumerate(rows):
+            for q, c in enumerate(cols):
+                greens[s][p * size : (p + 1) * size, q * size : (q + 1) * size] = green[
+                    block(r, size), block(c, size)
+                ]
+
+
+def pack(green_top, factor_cols, fill_blocks):
+    row_count = lax.axis_size("row")
+    col_count = lax.axis_size("col")
+    local_rows, order = factor_cols.shape
+    blocks = fill_blocks.shape[1]
+    size = order // blocks
+    group = blocks // col_count
+    half = group // 2
+    kept = blocks // row_count // 2
+    shapes = [
+        pltpu.VMEM((local_rows, row_count * kept * size), jnp.bfloat16),
+        pltpu.VMEM((half, group * size), jnp.float32),
+    ] + [pltpu.VMEM((half * size, kept * size), jnp.bfloat16)] * row_count
+    return pl.pallas_call(
+        lambda *refs: pack_kernel(row_count, col_count, *refs),
+        out_shape=shapes,
+        in_specs=[pl.BlockSpec(memory_space=pltpu.HBM)] * 3,
+        out_specs=[pl.BlockSpec(memory_space=pltpu.VMEM)] * len(shapes),
+        scratch_shapes=[
+            pltpu.SMEM(fill_blocks.shape, fill_blocks.dtype),
+            pltpu.VMEM(green_top.shape, green_top.dtype),
+            pltpu.VMEM(factor_cols.shape, factor_cols.dtype),
+            pltpu.SemaphoreType.DMA((3,)),
+        ],
+        name="pack",
+    )(fill_blocks, green_top, factor_cols)
+
+
+def solve_kernel(row_count, col_count, *refs):
+    factors, refs = refs[:col_count], refs[col_count:]
+    greens, (solved, partial_value, factor) = refs[:row_count], refs[row_count:]
+    row_index = lax.axis_index("row")
+    col_index = lax.axis_index("col")
+    local_rows = factors[0].shape[0]
+    rows, width = greens[0].shape
+    for t in range(col_count):
+        factor[block(col_index ^ t, local_rows), :] = factors[t][...]
+    total = jnp.zeros(solved.shape, jnp.float32)
+    for s in range(row_count):
+        total = total + lax.dot_general(
+            factor[:, block(row_index ^ s, width)],
+            greens[s][...],
+            (((1,), (1,)), ((), ())),
+            preferred_element_type=jnp.float32,
+        )
+    total = -total
+    solved[...] = total
+    pieces = []
+    rest = total
+    for _ in range(3):
+        pieces.append(rest.astype(jnp.bfloat16))
+        rest = rest - pieces[-1].astype(jnp.float32)
+    own = factor[:, block(col_index, rows)]
+    value = 0.0
+    for piece in pieces[::-1]:
+        value = value + lax.dot_general(
+            piece, own, (((1,), (1,)), ((), ())), preferred_element_type=jnp.float32
+        )
+    partial_value[...] = value
+
+
+def solve(factors, greens):
+    col_count, row_count = len(factors), len(greens)
+    local_rows, columns = factors[0].shape
+    count = col_count * local_rows
+    return pl.pallas_call(
+        lambda *refs: solve_kernel(row_count, col_count, *refs),
+        out_shape=[
+            pltpu.VMEM((count, greens[0].shape[0]), jnp.float32),
+            pltpu.VMEM((count, count), jnp.float32),
+        ],
+        in_specs=[pl.BlockSpec(memory_space=pltpu.VMEM)] * (row_count + col_count),
+        out_specs=[pl.BlockSpec(memory_space=pltpu.VMEM)] * 2,
+        scratch_shapes=[pltpu.VMEM((count, columns), jnp.bfloat16)],
+        compiler_params=pltpu.CompilerParams(vmem_limit_bytes=32 * 1024 * 1024),
+        name="solve",
+    )(*factors, *greens)
+
+
+def per_device(green_top, factor_cols, fill_blocks, diag_inverse):
+    row_count = lax.axis_size("row")
+    col_count = lax.axis_size("col")
+    blocks = fill_blocks.shape[1]
+    chunk = blocks // row_count
+    group = blocks // col_count
+    if chunk % group or green_top.size > 1 << 20:
+        return wide_device(green_top, factor_cols, fill_blocks, diag_inverse)
+    half = group // 2
+    size = factor_cols.shape[1] // blocks
+
+    own_factor, mask, *greens = pack(green_top, factor_cols, fill_blocks)
+    factors = [own_factor] + [partner(own_factor, "col", t) for t in range(1, col_count)]
+    greens = greens[:1] + [partner(greens[s], "row", s) for s in range(1, row_count)]
+    solved, partial_value = solve(factors, greens)
+    green_cols = None
+    for p in range(half):
+        term = mask[p : p + 1] * jnp.tile(solved[:, p * size : (p + 1) * size], (1, group))
+        green_cols = term if green_cols is None else green_cols + term
+    sums = [partial_value] + [partner(partial_value, "col", t) for t in range(1, col_count)]
+    while len(sums) > 1:
+        sums = [a + b for a, b in zip(sums[::2], sums[1::2])]
+    return (green_cols, diag_inverse - sums[0])
+
+
 def solution(mesh):
     placed = (
         P(("pole", "col"), "row"),

time: 48.3 us -> 24.8 us (0.51)
  between operations: 11.5 us -> 0.68 us
  other arithmetic: 9.6 us -> 1.38 us
  local copies, waits for them, and re-layouts: 3.63 us -> 0.12 us
  waiting for transfers between devices: 10.1 us -> 8.27 us
  Pallas kernels: 0 us -> 1.72 us
  matrix products: 1.03 us -> 0 us
    reduce_sum x6 -> x0, other arithmetic: 3.96 us -> none  [filled(): jnp.sum(jnp.where((line == 1) & (rank == p), place, 0))]
    another operation x12 -> x0, other arithmetic: 2.1 us -> none
    ppermute x9, waiting for transfers between devices: 10.1 us -> 8.27 us  [partner(): return lax.ppermute(value, axis, [(a, a ^ step) for a in range(size)])]
    pallas_call x0 -> x2, Pallas kernels: none -> 1.72 us  [the longest x1 1.18 us: pack(): pl.pallas_call(lambda *refs: pack_kernel(row_count, col_count, *refs), ou...]
    eq x12 -> x0, other arithmetic: 1.44 us -> none  [filled(): line == 1]
    dynamic_slice x3 -> x0, local copies, waits for them, and re-layouts: 1.28 us -> none  [the longest x1 1.21 us: fill_of(): return lax.dynamic_slice(fill_blocks, (k, start), (1, count))[0]]
    unnamed x20 -> x3, local copies, waits for them, and re-layouts: 1.21 us -> 0.03 us
    slice x2 -> x0, local copies, waits for them, and re-layouts: 1.1 us -> none  [the longest x1 0.58 us: per_device(): rank[b] == p]
  transfers between devices with their start and end apart: 9 -> 9, of which waited for: 3 -> 6; matrix products, arithmetic and copies ran while one was open for 17% -> 3% of each run, Pallas kernels for 0% -> 0%
where the time goes in v3:
time: 24.8 us; the launch traced here: 24.6 us
  starting transfers between devices  12.5 us (50%)
  waiting for transfers between devices  8.27 us (33%)
  Pallas kernels  1.72 us (7%)
  other arithmetic  1.38 us (6%)
  between operations  0.68 us (3%)
    ppermute x9, starting transfers between devices, partner(): return lax.ppermute(value, axis, [(a, a ^ step) for a in range(size)])  12.5 us
    ppermute x9, waiting for transfers between devices, partner(): return lax.ppermute(value, axis, [(a, a ^ step) for a in range(size)])  8.27 us
    pallas_call x1, Pallas kernels, pack(): pl.pallas_call(lambda *refs: pack_kernel(row_count, col_count, *refs), ou...  1.18 us
    mul x1, other arithmetic, per_device(): mask[p:p + 1] * jnp.tile(solved[:, p * size:(p + 1) * size], (1, group))  0.73 us
    sub x1, other arithmetic, per_device(): return (green_cols, diag_inverse - sums[0])  0.65 us
    pallas_call x1, Pallas kernels, solve(): pl.pallas_call(lambda *refs: solve_kernel(row_count, col_count, *refs), o...  0.54 us
  transfers between devices with their start and end apart: 9, of which 6 were waited for; matrix products, arithmetic and copies ran while one was open for 3% of the time, Pallas kernels for 0%

profile of v3, /device:TPU:0, one launch (start us, length us, event | category | flops | bytes accessed | tf_op | source)
XLA Modules:
  0.0 24.6 jit_solution(17895520608424460667)
XLA Ops:
  0.6 1.2 %pack.1 = (bf16[32,1024]{1,0:T(8,128)(2,1)S(1)}, f32[1,512]{1,0:T(1,128)S(1)}, bf16[256,256]{1,0:T(8,128)(2,1)S(1)}, bf16[256,256]{1,0:T(8,128)(2,1)S(1)}, bf16[...) custom-call(s32[4,8]{1,0:T(4,128)} %refs_0_.1, bf16[512,512]{1,0:T(8,128)(2,1)} %refs_1_.1, bf16[32,2048]{1,0:T(8,128)(2,1)} %refs_2_.1), custom_call_target="tpu_custom_call" | custom-call | tf_op jit(solution)/shard_map/pack/pallas_call | solution.py:212
  1.8 5.1 %collective-permute-start.2 = (bf16[32,1024]{1,0:T(8,128)(2,1)S(1)}, bf16[32,1024]{1,0:T(8,128)(2,1)S(1)}, u32[]{:S(2)}, u32[]{:S(2)}) collective-permute-start(bf16[32,1024]{1,0:T(8,128)(2,1)S(1)} %get-tuple-element.11.refs_0_), channel_id=1, source_target_pairs={{0,3},{1,2},{2,1},{3,0},{4,7},{5,6},{6,5},{7,4},{8,11},{9,10},{10,... | collective-permute-start | bytes 196616 | tf_op jit(solution)/shard_map/ppermute | solution.py:11
  6.9 0.0 collective-permute-start.3
  6.9 1.5 %collective-permute-start.4 = (bf16[256,256]{1,0:T(8,128)(2,1)S(1)}, bf16[256,256]{1,0:T(8,128)(2,1)S(1)}, u32[]{:S(2)}, u32[]{:S(2)}) collective-permute-start(bf16[256,256]{1,0:T(8,128)(2,1)S(1)} %get-tuple-element.14), channel_id=1, source_target_pairs={{0,8},{4,12},{8,0},{12,4},{1,9},{5,13},{9,1},{13,5},{2,10},{6,14},... | collective-permute-start | bytes 393224 | tf_op jit(solution)/shard_map/ppermute | solution.py:11
  8.4 0.4 %collective-permute-start.5 = (bf16[256,256]{1,0:T(8,128)(2,1)S(1)}, bf16[256,256]{1,0:T(8,128)(2,1)S(1)}, u32[]{:S(2)}, u32[]{:S(2)}) collective-permute-start(bf16[256,256]{1,0:T(8,128)(2,1)S(1)} %get-tuple-element.15), channel_id=1, source_target_pairs={{0,12},{4,8},{8,4},{12,0},{1,13},{5,9},{9,5},{13,1},{2,14},{6,10},... | collective-permute-start | bytes 393224 | tf_op jit(solution)/shard_map/ppermute | solution.py:11
  8.8 0.0 collective-permute-start.1
  8.8 0.4 %collective-permute-done.2.refs_3_ = bf16[32,1024]{1,0:T(8,128)(2,1)S(1)} collective-permute-done((bf16[32,1024]{1,0:T(8,128)(2,1)S(1)}, bf16[32,1024]{1,0:T(8,128)(2,1)S(1)}, u32[]{:S(2)}, u32[]{:S(2)}) %collective-permute-start.2) | collective-permute-done | bytes 65568 | tf_op jit(solution)/shard_map/ppermute | solution.py:11
  9.2 1.1 %collective-permute-start = (bf16[32,1024]{1,0:T(8,128)(2,1)S(1)}, bf16[32,1024]{1,0:T(8,128)(2,1)S(1)}, u32[]{:S(2)}, u32[]{:S(2)}) collective-permute-start(bf16[32,1024]{1,0:T(8,128)(2,1)S(1)} %get-tuple-element.11.refs_0_), channel_id=1, source_target_pairs={{0,1},{1,0},{2,3},{3,2},{4,5},{5,4},{6,7},{7,6},{8,9},{9,8},{10,11... | collective-permute-start | bytes 196616 | tf_op jit(solution)/shard_map/ppermute | solution.py:11
  10.3 4.2 %collective-permute-done.1.refs_2_ = bf16[32,1024]{1,0:T(8,128)(2,1)S(1)} collective-permute-done((bf16[32,1024]{1,0:T(8,128)(2,1)S(1)}, bf16[32,1024]{1,0:T(8,128)(2,1)S(1)}, u32[]{:S(2)}, u32[]{:S(2)}) %collective-permute-start.1) | collective-permute-done | bytes 65568 | tf_op jit(solution)/shard_map/ppermute | solution.py:11
  14.5 0.4 %collective-permute-done.refs_1_ = bf16[32,1024]{1,0:T(8,128)(2,1)S(1)} collective-permute-done((bf16[32,1024]{1,0:T(8,128)(2,1)S(1)}, bf16[32,1024]{1,0:T(8,128)(2,1)S(1)}, u32[]{:S(2)}, u32[]{:S(2)}) %collective-permute-start) | collective-permute-done | bytes 65568 | tf_op jit(solution)/shard_map/ppermute | solution.py:11
  14.9 0.0 collective-permute-done.3.refs_5_
  14.9 0.0 collective-permute-done.4.refs_6_
  14.9 0.4 %collective-permute-done.5.refs_7_ = bf16[256,256]{1,0:T(8,128)(2,1)S(1)} collective-permute-done((bf16[256,256]{1,0:T(8,128)(2,1)S(1)}, bf16[256,256]{1,0:T(8,128)(2,1)S(1)}, u32[]{:S(2)}, u32[]{:S(2)}) %collective-permute-start.5) | collective-permute-done | bytes 131104 | tf_op jit(solution)/shard_map/ppermute | solution.py:11
  15.3 0.5 %solve.1 = (f32[128,256]{1,0:T(8,128)S(1)}, f32[128,128]{1,0:T(8,128)S(1)}) custom-call(bf16[32,1024]{1,0:T(8,128)(2,1)S(1)} %get-tuple-element.11.refs_0_, bf16[32,1024]{1,0:T(8,128)(2,1)S(1)} %collective-permute-done.refs_1_, bf16[32,1024]{1,0:T(8,128)(2,1)S(1)} %collective-permute-done.1.refs_2_, bf16[32,1024]{1,0:T(8,128)(2,1)S(1)} %collective-permute-done.2.refs_3_, ...), custom_call_target="tpu_custom_call" | custom-call | tf_op jit(solution)/shard_map/solve/pallas_call | solution.py:264
  15.8 2.1 %collective-permute-start.8 = (f32[128,128]{1,0:T(8,128)S(1)}, f32[128,128]{1,0:T(8,128)S(1)}, u32[]{:S(2)}, u32[]{:S(2)}) collective-permute-start(f32[128,128]{1,0:T(8,128)S(1)} %get-tuple-element.17), channel_id=1, source_target_pairs={{0,3},{1,2},{2,1},{3,0},{4,7},{5,6},{6,5},{7,4},{8,11},{9,10},{10,... | collective-permute-start | bytes 196616 | tf_op jit(solution)/shard_map/ppermute | solution.py:11
  17.9 0.0 collective-permute-start.7
  17.9 2.3 %collective-permute-start.6 = (f32[128,128]{1,0:T(8,128)S(1)}, f32[128,128]{1,0:T(8,128)S(1)}, u32[]{:S(2)}, u32[]{:S(2)}) collective-permute-start(f32[128,128]{1,0:T(8,128)S(1)} %get-tuple-element.17), channel_id=1, source_target_pairs={{0,1},{1,0},{2,3},{3,2},{4,5},{5,4},{6,7},{7,6},{8,9},{9,8},{10,11... | collective-permute-start | bytes 196616 | tf_op jit(solution)/shard_map/ppermute | solution.py:11
  20.3 0.1 tile.4
  20.4 0.0 copy-start
  20.4 0.7 %broadcast_multiply_fusion = f32[128,512]{1,0:T(8,128)} fusion(f32[128,512]{1,0:T(8,128)S(1)} %bitcast.4, f32[512]{0:T(512)S(1)} %bitcast.3), kind=kLoop, calls=%fused_computation | loop fusion | flops 65536 | bytes 526336 | tf_op jit(solution)/shard_map/mul | solution.py:295
  21.1 1.5 %collective-permute-done.8 = f32[128,128]{1,0:T(8,128)S(1)} collective-permute-done((f32[128,128]{1,0:T(8,128)S(1)}, f32[128,128]{1,0:T(8,128)S(1)}, u32[]{:S(2)}, u32[]{:S(2)}) %collective-permute-start.8) | collective-permute-done | bytes 65568 | tf_op jit(solution)/shard_map/ppermute | solution.py:11
  22.6 1.4 %collective-permute-done.7 = f32[128,128]{1,0:T(8,128)S(1)} collective-permute-done((f32[128,128]{1,0:T(8,128)S(1)}, f32[128,128]{1,0:T(8,128)S(1)}, u32[]{:S(2)}, u32[]{:S(2)}) %collective-permute-start.7) | collective-permute-done | bytes 65568 | tf_op jit(solution)/shard_map/ppermute | solution.py:11
  24.0 0.0 collective-permute-done.6
  24.0 0.0 copy-done
  24.0 0.7 %add_subtract_fusion = f32[128,128]{1,0:T(8,128)} fusion(f32[128,128]{1,0:T(8,128)S(1)} %copy-done, f32[128,128]{1,0:T(8,128)S(1)} %collective-permute-done.7, f32[128,128]{1,0:T(8,128)S(1)} %collective-permute-done.8, f32[128,128]{1,0:T(8,128)S(1)} %get-tuple-element.17, f32[128,128]{1,0:T(8,128)S(1)} %collective-permute-done.6), kind=kLoop, calls=%fused_computation.1 | loop fusion | flops 65536 | bytes 393216 | tf_op jit(solution)/shard_map/sub | solution.py:300
  (1 shorter events, 0.0 us)
Async XLA Ops:
  1.8 7.4 %collective-permute-start.2 = (bf16[32,1024]{1,0:T(8,128)(2,1)S(1)}, bf16[32,1024]{1,0:T(8,128)(2,1)S(1)}, u32[]{:S(2)}, u32[]{:S(2)}) collective-permute-start(bf16[32,1024]{1,0:T(8,128)(2,1)S(1)} %get-tuple-element.11.refs_0_), channel_id=1, source_target_pairs={{0,3},{1,2},{2,1},{3,0},{4,7},{5,6},{6,5},{7,4},{8,11},{9,10},{10,... | collective-permute-start | bytes 196616 | tf_op jit(solution)/shard_map/ppermute | solution.py:11
  6.9 8.0 %collective-permute-start.3 = (bf16[256,256]{1,0:T(8,128)(2,1)S(1)}, bf16[256,256]{1,0:T(8,128)(2,1)S(1)}, u32[]{:S(2)}, u32[]{:S(2)}) collective-permute-start(bf16[256,256]{1,0:T(8,128)(2,1)S(1)} %get-tuple-element.13), channel_id=1, source_target_pairs={{0,4},{4,0},{8,12},{12,8},{1,5},{5,1},{9,13},{13,9},{2,6},{6,2},{1... | collective-permute-start | bytes 393224 | tf_op jit(solution)/shard_map/ppermute | solution.py:11
  6.9 8.0 %collective-permute-start.4 = (bf16[256,256]{1,0:T(8,128)(2,1)S(1)}, bf16[256,256]{1,0:T(8,128)(2,1)S(1)}, u32[]{:S(2)}, u32[]{:S(2)}) collective-permute-start(bf16[256,256]{1,0:T(8,128)(2,1)S(1)} %get-tuple-element.14), channel_id=1, source_target_pairs={{0,8},{4,12},{8,0},{12,4},{1,9},{5,13},{9,1},{13,5},{2,10},{6,14},... | collective-permute-start | bytes 393224 | tf_op jit(solution)/shard_map/ppermute | solution.py:11
  8.4 6.8 %collective-permute-start.5 = (bf16[256,256]{1,0:T(8,128)(2,1)S(1)}, bf16[256,256]{1,0:T(8,128)(2,1)S(1)}, u32[]{:S(2)}, u32[]{:S(2)}) collective-permute-start(bf16[256,256]{1,0:T(8,128)(2,1)S(1)} %get-tuple-element.15), channel_id=1, source_target_pairs={{0,12},{4,8},{8,4},{12,0},{1,13},{5,9},{9,5},{13,1},{2,14},{6,10},... | collective-permute-start | bytes 393224 | tf_op jit(solution)/shard_map/ppermute | solution.py:11
  8.8 5.7 %collective-permute-start.1 = (bf16[32,1024]{1,0:T(8,128)(2,1)S(1)}, bf16[32,1024]{1,0:T(8,128)(2,1)S(1)}, u32[]{:S(2)}, u32[]{:S(2)}) collective-permute-start(bf16[32,1024]{1,0:T(8,128)(2,1)S(1)} %get-tuple-element.11.refs_0_), channel_id=1, source_target_pairs={{0,2},{1,3},{2,0},{3,1},{4,6},{5,7},{6,4},{7,5},{8,10},{9,11},{10,... | collective-permute-start | bytes 196616 | tf_op jit(solution)/shard_map/ppermute | solution.py:11
  9.2 5.6 %collective-permute-start = (bf16[32,1024]{1,0:T(8,128)(2,1)S(1)}, bf16[32,1024]{1,0:T(8,128)(2,1)S(1)}, u32[]{:S(2)}, u32[]{:S(2)}) collective-permute-start(bf16[32,1024]{1,0:T(8,128)(2,1)S(1)} %get-tuple-element.11.refs_0_), channel_id=1, source_target_pairs={{0,1},{1,0},{2,3},{3,2},{4,5},{5,4},{6,7},{7,6},{8,9},{9,8},{10,11... | collective-permute-start | bytes 196616 | tf_op jit(solution)/shard_map/ppermute | solution.py:11
  15.8 6.8 %collective-permute-start.8 = (f32[128,128]{1,0:T(8,128)S(1)}, f32[128,128]{1,0:T(8,128)S(1)}, u32[]{:S(2)}, u32[]{:S(2)}) collective-permute-start(f32[128,128]{1,0:T(8,128)S(1)} %get-tuple-element.17), channel_id=1, source_target_pairs={{0,3},{1,2},{2,1},{3,0},{4,7},{5,6},{6,5},{7,4},{8,11},{9,10},{10,... | collective-permute-start | bytes 196616 | tf_op jit(solution)/shard_map/ppermute | solution.py:11
  17.9 6.0 %collective-permute-start.7 = (f32[128,128]{1,0:T(8,128)S(1)}, f32[128,128]{1,0:T(8,128)S(1)}, u32[]{:S(2)}, u32[]{:S(2)}) collective-permute-start(f32[128,128]{1,0:T(8,128)S(1)} %get-tuple-element.17), channel_id=1, source_target_pairs={{0,2},{1,3},{2,0},{3,1},{4,6},{5,7},{6,4},{7,5},{8,10},{9,11},{10,... | collective-permute-start | bytes 196616 | tf_op jit(solution)/shard_map/ppermute | solution.py:11
  17.9 6.1 %collective-permute-start.6 = (f32[128,128]{1,0:T(8,128)S(1)}, f32[128,128]{1,0:T(8,128)S(1)}, u32[]{:S(2)}, u32[]{:S(2)}) collective-permute-start(f32[128,128]{1,0:T(8,128)S(1)} %get-tuple-element.17), channel_id=1, source_target_pairs={{0,1},{1,0},{2,3},{3,2},{4,5},{5,4},{6,7},{7,6},{8,9},{9,8},{10,11... | collective-permute-start | bytes 196616 | tf_op jit(solution)/shard_map/ppermute | solution.py:11
  20.4 3.6 %copy-start = (f32[128,128]{1,0:T(8,128)S(1)}, f32[128,128]{1,0:T(8,128)}, u32[]{:S(2)}) copy-start(f32[128,128]{1,0:T(8,128)} %param.7) | copy-start | bytes 196612

commit v4 on v3

--- a/solution.py
+++ b/solution.py
@@ -4,6 +4,10 @@
 from jax.experimental import pallas as pl
 from jax.experimental.pallas import tpu as pltpu
 from jax.sharding import PartitionSpec as P
+
+
+EXPONENT_ROWS = 16
+OPERANDS = (0, 4, 6, 7, 2, 1, 5, 3)
 
 
 def partner(value, axis, step):
@@ -224,9 +228,17 @@
     )(fill_blocks, green_top, factor_cols)
 
 
+def split(given, row_count, col_count):
+    order = OPERANDS if (row_count, col_count) == (4, 4) else range(row_count + col_count)
+    placed = dict(zip(order, given))
+    return [placed[n] for n in range(col_count)], [
+        placed[col_count + n] for n in range(row_count)
+    ]
+
+
 def solve_kernel(row_count, col_count, *refs):
-    factors, refs = refs[:col_count], refs[col_count:]
-    greens, (solved, partial_value, factor) = refs[:row_count], refs[row_count:]
+    given, (solved, coded, factor) = refs[: row_count + col_count], refs[row_count + col_count :]
+    factors, greens = split(given, row_count, col_count)
     row_index = lax.axis_index("row")
     col_index = lax.axis_index("col")
     local_rows = factors[0].shape[0]
@@ -254,7 +266,14 @@
         value = value + lax.dot_general(
             piece, own, (((1,), (1,)), ((), ())), preferred_element_type=jnp.float32
         )
-    partial_value[...] = value
+    largest = jnp.max(jnp.abs(value), axis=0, keepdims=True)
+    exponent = jnp.floor(jnp.log2(jnp.maximum(largest, 2.0**-100)))
+    scaled = jnp.round(value * jnp.exp2(14.0 - exponent))
+    count = value.shape[0]
+    coded[:count, :] = jnp.clip(scaled, -32767.0, 32767.0).astype(jnp.int32).astype(jnp.int16)
+    coded[count:, :] = jnp.broadcast_to(
+        exponent.astype(jnp.int32), (EXPONENT_ROWS, value.shape[1])
+    ).astype(jnp.int16)
 
 
 def solve(factors, greens):
@@ -265,14 +284,38 @@
         lambda *refs: solve_kernel(row_count, col_count, *refs),
         out_shape=[
             pltpu.VMEM((count, greens[0].shape[0]), jnp.float32),
-            pltpu.VMEM((count, count), jnp.float32),
+            pltpu.VMEM((count + EXPONENT_ROWS, count), jnp.int16),
         ],
         in_specs=[pl.BlockSpec(memory_space=pltpu.VMEM)] * (row_count + col_count),
         out_specs=[pl.BlockSpec(memory_space=pltpu.VMEM)] * 2,
         scratch_shapes=[pltpu.VMEM((count, columns), jnp.bfloat16)],
         compiler_params=pltpu.CompilerParams(vmem_limit_bytes=32 * 1024 * 1024),
         name="solve",
-    )(*factors, *greens)
+    )(*[(list(factors) + list(greens))[n] for n in (OPERANDS if (row_count, col_count) == (4, 4) else range(row_count + col_count))])
+
+
+def finish_kernel(diag_inverse, *refs):
+    codes, out = refs[:-1], refs[-1]
+    count = diag_inverse.shape[0]
+    sums = []
+    for code in codes:
+        exponent = code[count:, :].astype(jnp.int32).astype(jnp.float32)[:1]
+        sums.append(code[:count, :].astype(jnp.int32).astype(jnp.float32) * jnp.exp2(exponent - 14.0))
+    sums = [sums[n] for n in [0, 1, 3, 2]]
+    while len(sums) > 1:
+        sums = [a + b for a, b in zip(sums[::2], sums[1::2])]
+    out[...] = diag_inverse[...] - sums[0]
+
+
+def finish(diag_inverse, codes):
+    return pl.pallas_call(
+        finish_kernel,
+        out_shape=jax.ShapeDtypeStruct(diag_inverse.shape, diag_inverse.dtype),
+        in_specs=[pl.BlockSpec(memory_space=pltpu.VMEM)] * (1 + len(codes)),
+        out_specs=pl.BlockSpec(memory_space=pltpu.VMEM),
+        compiler_params=pltpu.CompilerParams(vmem_limit_bytes=32 * 1024 * 1024),
+        name="finish",
+    )(diag_inverse, *codes)
 
 
 def per_device(green_top, factor_cols, fill_blocks, diag_inverse):
@@ -287,17 +330,24 @@
     size = factor_cols.shape[1] // blocks
 
     own_factor, mask, *greens = pack(green_top, factor_cols, fill_blocks)
-    factors = [own_factor] + [partner(own_factor, "col", t) for t in range(1, col_count)]
-    greens = greens[:1] + [partner(greens[s], "row", s) for s in range(1, row_count)]
-    solved, partial_value = solve(factors, greens)
+    far, cross = partner(greens[2], "row", 2), partner(greens[3], "row", 3)
+    near = partner(greens[1], "row", 1)
+    parts = {"c": near, "x": far, "xc": cross}
+    parts["z2"] = partner(own_factor, "col", 2)
+    parts["z1"] = partner(own_factor, "col", 1)
+    held = []
+    passed, *rest = lax.optimization_barrier((parts["z2"], *[parts[n] for n in held]))
+    parts.update(zip(held, rest))
+    parts["z3"] = partner(passed, "col", 1)
+    greens = [greens[0], parts["c"], parts["x"], parts["xc"]]
+    factors = [own_factor] + [parts["z%d" % t] for t in range(1, col_count)]
+    solved, code = solve(factors, greens)
     green_cols = None
     for p in range(half):
         term = mask[p : p + 1] * jnp.tile(solved[:, p * size : (p + 1) * size], (1, group))
         green_cols = term if green_cols is None else green_cols + term
-    sums = [partial_value] + [partner(partial_value, "col", t) for t in range(1, col_count)]
-    while len(sums) > 1:
-        sums = [a + b for a, b in zip(sums[::2], sums[1::2])]
-    return (green_cols, diag_inverse - sums[0])
+    codes = [code] + [partner(code, "col", t) for t in [1, 3, 2]]
+    return (green_cols, finish(diag_inverse, codes))
 
 
 def solution(mesh):

time: 24.8 us -> 23.3 us (0.940)
  waiting for transfers between devices: 8.27 us -> 6.79 us
  Pallas kernels: 1.72 us -> 2.44 us
  other arithmetic: 1.38 us -> 0.73 us
    ppermute x9, waiting for transfers between devices: 8.27 us -> 6.79 us  [partner(): return lax.ppermute(value, axis, [(a, a ^ step) for a in range(size)])]
    pallas_call x0 -> x1, Pallas kernels: none -> 0.67 us  [finish(): pl.pallas_call(finish_kernel, out_shape=jax.ShapeDtypeStruct(diag_inverse...]
    sub x1 -> x0, other arithmetic: 0.65 us -> none  [per_device(): return (green_cols, diag_inverse - sums[0])]
  transfers between devices with their start and end apart: 9 -> 9, of which waited for: 6 -> 4; matrix products, arithmetic and copies ran while one was open for 3% -> 4% of each run, Pallas kernels for 0% -> 0%
where the time goes in v4:
time: 23.3 us; the launch traced here: 23.1 us
  starting transfers between devices  12.4 us (53%)
  waiting for transfers between devices  6.79 us (29%)
  Pallas kernels  2.44 us (10%)
  other arithmetic  0.73 us (3%)
  between operations  0.68 us (3%)
    ppermute x9, starting transfers between devices, partner(): return lax.ppermute(value, axis, [(a, a ^ step) for a in range(size)])  12.4 us
    ppermute x9, waiting for transfers between devices, partner(): return lax.ppermute(value, axis, [(a, a ^ step) for a in range(size)])  6.79 us
    pallas_call x1, Pallas kernels, pack(): pl.pallas_call(lambda *refs: pack_kernel(row_count, col_count, *refs), ou...  1.18 us
    mul x1, other arithmetic, per_device(): mask[p:p + 1] * jnp.tile(solved[:, p * size:(p + 1) * size], (1, group))  0.73 us
    pallas_call x1, Pallas kernels, finish(): pl.pallas_call(finish_kernel, out_shape=jax.ShapeDtypeStruct(diag_inverse...  0.67 us
    pallas_call x1, Pallas kernels, solve(): pl.pallas_call(lambda *refs: solve_kernel(row_count, col_count, *refs), o...  0.58 us
  transfers between devices with their start and end apart: 9, of which 4 were waited for; matrix products, arithmetic and copies ran while one was open for 4% of the time, Pallas kernels for 0%

profile of v4, /device:TPU:0, one launch (start us, length us, event | category | flops | bytes accessed | tf_op | source)
XLA Modules:
  0.0 23.1 jit_solution(3740466066987798946)
XLA Ops:
  0.6 1.2 %pack.1 = (bf16[32,1024]{1,0:T(8,128)(2,1)S(1)}, f32[1,512]{1,0:T(1,128)S(1)}, bf16[256,256]{1,0:T(8,128)(2,1)S(1)}, bf16[256,256]{1,0:T(8,128)(2,1)S(1)}, bf16[...) custom-call(s32[4,8]{1,0:T(4,128)} %refs_0_.1, bf16[512,512]{1,0:T(8,128)(2,1)} %refs_1_.1, bf16[32,2048]{1,0:T(8,128)(2,1)} %refs_2_.1), custom_call_target="tpu_custom_call" | custom-call | tf_op jit(solution)/shard_map/pack/pallas_call | solution.py:216
  1.8 4.1 %collective-permute-start.2 = (bf16[32,1024]{1,0:T(8,128)(2,1)S(1)}, bf16[32,1024]{1,0:T(8,128)(2,1)S(1)}, u32[]{:S(2)}, u32[]{:S(2)}) collective-permute-start(bf16[32,1024]{1,0:T(8,128)(2,1)S(1)} %get-tuple-element.11.refs_0_), channel_id=1, source_target_pairs={{0,2},{1,3},{2,0},{3,1},{4,6},{5,7},{6,4},{7,5},{8,10},{9,11},{10,... | collective-permute-start | bytes 196616 | tf_op jit(solution)/shard_map/ppermute | solution.py:15
  5.9 1.5 %collective-permute-start = (bf16[256,256]{1,0:T(8,128)(2,1)S(1)}, bf16[256,256]{1,0:T(8,128)(2,1)S(1)}, u32[]{:S(2)}, u32[]{:S(2)}) collective-permute-start(bf16[256,256]{1,0:T(8,128)(2,1)S(1)} %get-tuple-element.13), channel_id=1, source_target_pairs={{0,8},{4,12},{8,0},{12,4},{1,9},{5,13},{9,1},{13,5},{2,10},{6,14},... | collective-permute-start | bytes 393224 | tf_op jit(solution)/shard_map/ppermute | solution.py:15
  7.4 0.0 collective-permute-start.1
  7.4 0.6 %collective-permute-start.4 = (bf16[256,256]{1,0:T(8,128)(2,1)S(1)}, bf16[256,256]{1,0:T(8,128)(2,1)S(1)}, u32[]{:S(2)}, u32[]{:S(2)}) collective-permute-start(bf16[256,256]{1,0:T(8,128)(2,1)S(1)} %get-tuple-element.15), channel_id=1, source_target_pairs={{0,4},{4,0},{8,12},{12,8},{1,5},{5,1},{9,13},{13,9},{2,6},{6,2},{1... | collective-permute-start | bytes 393224 | tf_op jit(solution)/shard_map/ppermute | solution.py:15
  8.1 1.6 %collective-permute-start.3 = (bf16[32,1024]{1,0:T(8,128)(2,1)S(1)}, bf16[32,1024]{1,0:T(8,128)(2,1)S(1)}, u32[]{:S(2)}, u32[]{:S(2)}) collective-permute-start(bf16[32,1024]{1,0:T(8,128)(2,1)S(1)} %get-tuple-element.11.refs_0_), channel_id=1, source_target_pairs={{0,1},{1,0},{2,3},{3,2},{4,5},{5,4},{6,7},{7,6},{8,9},{9,8},{10,11... | collective-permute-start | bytes 196616 | tf_op jit(solution)/shard_map/ppermute | solution.py:15
  9.6 0.0 collective-permute-done.2.refs_4_
  9.6 0.5 %collective-permute-start.5 = (bf16[32,1024]{1,0:T(8,128)(2,1)S(1)}, bf16[32,1024]{1,0:T(8,128)(2,1)S(1)}, u32[]{:S(2)}, u32[]{:S(2)}) collective-permute-start(bf16[32,1024]{1,0:T(8,128)(2,1)S(1)} %collective-permute-done.2.refs_4_), channel_id=1, source_target_pairs={{0,1},{1,0},{2,3},{3,2},{4,5},{5,4},{6,7},{7,6},{8,9},{9,8},{10,11... | collective-permute-start | bytes 196616 | tf_op jit(solution)/shard_map/ppermute | solution.py:15
  10.1 2.6 %collective-permute-done.3.refs_5_ = bf16[32,1024]{1,0:T(8,128)(2,1)S(1)} collective-permute-done((bf16[32,1024]{1,0:T(8,128)(2,1)S(1)}, bf16[32,1024]{1,0:T(8,128)(2,1)S(1)}, u32[]{:S(2)}, u32[]{:S(2)}) %collective-permute-start.3) | collective-permute-done | bytes 65568 | tf_op jit(solution)/shard_map/ppermute | solution.py:15
  12.7 1.2 %collective-permute-done.5.refs_7_ = bf16[32,1024]{1,0:T(8,128)(2,1)S(1)} collective-permute-done((bf16[32,1024]{1,0:T(8,128)(2,1)S(1)}, bf16[32,1024]{1,0:T(8,128)(2,1)S(1)}, u32[]{:S(2)}, u32[]{:S(2)}) %collective-permute-start.5) | collective-permute-done | bytes 65568 | tf_op jit(solution)/shard_map/ppermute | solution.py:15
  13.9 0.0 collective-permute-done.refs_2_
  13.9 0.0 collective-permute-done.1.refs_3_
  13.9 0.0 collective-permute-done.4.refs_6_
  13.9 0.6 %solve.1 = (f32[128,256]{1,0:T(8,128)S(1)}, s16[144,128]{1,0:T(8,128)(2,1)S(1)}) custom-call(bf16[32,1024]{1,0:T(8,128)(2,1)S(1)} %get-tuple-element.11.refs_0_, bf16[256,256]{1,0:T(8,128)(2,1)S(1)} %get-tuple-element.12.refs_1_, bf16[256,256]{1,0:T(8,128)(2,1)S(1)} %collective-permute-done.refs_2_, bf16[256,256]{1,0:T(8,128)(2,1)S(1)} %collective-permute-done.1.refs_3_, ...), custom_call_target="tpu_custom_call" | custom-call | tf_op jit(solution)/shard_map/solve/pallas_call | solution.py:283
  14.5 2.0 %collective-permute-start.8 = (s16[144,128]{1,0:T(8,128)(2,1)S(1)}, s16[144,128]{1,0:T(8,128)(2,1)S(1)}, u32[]{:S(2)}, u32[]{:S(2)}) collective-permute-start(s16[144,128]{1,0:T(8,128)(2,1)S(1)} %get-tuple-element.17.refs_0_), channel_id=1, source_target_pairs={{0,2},{1,3},{2,0},{3,1},{4,6},{5,7},{6,4},{7,5},{8,10},{9,11},{10,... | collective-permute-start | bytes 110600 | tf_op jit(solution)/shard_map/ppermute | solution.py:15
  16.5 1.5 %collective-permute-start.7 = (s16[144,128]{1,0:T(8,128)(2,1)S(1)}, s16[144,128]{1,0:T(8,128)(2,1)S(1)}, u32[]{:S(2)}, u32[]{:S(2)}) collective-permute-start(s16[144,128]{1,0:T(8,128)(2,1)S(1)} %get-tuple-element.17.refs_0_), channel_id=1, source_target_pairs={{0,3},{1,2},{2,1},{3,0},{4,7},{5,6},{6,5},{7,4},{8,11},{9,10},{10,... | collective-permute-start | bytes 110600 | tf_op jit(solution)/shard_map/ppermute | solution.py:15
  18.1 0.5 %collective-permute-start.6 = (s16[144,128]{1,0:T(8,128)(2,1)S(1)}, s16[144,128]{1,0:T(8,128)(2,1)S(1)}, u32[]{:S(2)}, u32[]{:S(2)}) collective-permute-start(s16[144,128]{1,0:T(8,128)(2,1)S(1)} %get-tuple-element.17.refs_0_), channel_id=1, source_target_pairs={{0,1},{1,0},{2,3},{3,2},{4,5},{5,4},{6,7},{7,6},{8,9},{9,8},{10,11... | collective-permute-start | bytes 110600 | tf_op jit(solution)/shard_map/ppermute | solution.py:15
  18.6 0.1 tile.4
  18.7 0.0 copy-start
  18.7 0.7 %broadcast_multiply_fusion = f32[128,512]{1,0:T(8,128)} fusion(f32[128,512]{1,0:T(8,128)S(1)} %bitcast.4, f32[512]{0:T(512)S(1)} %bitcast.3), kind=kLoop, calls=%fused_computation | loop fusion | flops 65536 | bytes 526336 | tf_op jit(solution)/shard_map/mul | solution.py:347
  19.4 1.4 %collective-permute-done.8.refs_3_ = s16[144,128]{1,0:T(8,128)(2,1)S(1)} collective-permute-done((s16[144,128]{1,0:T(8,128)(2,1)S(1)}, s16[144,128]{1,0:T(8,128)(2,1)S(1)}, u32[]{:S(2)}, u32[]{:S(2)}) %collective-permute-start.8) | collective-permute-done | bytes 36896 | tf_op jit(solution)/shard_map/ppermute | solution.py:15
  20.8 1.6 %collective-permute-done.7.refs_2_ = s16[144,128]{1,0:T(8,128)(2,1)S(1)} collective-permute-done((s16[144,128]{1,0:T(8,128)(2,1)S(1)}, s16[144,128]{1,0:T(8,128)(2,1)S(1)}, u32[]{:S(2)}, u32[]{:S(2)}) %collective-permute-start.7) | collective-permute-done | bytes 36896 | tf_op jit(solution)/shard_map/ppermute | solution.py:15
  22.4 0.0 collective-permute-done.6.refs_1_
  22.4 0.0 copy-done
  22.4 0.7 %finish.1 = f32[128,128]{1,0:T(8,128)} custom-call(f32[128,128]{1,0:T(8,128)S(1)} %copy-done, s16[144,128]{1,0:T(8,128)(2,1)S(1)} %get-tuple-element.17.refs_0_, s16[144,128]{1,0:T(8,128)(2,1)S(1)} %collective-permute-done.6.refs_1_, s16[144,128]{1,0:T(8,128)(2,1)S(1)} %collective-permute-done.7.refs_2_, s16[144,128]{1,0:T(8,128)(2,1)S(1)} %collective-permute-done.8.refs_3_), custom_call_target="tpu_custom_call" | custom-call | tf_op jit(solution)/shard_map/finish/pallas_call | solution.py:311
  (1 shorter events, 0.0 us)
Async XLA Ops:
  1.8 7.8 %collective-permute-start.2 = (bf16[32,1024]{1,0:T(8,128)(2,1)S(1)}, bf16[32,1024]{1,0:T(8,128)(2,1)S(1)}, u32[]{:S(2)}, u32[]{:S(2)}) collective-permute-start(bf16[32,1024]{1,0:T(8,128)(2,1)S(1)} %get-tuple-element.11.refs_0_), channel_id=1, source_target_pairs={{0,2},{1,3},{2,0},{3,1},{4,6},{5,7},{6,4},{7,5},{8,10},{9,11},{10,... | collective-permute-start | bytes 196616 | tf_op jit(solution)/shard_map/ppermute | solution.py:15
  5.9 8.0 %collective-permute-start = (bf16[256,256]{1,0:T(8,128)(2,1)S(1)}, bf16[256,256]{1,0:T(8,128)(2,1)S(1)}, u32[]{:S(2)}, u32[]{:S(2)}) collective-permute-start(bf16[256,256]{1,0:T(8,128)(2,1)S(1)} %get-tuple-element.13), channel_id=1, source_target_pairs={{0,8},{4,12},{8,0},{12,4},{1,9},{5,13},{9,1},{13,5},{2,10},{6,14},... | collective-permute-start | bytes 393224 | tf_op jit(solution)/shard_map/ppermute | solution.py:15
  7.4 6.5 %collective-permute-start.1 = (bf16[256,256]{1,0:T(8,128)(2,1)S(1)}, bf16[256,256]{1,0:T(8,128)(2,1)S(1)}, u32[]{:S(2)}, u32[]{:S(2)}) collective-permute-start(bf16[256,256]{1,0:T(8,128)(2,1)S(1)} %get-tuple-element.14), channel_id=1, source_target_pairs={{0,12},{4,8},{8,4},{12,0},{1,13},{5,9},{9,5},{13,1},{2,14},{6,10},... | collective-permute-start | bytes 393224 | tf_op jit(solution)/shard_map/ppermute | solution.py:15
  7.4 6.5 %collective-permute-start.4 = (bf16[256,256]{1,0:T(8,128)(2,1)S(1)}, bf16[256,256]{1,0:T(8,128)(2,1)S(1)}, u32[]{:S(2)}, u32[]{:S(2)}) collective-permute-start(bf16[256,256]{1,0:T(8,128)(2,1)S(1)} %get-tuple-element.15), channel_id=1, source_target_pairs={{0,4},{4,0},{8,12},{12,8},{1,5},{5,1},{9,13},{13,9},{2,6},{6,2},{1... | collective-permute-start | bytes 393224 | tf_op jit(solution)/shard_map/ppermute | solution.py:15
  8.1 4.6 %collective-permute-start.3 = (bf16[32,1024]{1,0:T(8,128)(2,1)S(1)}, bf16[32,1024]{1,0:T(8,128)(2,1)S(1)}, u32[]{:S(2)}, u32[]{:S(2)}) collective-permute-start(bf16[32,1024]{1,0:T(8,128)(2,1)S(1)} %get-tuple-element.11.refs_0_), channel_id=1, source_target_pairs={{0,1},{1,0},{2,3},{3,2},{4,5},{5,4},{6,7},{7,6},{8,9},{9,8},{10,11... | collective-permute-start | bytes 196616 | tf_op jit(solution)/shard_map/ppermute | solution.py:15
  9.6 4.3 %collective-permute-start.5 = (bf16[32,1024]{1,0:T(8,128)(2,1)S(1)}, bf16[32,1024]{1,0:T(8,128)(2,1)S(1)}, u32[]{:S(2)}, u32[]{:S(2)}) collective-permute-start(bf16[32,1024]{1,0:T(8,128)(2,1)S(1)} %collective-permute-done.2.refs_4_), channel_id=1, source_target_pairs={{0,1},{1,0},{2,3},{3,2},{4,5},{5,4},{6,7},{7,6},{8,9},{9,8},{10,11... | collective-permute-start | bytes 196616 | tf_op jit(solution)/shard_map/ppermute | solution.py:15
  14.5 6.3 %collective-permute-start.8 = (s16[144,128]{1,0:T(8,128)(2,1)S(1)}, s16[144,128]{1,0:T(8,128)(2,1)S(1)}, u32[]{:S(2)}, u32[]{:S(2)}) collective-permute-start(s16[144,128]{1,0:T(8,128)(2,1)S(1)} %get-tuple-element.17.refs_0_), channel_id=1, source_target_pairs={{0,2},{1,3},{2,0},{3,1},{4,6},{5,7},{6,4},{7,5},{8,10},{9,11},{10,... | collective-permute-start | bytes 110600 | tf_op jit(solution)/shard_map/ppermute | solution.py:15
  16.5 5.9 %collective-permute-start.7 = (s16[144,128]{1,0:T(8,128)(2,1)S(1)}, s16[144,128]{1,0:T(8,128)(2,1)S(1)}, u32[]{:S(2)}, u32[]{:S(2)}) collective-permute-start(s16[144,128]{1,0:T(8,128)(2,1)S(1)} %get-tuple-element.17.refs_0_), channel_id=1, source_target_pairs={{0,3},{1,2},{2,1},{3,0},{4,7},{5,6},{6,5},{7,4},{8,11},{9,10},{10,... | collective-permute-start | bytes 110600 | tf_op jit(solution)/shard_map/ppermute | solution.py:15
  18.1 4.4 %collective-permute-start.6 = (s16[144,128]{1,0:T(8,128)(2,1)S(1)}, s16[144,128]{1,0:T(8,128)(2,1)S(1)}, u32[]{:S(2)}, u32[]{:S(2)}) collective-permute-start(s16[144,128]{1,0:T(8,128)(2,1)S(1)} %get-tuple-element.17.refs_0_), channel_id=1, source_target_pairs={{0,1},{1,0},{2,3},{3,2},{4,5},{5,4},{6,7},{7,6},{8,9},{9,8},{10,11... | collective-permute-start | bytes 110600 | tf_op jit(solution)/shard_map/ppermute | solution.py:15
  18.7 3.8 %copy-start = (f32[128,128]{1,0:T(8,128)S(1)}, f32[128,128]{1,0:T(8,128)}, u32[]{:S(2)}) copy-start(f32[128,128]{1,0:T(8,128)} %diag_inverse.1) | copy-start | bytes 196612

commit v5 on v3

--- a/solution.py
+++ b/solution.py
@@ -4,6 +4,13 @@
 from jax.experimental import pallas as pl
 from jax.experimental.pallas import tpu as pltpu
 from jax.sharding import PartitionSpec as P
+
+
+EXPONENT_ROWS = 16
+RING = (1, 3, 0, 2)
+BACK = (2, 0, 3, 1)
+ACROSS = (3, 2, 1, 0)
+VMEM_LIMIT = 32 * 1024 * 1024
 
 
 def partner(value, axis, step):
@@ -224,20 +231,41 @@
     )(fill_blocks, green_top, factor_cols)
 
 
-def solve_kernel(row_count, col_count, *refs):
-    factors, refs = refs[:col_count], refs[col_count:]
-    greens, (solved, partial_value, factor) = refs[:row_count], refs[row_count:]
+def code_of(value, coded):
+    largest = jnp.max(jnp.abs(value), axis=0, keepdims=True)
+    exponent = jnp.floor(jnp.log2(jnp.maximum(largest, 2.0**-100)))
+    scaled = jnp.round(value * jnp.exp2(14.0 - exponent))
+    count = value.shape[0]
+    coded[:count, :] = jnp.clip(scaled, -32767.0, 32767.0).astype(jnp.int32).astype(jnp.int16)
+    coded[count:, :] = jnp.broadcast_to(
+        exponent.astype(jnp.int32), (EXPONENT_ROWS, value.shape[1])
+    ).astype(jnp.int16)
+
+
+def value_of(coded):
+    count = coded.shape[0] - EXPONENT_ROWS
+    exponent = coded[count:, :].astype(jnp.int32).astype(jnp.float32)[:1]
+    return coded[:count, :].astype(jnp.int32).astype(jnp.float32) * jnp.exp2(exponent - 14.0)
+
+
+def solve_kernel(origins, own_factor, own_green, *refs):
+    given, (solved, coded, factor) = refs[:-3], refs[-3:]
     row_index = lax.axis_index("row")
     col_index = lax.axis_index("col")
-    local_rows = factors[0].shape[0]
-    rows, width = greens[0].shape
-    for t in range(col_count):
-        factor[block(col_index ^ t, local_rows), :] = factors[t][...]
+    local_rows = own_factor.shape[0]
+    rows, width = own_green.shape
+    greens = [(0, own_green)]
+    factor[block(col_index, local_rows), :] = own_factor[...]
+    for (axis, step), part in zip(origins, given):
+        if axis == "col":
+            factor[block(col_index ^ step, local_rows), :] = part[...]
+        else:
+            greens.append((step, part))
     total = jnp.zeros(solved.shape, jnp.float32)
-    for s in range(row_count):
+    for step, green in sorted(greens, key=lambda one: one[0]):
         total = total + lax.dot_general(
-            factor[:, block(row_index ^ s, width)],
-            greens[s][...],
+            factor[:, block(row_index ^ step, width)],
+            green[...],
             (((1,), (1,)), ((), ())),
             preferred_element_type=jnp.float32,
         )
@@ -254,25 +282,40 @@
         value = value + lax.dot_general(
             piece, own, (((1,), (1,)), ((), ())), preferred_element_type=jnp.float32
         )
-    partial_value[...] = value
-
-
-def solve(factors, greens):
-    col_count, row_count = len(factors), len(greens)
-    local_rows, columns = factors[0].shape
+    code_of(value, coded)
+
+
+def solve(own_factor, own_green, origins, given, col_count):
+    local_rows, columns = own_factor.shape
     count = col_count * local_rows
     return pl.pallas_call(
-        lambda *refs: solve_kernel(row_count, col_count, *refs),
+        lambda *refs: solve_kernel(origins, *refs),
         out_shape=[
-            pltpu.VMEM((count, greens[0].shape[0]), jnp.float32),
-            pltpu.VMEM((count, count), jnp.float32),
-        ],
-        in_specs=[pl.BlockSpec(memory_space=pltpu.VMEM)] * (row_count + col_count),
+            pltpu.VMEM((count, own_green.shape[0]), jnp.float32),
+            pltpu.VMEM((count + EXPONENT_ROWS, count), jnp.int16),
+        ],
+        in_specs=[pl.BlockSpec(memory_space=pltpu.VMEM)] * (2 + len(given)),
         out_specs=[pl.BlockSpec(memory_space=pltpu.VMEM)] * 2,
         scratch_shapes=[pltpu.VMEM((count, columns), jnp.bfloat16)],
-        compiler_params=pltpu.CompilerParams(vmem_limit_bytes=32 * 1024 * 1024),
+        compiler_params=pltpu.CompilerParams(vmem_limit_bytes=VMEM_LIMIT),
         name="solve",
-    )(*factors, *greens)
+    )(own_factor, own_green, *given)
+
+
+def finish_kernel(diag_inverse, own, back, across, ring, out):
+    total = (value_of(own) + value_of(across)) + (value_of(ring) + value_of(back))
+    out[...] = diag_inverse[...] - total
+
+
+def finish(diag_inverse, codes):
+    return pl.pallas_call(
+        finish_kernel,
+        out_shape=jax.ShapeDtypeStruct(diag_inverse.shape, diag_inverse.dtype),
+        in_specs=[pl.BlockSpec(memory_space=pltpu.VMEM)] * (1 + len(codes)),
+        out_specs=pl.BlockSpec(memory_space=pltpu.VMEM),
+        compiler_params=pltpu.CompilerParams(vmem_limit_bytes=VMEM_LIMIT),
+        name="finish",
+    )(diag_inverse, *codes)
 
 
 def per_device(green_top, factor_cols, fill_blocks, diag_inverse):
@@ -281,23 +324,33 @@
     blocks = fill_blocks.shape[1]
     chunk = blocks // row_count
     group = blocks // col_count
-    if chunk % group or green_top.size > 1 << 20:
+    fits = row_count == 4 and col_count == 4 and chunk % group == 0
+    if not fits or green_top.size > 1 << 20:
         return wide_device(green_top, factor_cols, fill_blocks, diag_inverse)
     half = group // 2
     size = factor_cols.shape[1] // blocks
 
     own_factor, mask, *greens = pack(green_top, factor_cols, fill_blocks)
-    factors = [own_factor] + [partner(own_factor, "col", t) for t in range(1, col_count)]
-    greens = greens[:1] + [partner(greens[s], "row", s) for s in range(1, row_count)]
-    solved, partial_value = solve(factors, greens)
+    second = partner(own_factor, "col", 2)
+    received = {
+        ("row", 2): partner(greens[2], "row", 2),
+        ("row", 3): partner(greens[3], "row", 3),
+        ("row", 1): partner(greens[1], "row", 1),
+        ("col", 2): second,
+        ("col", 1): partner(own_factor, "col", 1),
+        ("col", 3): partner(second, "col", 1),
+    }
+    solved, code = solve(
+        own_factor, greens[0], tuple(received), tuple(received.values()), col_count
+    )
     green_cols = None
     for p in range(half):
         term = mask[p : p + 1] * jnp.tile(solved[:, p * size : (p + 1) * size], (1, group))
         green_cols = term if green_cols is None else green_cols + term
-    sums = [partial_value] + [partner(partial_value, "col", t) for t in range(1, col_count)]
-    while len(sums) > 1:
-        sums = [a + b for a, b in zip(sums[::2], sums[1::2])]
-    return (green_cols, diag_inverse - sums[0])
+    codes = [code] + [
+        lax.ppermute(code, "col", list(enumerate(moves))) for moves in (BACK, ACROSS, RING)
+    ]
+    return (green_cols, finish(diag_inverse, codes))
 
 
 def solution(mesh):

time: 24.8 us -> 22.8 us (0.919)
  waiting for transfers between devices: 8.27 us -> 4.93 us
  starting transfers between devices: 12.5 us -> 13.8 us
  Pallas kernels: 1.72 us -> 2.43 us
  other arithmetic: 1.38 us -> 0.73 us
    ppermute x0 -> x3, starting transfers between devices: none -> 5.49 us  [per_device(): lax.ppermute(code, 'col', list(enumerate(moves)))]
    ppermute x9 -> x6, waiting for transfers between devices: 8.27 us -> 3.78 us  [partner(): return lax.ppermute(value, axis, [(a, a ^ step) for a in range(size)])]
    ppermute x9 -> x6, starting transfers between devices: 12.5 us -> 8.31 us  [partner(): return lax.ppermute(value, axis, [(a, a ^ step) for a in range(size)])]
    ppermute x0 -> x3, waiting for transfers between devices: none -> 1.15 us  [per_device(): lax.ppermute(code, 'col', list(enumerate(moves)))]
    pallas_call x1 -> x2, Pallas kernels: 0.54 us -> 1.25 us  [the longest x1 0.67 us: finish(): pl.pallas_call(finish_kernel, out_shape=jax.ShapeDtypeStruct(diag_inverse...]
    sub x1 -> x0, other arithmetic: 0.65 us -> none  [per_device(): return (green_cols, diag_inverse - sums[0])]
  transfers between devices with their start and end apart: 9 -> 9, of which waited for: 6 -> 4; matrix products, arithmetic and copies ran while one was open for 3% -> 4% of each run, Pallas kernels for 0% -> 0%
where the time goes in v5:
time: 22.8 us; the launch traced here: 22.7 us
  starting transfers between devices  13.8 us (61%)
  waiting for transfers between devices  4.93 us (22%)
  Pallas kernels  2.43 us (11%)
  other arithmetic  0.73 us (3%)
  between operations  0.68 us (3%)
    ppermute x6, starting transfers between devices, partner(): return lax.ppermute(value, axis, [(a, a ^ step) for a in range(size)])  8.31 us
    ppermute x3, starting transfers between devices, per_device(): lax.ppermute(code, 'col', list(enumerate(moves)))  5.49 us
    ppermute x6, waiting for transfers between devices, partner(): return lax.ppermute(value, axis, [(a, a ^ step) for a in range(size)])  3.78 us
    pallas_call x1, Pallas kernels, pack(): pl.pallas_call(lambda *refs: pack_kernel(row_count, col_count, *refs), ou...  1.18 us
    ppermute x3, waiting for transfers between devices, per_device(): lax.ppermute(code, 'col', list(enumerate(moves)))  1.15 us
    mul x1, other arithmetic, per_device(): mask[p:p + 1] * jnp.tile(solved[:, p * size:(p + 1) * size], (1, group))  0.73 us
    pallas_call x1, Pallas kernels, finish(): pl.pallas_call(finish_kernel, out_shape=jax.ShapeDtypeStruct(diag_inverse...  0.67 us
    pallas_call x1, Pallas kernels, solve(): pl.pallas_call(lambda *refs: solve_kernel(origins, *refs), out_shape=[plt...  0.58 us
  transfers between devices with their start and end apart: 9, of which 4 were waited for; matrix products, arithmetic and copies ran while one was open for 4% of the time, Pallas kernels for 0%

profile of v5, /device:TPU:0, one launch (start us, length us, event | category | flops | bytes accessed | tf_op | source)
XLA Modules:
  0.0 22.7 jit_solution(9191503289527914001)
XLA Ops:
  0.6 1.2 %pack.1 = (bf16[32,1024]{1,0:T(8,128)(2,1)S(1)}, f32[1,512]{1,0:T(1,128)S(1)}, bf16[256,256]{1,0:T(8,128)(2,1)S(1)}, bf16[256,256]{1,0:T(8,128)(2,1)S(1)}, bf16[...) custom-call(s32[4,8]{1,0:T(4,128)} %refs_0_.1, bf16[512,512]{1,0:T(8,128)(2,1)} %refs_1_.1, bf16[32,2048]{1,0:T(8,128)(2,1)} %refs_2_.1), custom_call_target="tpu_custom_call" | custom-call | tf_op jit(solution)/shard_map/pack/pallas_call | solution.py:219
  1.8 4.1 %collective-permute-start.3 = (bf16[32,1024]{1,0:T(8,128)(2,1)S(1)}, bf16[32,1024]{1,0:T(8,128)(2,1)S(1)}, u32[]{:S(2)}, u32[]{:S(2)}) collective-permute-start(bf16[32,1024]{1,0:T(8,128)(2,1)S(1)} %get-tuple-element.11.refs_0_), channel_id=1, source_target_pairs={{0,2},{1,3},{2,0},{3,1},{4,6},{5,7},{6,4},{7,5},{8,10},{9,11},{10,... | collective-permute-start | bytes 196616 | tf_op jit(solution)/shard_map/ppermute | solution.py:18
  5.9 1.5 %collective-permute-start = (bf16[256,256]{1,0:T(8,128)(2,1)S(1)}, bf16[256,256]{1,0:T(8,128)(2,1)S(1)}, u32[]{:S(2)}, u32[]{:S(2)}) collective-permute-start(bf16[256,256]{1,0:T(8,128)(2,1)S(1)} %get-tuple-element.13), channel_id=1, source_target_pairs={{0,8},{4,12},{8,0},{12,4},{1,9},{5,13},{9,1},{13,5},{2,10},{6,14},... | collective-permute-start | bytes 393224 | tf_op jit(solution)/shard_map/ppermute | solution.py:18
  7.4 0.0 collective-permute-start.1
  7.4 0.6 %collective-permute-start.2 = (bf16[256,256]{1,0:T(8,128)(2,1)S(1)}, bf16[256,256]{1,0:T(8,128)(2,1)S(1)}, u32[]{:S(2)}, u32[]{:S(2)}) collective-permute-start(bf16[256,256]{1,0:T(8,128)(2,1)S(1)} %get-tuple-element.15), channel_id=1, source_target_pairs={{0,4},{4,0},{8,12},{12,8},{1,5},{5,1},{9,13},{13,9},{2,6},{6,2},{1... | collective-permute-start | bytes 393224 | tf_op jit(solution)/shard_map/ppermute | solution.py:18
  8.1 1.6 %collective-permute-start.4 = (bf16[32,1024]{1,0:T(8,128)(2,1)S(1)}, bf16[32,1024]{1,0:T(8,128)(2,1)S(1)}, u32[]{:S(2)}, u32[]{:S(2)}) collective-permute-start(bf16[32,1024]{1,0:T(8,128)(2,1)S(1)} %get-tuple-element.11.refs_0_), channel_id=1, source_target_pairs={{0,1},{1,0},{2,3},{3,2},{4,5},{5,4},{6,7},{7,6},{8,9},{9,8},{10,11... | collective-permute-start | bytes 196616 | tf_op jit(solution)/shard_map/ppermute | solution.py:18
  9.6 0.0 collective-permute-done.3.refs_5_
  9.6 0.5 %collective-permute-start.5 = (bf16[32,1024]{1,0:T(8,128)(2,1)S(1)}, bf16[32,1024]{1,0:T(8,128)(2,1)S(1)}, u32[]{:S(2)}, u32[]{:S(2)}) collective-permute-start(bf16[32,1024]{1,0:T(8,128)(2,1)S(1)} %collective-permute-done.3.refs_5_), channel_id=1, source_target_pairs={{0,1},{1,0},{2,3},{3,2},{4,5},{5,4},{6,7},{7,6},{8,9},{9,8},{10,11... | collective-permute-start | bytes 196616 | tf_op jit(solution)/shard_map/ppermute | solution.py:18
  10.1 2.6 %collective-permute-done.4.refs_6_ = bf16[32,1024]{1,0:T(8,128)(2,1)S(1)} collective-permute-done((bf16[32,1024]{1,0:T(8,128)(2,1)S(1)}, bf16[32,1024]{1,0:T(8,128)(2,1)S(1)}, u32[]{:S(2)}, u32[]{:S(2)}) %collective-permute-start.4) | collective-permute-done | bytes 65568 | tf_op jit(solution)/shard_map/ppermute | solution.py:18
  12.7 1.2 %collective-permute-done.5.refs_7_ = bf16[32,1024]{1,0:T(8,128)(2,1)S(1)} collective-permute-done((bf16[32,1024]{1,0:T(8,128)(2,1)S(1)}, bf16[32,1024]{1,0:T(8,128)(2,1)S(1)}, u32[]{:S(2)}, u32[]{:S(2)}) %collective-permute-start.5) | collective-permute-done | bytes 65568 | tf_op jit(solution)/shard_map/ppermute | solution.py:18
  13.9 0.0 collective-permute-done.refs_2_
  13.9 0.0 collective-permute-done.1.refs_3_
  13.9 0.0 collective-permute-done.2.refs_4_
  13.9 0.6 %solve.1 = (f32[128,256]{1,0:T(8,128)S(1)}, s16[144,128]{1,0:T(8,128)(2,1)S(1)}) custom-call(bf16[32,1024]{1,0:T(8,128)(2,1)S(1)} %get-tuple-element.11.refs_0_, bf16[256,256]{1,0:T(8,128)(2,1)S(1)} %get-tuple-element.12.refs_1_, bf16[256,256]{1,0:T(8,128)(2,1)S(1)} %collective-permute-done.refs_2_, bf16[256,256]{1,0:T(8,128)(2,1)S(1)} %collective-permute-done.1.refs_3_, ...), custom_call_target="tpu_custom_call" | custom-call | tf_op jit(solution)/shard_map/solve/pallas_call | solution.py:291
  14.5 1.2 %collective-permute-start.8 = (s16[144,128]{1,0:T(8,128)(2,1)S(1)}, s16[144,128]{1,0:T(8,128)(2,1)S(1)}, u32[]{:S(2)}, u32[]{:S(2)}) collective-permute-start(s16[144,128]{1,0:T(8,128)(2,1)S(1)} %get-tuple-element.17.own), channel_id=1, source_target_pairs={{0,1},{1,3},{2,0},{3,2},{4,5},{5,7},{6,4},{7,6},{8,9},{9,11},{10,8... | collective-permute-start | bytes 110600 | tf_op jit(solution)/shard_map/ppermute | solution.py:351
  15.7 2.4 %collective-permute-start.7 = (s16[144,128]{1,0:T(8,128)(2,1)S(1)}, s16[144,128]{1,0:T(8,128)(2,1)S(1)}, u32[]{:S(2)}, u32[]{:S(2)}) collective-permute-start(s16[144,128]{1,0:T(8,128)(2,1)S(1)} %get-tuple-element.17.own), channel_id=1, source_target_pairs={{0,3},{1,2},{2,1},{3,0},{4,7},{5,6},{6,5},{7,4},{8,11},{9,10},{10,... | collective-permute-start | bytes 110600 | tf_op jit(solution)/shard_map/ppermute | solution.py:351
  18.1 1.9 %collective-permute-start.6 = (s16[144,128]{1,0:T(8,128)(2,1)S(1)}, s16[144,128]{1,0:T(8,128)(2,1)S(1)}, u32[]{:S(2)}, u32[]{:S(2)}) collective-permute-start(s16[144,128]{1,0:T(8,128)(2,1)S(1)} %get-tuple-element.17.own), channel_id=1, source_target_pairs={{0,2},{1,0},{2,3},{3,1},{4,6},{5,4},{6,7},{7,5},{8,10},{9,8},{10,1... | collective-permute-start | bytes 110600 | tf_op jit(solution)/shard_map/ppermute | solution.py:351
  20.0 0.1 tile.4
  20.1 0.0 copy-start
  20.1 0.7 %broadcast_multiply_fusion = f32[128,512]{1,0:T(8,128)} fusion(f32[128,512]{1,0:T(8,128)S(1)} %bitcast.4, f32[512]{0:T(512)S(1)} %bitcast.3), kind=kLoop, calls=%fused_computation | loop fusion | flops 65536 | bytes 526336 | tf_op jit(solution)/shard_map/mul | solution.py:348
  20.9 0.0 collective-permute-done.8.ring
  20.9 0.6 %collective-permute-done.7.across = s16[144,128]{1,0:T(8,128)(2,1)S(1)} collective-permute-done((s16[144,128]{1,0:T(8,128)(2,1)S(1)}, s16[144,128]{1,0:T(8,128)(2,1)S(1)}, u32[]{:S(2)}, u32[]{:S(2)}) %collective-permute-start.7) | collective-permute-done | bytes 36896 | tf_op jit(solution)/shard_map/ppermute | solution.py:351
  21.5 0.6 %collective-permute-done.6.back = s16[144,128]{1,0:T(8,128)(2,1)S(1)} collective-permute-done((s16[144,128]{1,0:T(8,128)(2,1)S(1)}, s16[144,128]{1,0:T(8,128)(2,1)S(1)}, u32[]{:S(2)}, u32[]{:S(2)}) %collective-permute-start.6) | collective-permute-done | bytes 36896 | tf_op jit(solution)/shard_map/ppermute | solution.py:351
  22.0 0.0 copy-done
  22.0 0.7 %finish.1 = f32[128,128]{1,0:T(8,128)} custom-call(f32[128,128]{1,0:T(8,128)S(1)} %copy-done, s16[144,128]{1,0:T(8,128)(2,1)S(1)} %get-tuple-element.17.own, s16[144,128]{1,0:T(8,128)(2,1)S(1)} %collective-permute-done.6.back, s16[144,128]{1,0:T(8,128)(2,1)S(1)} %collective-permute-done.7.across, s16[144,128]{1,0:T(8,128)(2,1)S(1)} %collective-permute-done.8.ring), custom_call_target="tpu_custom_call" | custom-call | tf_op jit(solution)/shard_map/finish/pallas_call | solution.py:311
  (1 shorter events, 0.0 us)
Async XLA Ops:
  1.8 7.8 %collective-permute-start.3 = (bf16[32,1024]{1,0:T(8,128)(2,1)S(1)}, bf16[32,1024]{1,0:T(8,128)(2,1)S(1)}, u32[]{:S(2)}, u32[]{:S(2)}) collective-permute-start(bf16[32,1024]{1,0:T(8,128)(2,1)S(1)} %get-tuple-element.11.refs_0_), channel_id=1, source_target_pairs={{0,2},{1,3},{2,0},{3,1},{4,6},{5,7},{6,4},{7,5},{8,10},{9,11},{10,... | collective-permute-start | bytes 196616 | tf_op jit(solution)/shard_map/ppermute | solution.py:18
  5.9 8.0 %collective-permute-start = (bf16[256,256]{1,0:T(8,128)(2,1)S(1)}, bf16[256,256]{1,0:T(8,128)(2,1)S(1)}, u32[]{:S(2)}, u32[]{:S(2)}) collective-permute-start(bf16[256,256]{1,0:T(8,128)(2,1)S(1)} %get-tuple-element.13), channel_id=1, source_target_pairs={{0,8},{4,12},{8,0},{12,4},{1,9},{5,13},{9,1},{13,5},{2,10},{6,14},... | collective-permute-start | bytes 393224 | tf_op jit(solution)/shard_map/ppermute | solution.py:18
  7.4 6.5 %collective-permute-start.1 = (bf16[256,256]{1,0:T(8,128)(2,1)S(1)}, bf16[256,256]{1,0:T(8,128)(2,1)S(1)}, u32[]{:S(2)}, u32[]{:S(2)}) collective-permute-start(bf16[256,256]{1,0:T(8,128)(2,1)S(1)} %get-tuple-element.14), channel_id=1, source_target_pairs={{0,12},{4,8},{8,4},{12,0},{1,13},{5,9},{9,5},{13,1},{2,14},{6,10},... | collective-permute-start | bytes 393224 | tf_op jit(solution)/shard_map/ppermute | solution.py:18
  7.4 6.5 %collective-permute-start.2 = (bf16[256,256]{1,0:T(8,128)(2,1)S(1)}, bf16[256,256]{1,0:T(8,128)(2,1)S(1)}, u32[]{:S(2)}, u32[]{:S(2)}) collective-permute-start(bf16[256,256]{1,0:T(8,128)(2,1)S(1)} %get-tuple-element.15), channel_id=1, source_target_pairs={{0,4},{4,0},{8,12},{12,8},{1,5},{5,1},{9,13},{13,9},{2,6},{6,2},{1... | collective-permute-start | bytes 393224 | tf_op jit(solution)/shard_map/ppermute | solution.py:18
  8.1 4.6 %collective-permute-start.4 = (bf16[32,1024]{1,0:T(8,128)(2,1)S(1)}, bf16[32,1024]{1,0:T(8,128)(2,1)S(1)}, u32[]{:S(2)}, u32[]{:S(2)}) collective-permute-start(bf16[32,1024]{1,0:T(8,128)(2,1)S(1)} %get-tuple-element.11.refs_0_), channel_id=1, source_target_pairs={{0,1},{1,0},{2,3},{3,2},{4,5},{5,4},{6,7},{7,6},{8,9},{9,8},{10,11... | collective-permute-start | bytes 196616 | tf_op jit(solution)/shard_map/ppermute | solution.py:18
  9.6 4.3 %collective-permute-start.5 = (bf16[32,1024]{1,0:T(8,128)(2,1)S(1)}, bf16[32,1024]{1,0:T(8,128)(2,1)S(1)}, u32[]{:S(2)}, u32[]{:S(2)}) collective-permute-start(bf16[32,1024]{1,0:T(8,128)(2,1)S(1)} %collective-permute-done.3.refs_5_), channel_id=1, source_target_pairs={{0,1},{1,0},{2,3},{3,2},{4,5},{5,4},{6,7},{7,6},{8,9},{9,8},{10,11... | collective-permute-start | bytes 196616 | tf_op jit(solution)/shard_map/ppermute | solution.py:18
  14.5 6.4 %collective-permute-start.8 = (s16[144,128]{1,0:T(8,128)(2,1)S(1)}, s16[144,128]{1,0:T(8,128)(2,1)S(1)}, u32[]{:S(2)}, u32[]{:S(2)}) collective-permute-start(s16[144,128]{1,0:T(8,128)(2,1)S(1)} %get-tuple-element.17.own), channel_id=1, source_target_pairs={{0,1},{1,3},{2,0},{3,2},{4,5},{5,7},{6,4},{7,6},{8,9},{9,11},{10,8... | collective-permute-start | bytes 110600 | tf_op jit(solution)/shard_map/ppermute | solution.py:351
  15.7 5.8 %collective-permute-start.7 = (s16[144,128]{1,0:T(8,128)(2,1)S(1)}, s16[144,128]{1,0:T(8,128)(2,1)S(1)}, u32[]{:S(2)}, u32[]{:S(2)}) collective-permute-start(s16[144,128]{1,0:T(8,128)(2,1)S(1)} %get-tuple-element.17.own), channel_id=1, source_target_pairs={{0,3},{1,2},{2,1},{3,0},{4,7},{5,6},{6,5},{7,4},{8,11},{9,10},{10,... | collective-permute-start | bytes 110600 | tf_op jit(solution)/shard_map/ppermute | solution.py:351
  18.1 4.0 %collective-permute-start.6 = (s16[144,128]{1,0:T(8,128)(2,1)S(1)}, s16[144,128]{1,0:T(8,128)(2,1)S(1)}, u32[]{:S(2)}, u32[]{:S(2)}) collective-permute-start(s16[144,128]{1,0:T(8,128)(2,1)S(1)} %get-tuple-element.17.own), channel_id=1, source_target_pairs={{0,2},{1,0},{2,3},{3,1},{4,6},{5,4},{6,7},{7,5},{8,10},{9,8},{10,1... | collective-permute-start | bytes 110600 | tf_op jit(solution)/shard_map/ppermute | solution.py:351
  20.1 1.9 %copy-start = (f32[128,128]{1,0:T(8,128)S(1)}, f32[128,128]{1,0:T(8,128)}, u32[]{:S(2)}) copy-start(f32[128,128]{1,0:T(8,128)} %diag_inverse.1) | copy-start | bytes 196612

commit v6 on v5

--- a/solution.py
+++ b/solution.py
@@ -248,21 +248,37 @@
     return coded[:count, :].astype(jnp.int32).astype(jnp.float32) * jnp.exp2(exponent - 14.0)
 
 
-def solve_kernel(origins, own_factor, own_green, *refs):
-    given, (solved, coded, factor) = refs[:-3], refs[-3:]
+def held_kernel(value, out):
+    out[...] = value[...]
+
+
+def held(value):
+    return pl.pallas_call(
+        held_kernel,
+        out_shape=pltpu.VMEM(value.shape, value.dtype),
+        in_specs=[pl.BlockSpec(memory_space=pltpu.VMEM)],
+        out_specs=pl.BlockSpec(memory_space=pltpu.VMEM),
+        compiler_params=pltpu.CompilerParams(vmem_limit_bytes=VMEM_LIMIT),
+        cost_estimate=pl.CostEstimate(flops=10**9, bytes_accessed=1 << 20, transcendentals=0),
+        name="held",
+    )(value)
+
+
+def gather_kernel(steps, own_factor, *refs):
+    parts, factor = refs[: len(steps)], refs[-1]
+    col_index = lax.axis_index("col")
+    local_rows = own_factor.shape[0]
+    for step, part in zip((0, *steps), (own_factor, *parts)):
+        factor[block(col_index ^ step, local_rows), :] = part[...]
+
+
+def solve_kernel(steps, factor, *refs):
+    greens, (solved, coded) = refs[:-2], refs[-2:]
     row_index = lax.axis_index("row")
     col_index = lax.axis_index("col")
-    local_rows = own_factor.shape[0]
-    rows, width = own_green.shape
-    greens = [(0, own_green)]
-    factor[block(col_index, local_rows), :] = own_factor[...]
-    for (axis, step), part in zip(origins, given):
-        if axis == "col":
-            factor[block(col_index ^ step, local_rows), :] = part[...]
-        else:
-            greens.append((step, part))
+    rows, width = greens[0].shape
     total = jnp.zeros(solved.shape, jnp.float32)
-    for step, green in sorted(greens, key=lambda one: one[0]):
+    for step, green in zip(steps, greens):
         total = total + lax.dot_general(
             factor[:, block(row_index ^ step, width)],
             green[...],
@@ -285,21 +301,35 @@
     code_of(value, coded)
 
 
-def solve(own_factor, own_green, origins, given, col_count):
+def solve(own_factor, own_green, received, col_count):
     local_rows, columns = own_factor.shape
     count = col_count * local_rows
+    params = pltpu.CompilerParams(vmem_limit_bytes=VMEM_LIMIT)
+    vmem = pl.BlockSpec(memory_space=pltpu.VMEM)
+    factors = [(step, part) for (axis, step), part in received.items() if axis == "col"]
+    greens = [(step, part) for (axis, step), part in received.items() if axis == "row"]
+    ahead = [part for step, part in greens if step != 1]
+    factor = pl.pallas_call(
+        lambda *refs: gather_kernel([step for step, _ in factors], *refs),
+        out_shape=pltpu.VMEM((count, columns), jnp.bfloat16),
+        in_specs=[vmem] * (1 + len(factors) + len(ahead)),
+        out_specs=vmem,
+        compiler_params=params,
+        cost_estimate=pl.CostEstimate(flops=10**10, bytes_accessed=1 << 20, transcendentals=0),
+        name="gather",
+    )(own_factor, *[part for _, part in factors], *ahead)
+    greens = [(0, own_green)] + sorted(greens, key=lambda one: one[0])
     return pl.pallas_call(
-        lambda *refs: solve_kernel(origins, *refs),
+        lambda *refs: solve_kernel([step for step, _ in greens], *refs),
         out_shape=[
             pltpu.VMEM((count, own_green.shape[0]), jnp.float32),
             pltpu.VMEM((count + EXPONENT_ROWS, count), jnp.int16),
         ],
-        in_specs=[pl.BlockSpec(memory_space=pltpu.VMEM)] * (2 + len(given)),
-        out_specs=[pl.BlockSpec(memory_space=pltpu.VMEM)] * 2,
-        scratch_shapes=[pltpu.VMEM((count, columns), jnp.bfloat16)],
-        compiler_params=pltpu.CompilerParams(vmem_limit_bytes=VMEM_LIMIT),
+        in_specs=[vmem] * (1 + len(greens)),
+        out_specs=[vmem] * 2,
+        compiler_params=params,
         name="solve",
-    )(own_factor, own_green, *given)
+    )(factor, *[part for _, part in greens])
 
 
 def finish_kernel(diag_inverse, own, back, across, ring, out):
@@ -331,18 +361,15 @@
     size = factor_cols.shape[1] // blocks
 
     own_factor, mask, *greens = pack(green_top, factor_cols, fill_blocks)
-    second = partner(own_factor, "col", 2)
-    received = {
+    transfers = {
         ("row", 2): partner(greens[2], "row", 2),
         ("row", 3): partner(greens[3], "row", 3),
         ("row", 1): partner(greens[1], "row", 1),
-        ("col", 2): second,
+        ("col", 2): held(partner(own_factor, "col", 2)),
         ("col", 1): partner(own_factor, "col", 1),
-        ("col", 3): partner(second, "col", 1),
+        ("col", 3): partner(own_factor, "col", 3),
     }
-    solved, code = solve(
-        own_factor, greens[0], tuple(received), tuple(received.values()), col_count
-    )
+    solved, code = solve(own_factor, greens[0], transfers, col_count)
     green_cols = None
     for p in range(half):
         term = mask[p : p + 1] * jnp.tile(solved[:, p * size : (p + 1) * size], (1, group))

time: 22.8 us -> 22.8 us (level)
  starting transfers between devices: 13.8 us -> 11.4 us
  waiting for transfers between devices: 4.93 us -> 7.23 us
    ppermute x6, waiting for transfers between devices: 3.78 us -> 5.53 us  [partner(): return lax.ppermute(value, axis, [(a, a ^ step) for a in range(size)])]
    ppermute x3, starting transfers between devices: 5.49 us -> 4.26 us  [per_device(): lax.ppermute(code, 'col', list(enumerate(moves)))]
    ppermute x6, starting transfers between devices: 8.31 us -> 7.18 us  [partner(): return lax.ppermute(value, axis, [(a, a ^ step) for a in range(size)])]
    ppermute x3, waiting for transfers between devices: 1.15 us -> 1.7 us  [per_device(): lax.ppermute(code, 'col', list(enumerate(moves)))]
    pallas_call x1 -> x3, Pallas kernels: 0.58 us -> 0.62 us  [the longest x1 0.59 us: solve(): pl.pallas_call(lambda *refs: solve_kernel([step for step, _ in greens], *...]
  transfers between devices with their start and end apart: 9 -> 9, of which waited for: 4 -> 5; matrix products, arithmetic and copies ran while one was open for 4% -> 4% of each run, Pallas kernels for 0% -> 0%
where the time goes in v6:
time: 22.8 us; the launch traced here: 22.7 us
  starting transfers between devices  11.4 us (50%)
  waiting for transfers between devices  7.23 us (32%)
  Pallas kernels  2.48 us (11%)
  other arithmetic  0.73 us (3%)
  between operations  0.69 us (3%)
    ppermute x6, starting transfers between devices, partner(): return lax.ppermute(value, axis, [(a, a ^ step) for a in range(size)])  7.18 us
    ppermute x6, waiting for transfers between devices, partner(): return lax.ppermute(value, axis, [(a, a ^ step) for a in range(size)])  5.53 us
    ppermute x3, starting transfers between devices, per_device(): lax.ppermute(code, 'col', list(enumerate(moves)))  4.26 us
    ppermute x3, waiting for transfers between devices, per_device(): lax.ppermute(code, 'col', list(enumerate(moves)))  1.7 us
    pallas_call x1, Pallas kernels, pack(): pl.pallas_call(lambda *refs: pack_kernel(row_count, col_count, *refs), ou...  1.18 us
    mul x1, other arithmetic, per_device(): mask[p:p + 1] * jnp.tile(solved[:, p * size:(p + 1) * size], (1, group))  0.73 us
    pallas_call x1, Pallas kernels, finish(): pl.pallas_call(finish_kernel, out_shape=jax.ShapeDtypeStruct(diag_inverse...  0.67 us
    pallas_call x1, Pallas kernels, solve(): pl.pallas_call(lambda *refs: solve_kernel([step for step, _ in greens], *...  0.59 us
  transfers between devices with their start and end apart: 9, of which 5 were waited for; matrix products, arithmetic and copies ran while one was open for 4% of the time, Pallas kernels for 0%

profile of v6, /device:TPU:0, one launch (start us, length us, event | category | flops | bytes accessed | tf_op | source)
XLA Modules:
  0.0 22.7 jit_solution(6967980875376078190)
XLA Ops:
  0.6 1.2 %pack.1 = (bf16[32,1024]{1,0:T(8,128)(2,1)S(1)}, f32[1,512]{1,0:T(1,128)S(1)}, bf16[256,256]{1,0:T(8,128)(2,1)S(1)}, bf16[256,256]{1,0:T(8,128)(2,1)S(1)}, bf16[...) custom-call(s32[4,8]{1,0:T(4,128)} %refs_0_.1, bf16[512,512]{1,0:T(8,128)(2,1)} %refs_1_.1, bf16[32,2048]{1,0:T(8,128)(2,1)} %refs_2_.1), custom_call_target="tpu_custom_call" | custom-call | tf_op jit(solution)/shard_map/pack/pallas_call | solution.py:219
  1.8 4.1 %collective-permute-start = (bf16[32,1024]{1,0:T(8,128)(2,1)S(1)}, bf16[32,1024]{1,0:T(8,128)(2,1)S(1)}, u32[]{:S(2)}, u32[]{:S(2)}) collective-permute-start(bf16[32,1024]{1,0:T(8,128)(2,1)S(1)} %get-tuple-element.11.refs_0_), channel_id=1, source_target_pairs={{0,2},{1,3},{2,0},{3,1},{4,6},{5,7},{6,4},{7,5},{8,10},{9,11},{10,... | collective-permute-start | bytes 196616 | tf_op jit(solution)/shard_map/ppermute | solution.py:18
  5.9 1.5 %collective-permute-start.3 = (bf16[256,256]{1,0:T(8,128)(2,1)S(1)}, bf16[256,256]{1,0:T(8,128)(2,1)S(1)}, u32[]{:S(2)}, u32[]{:S(2)}) collective-permute-start(bf16[256,256]{1,0:T(8,128)(2,1)S(1)} %get-tuple-element.12), channel_id=1, source_target_pairs={{0,8},{4,12},{8,0},{12,4},{1,9},{5,13},{9,1},{13,5},{2,10},{6,14},... | collective-permute-start | bytes 393224 | tf_op jit(solution)/shard_map/ppermute | solution.py:18
  7.4 0.0 collective-permute-start.4
  7.4 1.3 %collective-permute-start.2 = (bf16[32,1024]{1,0:T(8,128)(2,1)S(1)}, bf16[32,1024]{1,0:T(8,128)(2,1)S(1)}, u32[]{:S(2)}, u32[]{:S(2)}) collective-permute-start(bf16[32,1024]{1,0:T(8,128)(2,1)S(1)} %get-tuple-element.11.refs_0_), channel_id=1, source_target_pairs={{0,3},{1,2},{2,1},{3,0},{4,7},{5,6},{6,5},{7,4},{8,11},{9,10},{10,... | collective-permute-start | bytes 196616 | tf_op jit(solution)/shard_map/ppermute | solution.py:18
  8.8 0.2 %collective-permute-start.1 = (bf16[32,1024]{1,0:T(8,128)(2,1)S(1)}, bf16[32,1024]{1,0:T(8,128)(2,1)S(1)}, u32[]{:S(2)}, u32[]{:S(2)}) collective-permute-start(bf16[32,1024]{1,0:T(8,128)(2,1)S(1)} %get-tuple-element.11.refs_0_), channel_id=1, source_target_pairs={{0,1},{1,0},{2,3},{3,2},{4,5},{5,4},{6,7},{7,6},{8,9},{9,8},{10,11... | collective-permute-start | bytes 196616 | tf_op jit(solution)/shard_map/ppermute | solution.py:18
  9.0 0.6 %collective-permute-done.value = bf16[32,1024]{1,0:T(8,128)(2,1)S(1)} collective-permute-done((bf16[32,1024]{1,0:T(8,128)(2,1)S(1)}, bf16[32,1024]{1,0:T(8,128)(2,1)S(1)}, u32[]{:S(2)}, u32[]{:S(2)}) %collective-permute-start) | collective-permute-done | bytes 65568 | tf_op jit(solution)/shard_map/ppermute | solution.py:18
  9.6 0.0 collective-permute-start.5
  9.6 4.6 %collective-permute-done.2.refs_3_ = bf16[32,1024]{1,0:T(8,128)(2,1)S(1)} collective-permute-done((bf16[32,1024]{1,0:T(8,128)(2,1)S(1)}, bf16[32,1024]{1,0:T(8,128)(2,1)S(1)}, u32[]{:S(2)}, u32[]{:S(2)}) %collective-permute-start.2) | collective-permute-done | bytes 65568 | tf_op jit(solution)/shard_map/ppermute | solution.py:18
  14.2 0.3 %collective-permute-done.1.refs_2_ = bf16[32,1024]{1,0:T(8,128)(2,1)S(1)} collective-permute-done((bf16[32,1024]{1,0:T(8,128)(2,1)S(1)}, bf16[32,1024]{1,0:T(8,128)(2,1)S(1)}, u32[]{:S(2)}, u32[]{:S(2)}) %collective-permute-start.1) | collective-permute-done | bytes 65568 | tf_op jit(solution)/shard_map/ppermute | solution.py:18
  14.5 0.0 collective-permute-done.3.refs_4_.refs_3_
  14.5 0.0 collective-permute-done.4.refs_5_.refs_4_
  14.6 0.0 collective-permute-done.5.refs_2_
  14.6 0.6 %solve.1 = (f32[128,256]{1,0:T(8,128)S(1)}, s16[144,128]{1,0:T(8,128)(2,1)S(1)}) custom-call(bf16[128,1024]{1,0:T(8,128)(2,1)S(1)} %gather.1.refs_0_, bf16[256,256]{1,0:T(8,128)(2,1)S(1)} %get-tuple-element.14.refs_1_, bf16[256,256]{1,0:T(8,128)(2,1)S(1)} %collective-permute-done.5.refs_2_, bf16[256,256]{1,0:T(8,128)(2,1)S(1)} %collective-permute-done.3.refs_4_.refs_3_, ...), custom_call_target="tpu_custom_call" | custom-call | tf_op jit(solution)/shard_map/solve/pallas_call | solution.py:322
  15.2 0.6 %collective-permute-start.8 = (s16[144,128]{1,0:T(8,128)(2,1)S(1)}, s16[144,128]{1,0:T(8,128)(2,1)S(1)}, u32[]{:S(2)}, u32[]{:S(2)}) collective-permute-start(s16[144,128]{1,0:T(8,128)(2,1)S(1)} %get-tuple-element.17.own), channel_id=1, source_target_pairs={{0,1},{1,3},{2,0},{3,2},{4,5},{5,7},{6,4},{7,6},{8,9},{9,11},{10,8... | collective-permute-start | bytes 110600 | tf_op jit(solution)/shard_map/ppermute | solution.py:378
  15.8 2.3 %collective-permute-start.7 = (s16[144,128]{1,0:T(8,128)(2,1)S(1)}, s16[144,128]{1,0:T(8,128)(2,1)S(1)}, u32[]{:S(2)}, u32[]{:S(2)}) collective-permute-start(s16[144,128]{1,0:T(8,128)(2,1)S(1)} %get-tuple-element.17.own), channel_id=1, source_target_pairs={{0,3},{1,2},{2,1},{3,0},{4,7},{5,6},{6,5},{7,4},{8,11},{9,10},{10,... | collective-permute-start | bytes 110600 | tf_op jit(solution)/shard_map/ppermute | solution.py:378
  18.0 1.4 %collective-permute-start.6 = (s16[144,128]{1,0:T(8,128)(2,1)S(1)}, s16[144,128]{1,0:T(8,128)(2,1)S(1)}, u32[]{:S(2)}, u32[]{:S(2)}) collective-permute-start(s16[144,128]{1,0:T(8,128)(2,1)S(1)} %get-tuple-element.17.own), channel_id=1, source_target_pairs={{0,2},{1,0},{2,3},{3,1},{4,6},{5,4},{6,7},{7,5},{8,10},{9,8},{10,1... | collective-permute-start | bytes 110600 | tf_op jit(solution)/shard_map/ppermute | solution.py:378
  19.4 0.1 tile.4
  19.6 0.0 copy-start
  19.6 0.7 %broadcast_multiply_fusion = f32[128,512]{1,0:T(8,128)} fusion(f32[128,512]{1,0:T(8,128)S(1)} %bitcast.4, f32[512]{0:T(512)S(1)} %bitcast.3), kind=kLoop, calls=%fused_computation | loop fusion | flops 65536 | bytes 526336 | tf_op jit(solution)/shard_map/mul | solution.py:375
  20.3 1.3 %collective-permute-done.8.ring = s16[144,128]{1,0:T(8,128)(2,1)S(1)} collective-permute-done((s16[144,128]{1,0:T(8,128)(2,1)S(1)}, s16[144,128]{1,0:T(8,128)(2,1)S(1)}, u32[]{:S(2)}, u32[]{:S(2)}) %collective-permute-start.8) | collective-permute-done | bytes 36896 | tf_op jit(solution)/shard_map/ppermute | solution.py:378
  21.6 0.0 collective-permute-done.7.across
  21.6 0.4 %collective-permute-done.6.back = s16[144,128]{1,0:T(8,128)(2,1)S(1)} collective-permute-done((s16[144,128]{1,0:T(8,128)(2,1)S(1)}, s16[144,128]{1,0:T(8,128)(2,1)S(1)}, u32[]{:S(2)}, u32[]{:S(2)}) %collective-permute-start.6) | collective-permute-done | bytes 36896 | tf_op jit(solution)/shard_map/ppermute | solution.py:378
  22.0 0.0 copy-done
  22.0 0.7 %finish.1 = f32[128,128]{1,0:T(8,128)} custom-call(f32[128,128]{1,0:T(8,128)S(1)} %copy-done, s16[144,128]{1,0:T(8,128)(2,1)S(1)} %get-tuple-element.17.own, s16[144,128]{1,0:T(8,128)(2,1)S(1)} %collective-permute-done.6.back, s16[144,128]{1,0:T(8,128)(2,1)S(1)} %collective-permute-done.7.across, s16[144,128]{1,0:T(8,128)(2,1)S(1)} %collective-permute-done.8.ring), custom_call_target="tpu_custom_call" | custom-call | tf_op jit(solution)/shard_map/finish/pallas_call | solution.py:341
  (3 shorter events, 0.0 us)
Async XLA Ops:
  1.8 7.8 %collective-permute-start = (bf16[32,1024]{1,0:T(8,128)(2,1)S(1)}, bf16[32,1024]{1,0:T(8,128)(2,1)S(1)}, u32[]{:S(2)}, u32[]{:S(2)}) collective-permute-start(bf16[32,1024]{1,0:T(8,128)(2,1)S(1)} %get-tuple-element.11.refs_0_), channel_id=1, source_target_pairs={{0,2},{1,3},{2,0},{3,1},{4,6},{5,7},{6,4},{7,5},{8,10},{9,11},{10,... | collective-permute-start | bytes 196616 | tf_op jit(solution)/shard_map/ppermute | solution.py:18
  5.9 8.6 %collective-permute-start.3 = (bf16[256,256]{1,0:T(8,128)(2,1)S(1)}, bf16[256,256]{1,0:T(8,128)(2,1)S(1)}, u32[]{:S(2)}, u32[]{:S(2)}) collective-permute-start(bf16[256,256]{1,0:T(8,128)(2,1)S(1)} %get-tuple-element.12), channel_id=1, source_target_pairs={{0,8},{4,12},{8,0},{12,4},{1,9},{5,13},{9,1},{13,5},{2,10},{6,14},... | collective-permute-start | bytes 393224 | tf_op jit(solution)/shard_map/ppermute | solution.py:18
  7.4 7.1 %collective-permute-start.4 = (bf16[256,256]{1,0:T(8,128)(2,1)S(1)}, bf16[256,256]{1,0:T(8,128)(2,1)S(1)}, u32[]{:S(2)}, u32[]{:S(2)}) collective-permute-start(bf16[256,256]{1,0:T(8,128)(2,1)S(1)} %get-tuple-element.13), channel_id=1, source_target_pairs={{0,12},{4,8},{8,4},{12,0},{1,13},{5,9},{9,5},{13,1},{2,14},{6,10},... | collective-permute-start | bytes 393224 | tf_op jit(solution)/shard_map/ppermute | solution.py:18
  7.4 6.8 %collective-permute-start.2 = (bf16[32,1024]{1,0:T(8,128)(2,1)S(1)}, bf16[32,1024]{1,0:T(8,128)(2,1)S(1)}, u32[]{:S(2)}, u32[]{:S(2)}) collective-permute-start(bf16[32,1024]{1,0:T(8,128)(2,1)S(1)} %get-tuple-element.11.refs_0_), channel_id=1, source_target_pairs={{0,3},{1,2},{2,1},{3,0},{4,7},{5,6},{6,5},{7,4},{8,11},{9,10},{10,... | collective-permute-start | bytes 196616 | tf_op jit(solution)/shard_map/ppermute | solution.py:18
  8.8 5.8 %collective-permute-start.1 = (bf16[32,1024]{1,0:T(8,128)(2,1)S(1)}, bf16[32,1024]{1,0:T(8,128)(2,1)S(1)}, u32[]{:S(2)}, u32[]{:S(2)}) collective-permute-start(bf16[32,1024]{1,0:T(8,128)(2,1)S(1)} %get-tuple-element.11.refs_0_), channel_id=1, source_target_pairs={{0,1},{1,0},{2,3},{3,2},{4,5},{5,4},{6,7},{7,6},{8,9},{9,8},{10,11... | collective-permute-start | bytes 196616 | tf_op jit(solution)/shard_map/ppermute | solution.py:18
  9.6 5.0 %collective-permute-start.5 = (bf16[256,256]{1,0:T(8,128)(2,1)S(1)}, bf16[256,256]{1,0:T(8,128)(2,1)S(1)}, u32[]{:S(2)}, u32[]{:S(2)}) collective-permute-start(bf16[256,256]{1,0:T(8,128)(2,1)S(1)} %get-tuple-element.15), channel_id=1, source_target_pairs={{0,4},{4,0},{8,12},{12,8},{1,5},{5,1},{9,13},{13,9},{2,6},{6,2},{1... | collective-permute-start | bytes 393224 | tf_op jit(solution)/shard_map/ppermute | solution.py:18
  15.2 6.4 %collective-permute-start.8 = (s16[144,128]{1,0:T(8,128)(2,1)S(1)}, s16[144,128]{1,0:T(8,128)(2,1)S(1)}, u32[]{:S(2)}, u32[]{:S(2)}) collective-permute-start(s16[144,128]{1,0:T(8,128)(2,1)S(1)} %get-tuple-element.17.own), channel_id=1, source_target_pairs={{0,1},{1,3},{2,0},{3,2},{4,5},{5,7},{6,4},{7,6},{8,9},{9,11},{10,8... | collective-permute-start | bytes 110600 | tf_op jit(solution)/shard_map/ppermute | solution.py:378
  15.8 5.8 %collective-permute-start.7 = (s16[144,128]{1,0:T(8,128)(2,1)S(1)}, s16[144,128]{1,0:T(8,128)(2,1)S(1)}, u32[]{:S(2)}, u32[]{:S(2)}) collective-permute-start(s16[144,128]{1,0:T(8,128)(2,1)S(1)} %get-tuple-element.17.own), channel_id=1, source_target_pairs={{0,3},{1,2},{2,1},{3,0},{4,7},{5,6},{6,5},{7,4},{8,11},{9,10},{10,... | collective-permute-start | bytes 110600 | tf_op jit(solution)/shard_map/ppermute | solution.py:378
  18.0 4.0 %collective-permute-start.6 = (s16[144,128]{1,0:T(8,128)(2,1)S(1)}, s16[144,128]{1,0:T(8,128)(2,1)S(1)}, u32[]{:S(2)}, u32[]{:S(2)}) collective-permute-start(s16[144,128]{1,0:T(8,128)(2,1)S(1)} %get-tuple-element.17.own), channel_id=1, source_target_pairs={{0,2},{1,0},{2,3},{3,1},{4,6},{5,4},{6,7},{7,5},{8,10},{9,8},{10,1... | collective-permute-start | bytes 110600 | tf_op jit(solution)/shard_map/ppermute | solution.py:378
  19.6 2.4 %copy-start = (f32[128,128]{1,0:T(8,128)S(1)}, f32[128,128]{1,0:T(8,128)}, u32[]{:S(2)}) copy-start(f32[128,128]{1,0:T(8,128)} %diag_inverse.1) | copy-start | bytes 196612

commit v7 on v5

--- a/solution.py
+++ b/solution.py
@@ -334,8 +334,8 @@
     second = partner(own_factor, "col", 2)
     received = {
         ("row", 2): partner(greens[2], "row", 2),
+        ("row", 1): partner(greens[1], "row", 1),
         ("row", 3): partner(greens[3], "row", 3),
-        ("row", 1): partner(greens[1], "row", 1),
         ("col", 2): second,
         ("col", 1): partner(own_factor, "col", 1),
         ("col", 3): partner(second, "col", 1),

time: 22.8 us -> 22.8 us (level)
  no operation moved by 1% of the time
where the time goes in v7:
time: 22.8 us; the launch traced here: 22.7 us
  starting transfers between devices  13.8 us (61%)
  waiting for transfers between devices  4.93 us (22%)
  Pallas kernels  2.44 us (11%)
  other arithmetic  0.73 us (3%)
  between operations  0.68 us (3%)
    ppermute x6, starting transfers between devices, partner(): return lax.ppermute(value, axis, [(a, a ^ step) for a in range(size)])  8.31 us
    ppermute x3, starting transfers between devices, per_device(): lax.ppermute(code, 'col', list(enumerate(moves)))  5.49 us
    ppermute x6, waiting for transfers between devices, partner(): return lax.ppermute(value, axis, [(a, a ^ step) for a in range(size)])  3.78 us
    pallas_call x1, Pallas kernels, pack(): pl.pallas_call(lambda *refs: pack_kernel(row_count, col_count, *refs), ou...  1.18 us
    ppermute x3, waiting for transfers between devices, per_device(): lax.ppermute(code, 'col', list(enumerate(moves)))  1.15 us
    mul x1, other arithmetic, per_device(): mask[p:p + 1] * jnp.tile(solved[:, p * size:(p + 1) * size], (1, group))  0.73 us
    pallas_call x1, Pallas kernels, finish(): pl.pallas_call(finish_kernel, out_shape=jax.ShapeDtypeStruct(diag_inverse...  0.67 us
    pallas_call x1, Pallas kernels, solve(): pl.pallas_call(lambda *refs: solve_kernel(origins, *refs), out_shape=[plt...  0.58 us
  transfers between devices with their start and end apart: 9, of which 4 were waited for; matrix products, arithmetic and copies ran while one was open for 4% of the time, Pallas kernels for 0%

profile of v7, /device:TPU:0, one launch (start us, length us, event | category | flops | bytes accessed | tf_op | source)
XLA Modules:
  0.0 22.7 jit_solution(17584772727222387261)
XLA Ops:
  0.6 1.2 %pack.1 = (bf16[32,1024]{1,0:T(8,128)(2,1)S(1)}, f32[1,512]{1,0:T(1,128)S(1)}, bf16[256,256]{1,0:T(8,128)(2,1)S(1)}, bf16[256,256]{1,0:T(8,128)(2,1)S(1)}, bf16[...) custom-call(s32[4,8]{1,0:T(4,128)} %refs_0_.1, bf16[512,512]{1,0:T(8,128)(2,1)} %refs_1_.1, bf16[32,2048]{1,0:T(8,128)(2,1)} %refs_2_.1), custom_call_target="tpu_custom_call" | custom-call | tf_op jit(solution)/shard_map/pack/pallas_call | solution.py:219
  1.8 4.1 %collective-permute-start.3 = (bf16[32,1024]{1,0:T(8,128)(2,1)S(1)}, bf16[32,1024]{1,0:T(8,128)(2,1)S(1)}, u32[]{:S(2)}, u32[]{:S(2)}) collective-permute-start(bf16[32,1024]{1,0:T(8,128)(2,1)S(1)} %get-tuple-element.11.refs_0_), channel_id=1, source_target_pairs={{0,2},{1,3},{2,0},{3,1},{4,6},{5,7},{6,4},{7,5},{8,10},{9,11},{10,... | collective-permute-start | bytes 196616 | tf_op jit(solution)/shard_map/ppermute | solution.py:18
  5.9 1.5 %collective-permute-start = (bf16[256,256]{1,0:T(8,128)(2,1)S(1)}, bf16[256,256]{1,0:T(8,128)(2,1)S(1)}, u32[]{:S(2)}, u32[]{:S(2)}) collective-permute-start(bf16[256,256]{1,0:T(8,128)(2,1)S(1)} %get-tuple-element.13), channel_id=1, source_target_pairs={{0,8},{4,12},{8,0},{12,4},{1,9},{5,13},{9,1},{13,5},{2,10},{6,14},... | collective-permute-start | bytes 393224 | tf_op jit(solution)/shard_map/ppermute | solution.py:18
  7.4 0.0 collective-permute-start.1
  7.4 0.6 %collective-permute-start.2 = (bf16[256,256]{1,0:T(8,128)(2,1)S(1)}, bf16[256,256]{1,0:T(8,128)(2,1)S(1)}, u32[]{:S(2)}, u32[]{:S(2)}) collective-permute-start(bf16[256,256]{1,0:T(8,128)(2,1)S(1)} %get-tuple-element.15), channel_id=1, source_target_pairs={{0,12},{4,8},{8,4},{12,0},{1,13},{5,9},{9,5},{13,1},{2,14},{6,10},... | collective-permute-start | bytes 393224 | tf_op jit(solution)/shard_map/ppermute | solution.py:18
  8.1 1.6 %collective-permute-start.4 = (bf16[32,1024]{1,0:T(8,128)(2,1)S(1)}, bf16[32,1024]{1,0:T(8,128)(2,1)S(1)}, u32[]{:S(2)}, u32[]{:S(2)}) collective-permute-start(bf16[32,1024]{1,0:T(8,128)(2,1)S(1)} %get-tuple-element.11.refs_0_), channel_id=1, source_target_pairs={{0,1},{1,0},{2,3},{3,2},{4,5},{5,4},{6,7},{7,6},{8,9},{9,8},{10,11... | collective-permute-start | bytes 196616 | tf_op jit(solution)/shard_map/ppermute | solution.py:18
  9.6 0.0 collective-permute-done.3.refs_5_
  9.6 0.5 %collective-permute-start.5 = (bf16[32,1024]{1,0:T(8,128)(2,1)S(1)}, bf16[32,1024]{1,0:T(8,128)(2,1)S(1)}, u32[]{:S(2)}, u32[]{:S(2)}) collective-permute-start(bf16[32,1024]{1,0:T(8,128)(2,1)S(1)} %collective-permute-done.3.refs_5_), channel_id=1, source_target_pairs={{0,1},{1,0},{2,3},{3,2},{4,5},{5,4},{6,7},{7,6},{8,9},{9,8},{10,11... | collective-permute-start | bytes 196616 | tf_op jit(solution)/shard_map/ppermute | solution.py:18
  10.1 2.6 %collective-permute-done.4.refs_6_ = bf16[32,1024]{1,0:T(8,128)(2,1)S(1)} collective-permute-done((bf16[32,1024]{1,0:T(8,128)(2,1)S(1)}, bf16[32,1024]{1,0:T(8,128)(2,1)S(1)}, u32[]{:S(2)}, u32[]{:S(2)}) %collective-permute-start.4) | collective-permute-done | bytes 65568 | tf_op jit(solution)/shard_map/ppermute | solution.py:18
  12.7 1.2 %collective-permute-done.5.refs_7_ = bf16[32,1024]{1,0:T(8,128)(2,1)S(1)} collective-permute-done((bf16[32,1024]{1,0:T(8,128)(2,1)S(1)}, bf16[32,1024]{1,0:T(8,128)(2,1)S(1)}, u32[]{:S(2)}, u32[]{:S(2)}) %collective-permute-start.5) | collective-permute-done | bytes 65568 | tf_op jit(solution)/shard_map/ppermute | solution.py:18
  13.9 0.0 collective-permute-done.refs_2_
  13.9 0.0 collective-permute-done.1.refs_3_
  13.9 0.0 collective-permute-done.2.refs_4_
  13.9 0.6 %solve.1 = (f32[128,256]{1,0:T(8,128)S(1)}, s16[144,128]{1,0:T(8,128)(2,1)S(1)}) custom-call(bf16[32,1024]{1,0:T(8,128)(2,1)S(1)} %get-tuple-element.11.refs_0_, bf16[256,256]{1,0:T(8,128)(2,1)S(1)} %get-tuple-element.12.refs_1_, bf16[256,256]{1,0:T(8,128)(2,1)S(1)} %collective-permute-done.refs_2_, bf16[256,256]{1,0:T(8,128)(2,1)S(1)} %collective-permute-done.1.refs_3_, ...), custom_call_target="tpu_custom_call" | custom-call | tf_op jit(solution)/shard_map/solve/pallas_call | solution.py:291
  14.5 1.2 %collective-permute-start.8 = (s16[144,128]{1,0:T(8,128)(2,1)S(1)}, s16[144,128]{1,0:T(8,128)(2,1)S(1)}, u32[]{:S(2)}, u32[]{:S(2)}) collective-permute-start(s16[144,128]{1,0:T(8,128)(2,1)S(1)} %get-tuple-element.17.own), channel_id=1, source_target_pairs={{0,1},{1,3},{2,0},{3,2},{4,5},{5,7},{6,4},{7,6},{8,9},{9,11},{10,8... | collective-permute-start | bytes 110600 | tf_op jit(solution)/shard_map/ppermute | solution.py:351
  15.7 2.4 %collective-permute-start.7 = (s16[144,128]{1,0:T(8,128)(2,1)S(1)}, s16[144,128]{1,0:T(8,128)(2,1)S(1)}, u32[]{:S(2)}, u32[]{:S(2)}) collective-permute-start(s16[144,128]{1,0:T(8,128)(2,1)S(1)} %get-tuple-element.17.own), channel_id=1, source_target_pairs={{0,3},{1,2},{2,1},{3,0},{4,7},{5,6},{6,5},{7,4},{8,11},{9,10},{10,... | collective-permute-start | bytes 110600 | tf_op jit(solution)/shard_map/ppermute | solution.py:351
  18.1 1.9 %collective-permute-start.6 = (s16[144,128]{1,0:T(8,128)(2,1)S(1)}, s16[144,128]{1,0:T(8,128)(2,1)S(1)}, u32[]{:S(2)}, u32[]{:S(2)}) collective-permute-start(s16[144,128]{1,0:T(8,128)(2,1)S(1)} %get-tuple-element.17.own), channel_id=1, source_target_pairs={{0,2},{1,0},{2,3},{3,1},{4,6},{5,4},{6,7},{7,5},{8,10},{9,8},{10,1... | collective-permute-start | bytes 110600 | tf_op jit(solution)/shard_map/ppermute | solution.py:351
  20.0 0.1 tile.4
  20.1 0.0 copy-start
  20.1 0.7 %broadcast_multiply_fusion = f32[128,512]{1,0:T(8,128)} fusion(f32[128,512]{1,0:T(8,128)S(1)} %bitcast.4, f32[512]{0:T(512)S(1)} %bitcast.3), kind=kLoop, calls=%fused_computation | loop fusion | flops 65536 | bytes 526336 | tf_op jit(solution)/shard_map/mul | solution.py:348
  20.9 0.0 collective-permute-done.8.ring
  20.9 0.6 %collective-permute-done.7.across = s16[144,128]{1,0:T(8,128)(2,1)S(1)} collective-permute-done((s16[144,128]{1,0:T(8,128)(2,1)S(1)}, s16[144,128]{1,0:T(8,128)(2,1)S(1)}, u32[]{:S(2)}, u32[]{:S(2)}) %collective-permute-start.7) | collective-permute-done | bytes 36896 | tf_op jit(solution)/shard_map/ppermute | solution.py:351
  21.5 0.6 %collective-permute-done.6.back = s16[144,128]{1,0:T(8,128)(2,1)S(1)} collective-permute-done((s16[144,128]{1,0:T(8,128)(2,1)S(1)}, s16[144,128]{1,0:T(8,128)(2,1)S(1)}, u32[]{:S(2)}, u32[]{:S(2)}) %collective-permute-start.6) | collective-permute-done | bytes 36896 | tf_op jit(solution)/shard_map/ppermute | solution.py:351
  22.0 0.0 copy-done
  22.0 0.7 %finish.1 = f32[128,128]{1,0:T(8,128)} custom-call(f32[128,128]{1,0:T(8,128)S(1)} %copy-done, s16[144,128]{1,0:T(8,128)(2,1)S(1)} %get-tuple-element.17.own, s16[144,128]{1,0:T(8,128)(2,1)S(1)} %collective-permute-done.6.back, s16[144,128]{1,0:T(8,128)(2,1)S(1)} %collective-permute-done.7.across, s16[144,128]{1,0:T(8,128)(2,1)S(1)} %collective-permute-done.8.ring), custom_call_target="tpu_custom_call" | custom-call | tf_op jit(solution)/shard_map/finish/pallas_call | solution.py:311
  (1 shorter events, 0.0 us)
Async XLA Ops:
  1.8 7.8 %collective-permute-start.3 = (bf16[32,1024]{1,0:T(8,128)(2,1)S(1)}, bf16[32,1024]{1,0:T(8,128)(2,1)S(1)}, u32[]{:S(2)}, u32[]{:S(2)}) collective-permute-start(bf16[32,1024]{1,0:T(8,128)(2,1)S(1)} %get-tuple-element.11.refs_0_), channel_id=1, source_target_pairs={{0,2},{1,3},{2,0},{3,1},{4,6},{5,7},{6,4},{7,5},{8,10},{9,11},{10,... | collective-permute-start | bytes 196616 | tf_op jit(solution)/shard_map/ppermute | solution.py:18
  5.9 8.0 %collective-permute-start = (bf16[256,256]{1,0:T(8,128)(2,1)S(1)}, bf16[256,256]{1,0:T(8,128)(2,1)S(1)}, u32[]{:S(2)}, u32[]{:S(2)}) collective-permute-start(bf16[256,256]{1,0:T(8,128)(2,1)S(1)} %get-tuple-element.13), channel_id=1, source_target_pairs={{0,8},{4,12},{8,0},{12,4},{1,9},{5,13},{9,1},{13,5},{2,10},{6,14},... | collective-permute-start | bytes 393224 | tf_op jit(solution)/shard_map/ppermute | solution.py:18
  7.4 6.5 %collective-permute-start.1 = (bf16[256,256]{1,0:T(8,128)(2,1)S(1)}, bf16[256,256]{1,0:T(8,128)(2,1)S(1)}, u32[]{:S(2)}, u32[]{:S(2)}) collective-permute-start(bf16[256,256]{1,0:T(8,128)(2,1)S(1)} %get-tuple-element.14), channel_id=1, source_target_pairs={{0,4},{4,0},{8,12},{12,8},{1,5},{5,1},{9,13},{13,9},{2,6},{6,2},{1... | collective-permute-start | bytes 393224 | tf_op jit(solution)/shard_map/ppermute | solution.py:18
  7.4 6.5 %collective-permute-start.2 = (bf16[256,256]{1,0:T(8,128)(2,1)S(1)}, bf16[256,256]{1,0:T(8,128)(2,1)S(1)}, u32[]{:S(2)}, u32[]{:S(2)}) collective-permute-start(bf16[256,256]{1,0:T(8,128)(2,1)S(1)} %get-tuple-element.15), channel_id=1, source_target_pairs={{0,12},{4,8},{8,4},{12,0},{1,13},{5,9},{9,5},{13,1},{2,14},{6,10},... | collective-permute-start | bytes 393224 | tf_op jit(solution)/shard_map/ppermute | solution.py:18
  8.1 4.6 %collective-permute-start.4 = (bf16[32,1024]{1,0:T(8,128)(2,1)S(1)}, bf16[32,1024]{1,0:T(8,128)(2,1)S(1)}, u32[]{:S(2)}, u32[]{:S(2)}) collective-permute-start(bf16[32,1024]{1,0:T(8,128)(2,1)S(1)} %get-tuple-element.11.refs_0_), channel_id=1, source_target_pairs={{0,1},{1,0},{2,3},{3,2},{4,5},{5,4},{6,7},{7,6},{8,9},{9,8},{10,11... | collective-permute-start | bytes 196616 | tf_op jit(solution)/shard_map/ppermute | solution.py:18
  9.6 4.3 %collective-permute-start.5 = (bf16[32,1024]{1,0:T(8,128)(2,1)S(1)}, bf16[32,1024]{1,0:T(8,128)(2,1)S(1)}, u32[]{:S(2)}, u32[]{:S(2)}) collective-permute-start(bf16[32,1024]{1,0:T(8,128)(2,1)S(1)} %collective-permute-done.3.refs_5_), channel_id=1, source_target_pairs={{0,1},{1,0},{2,3},{3,2},{4,5},{5,4},{6,7},{7,6},{8,9},{9,8},{10,11... | collective-permute-start | bytes 196616 | tf_op jit(solution)/shard_map/ppermute | solution.py:18
  14.5 6.4 %collective-permute-start.8 = (s16[144,128]{1,0:T(8,128)(2,1)S(1)}, s16[144,128]{1,0:T(8,128)(2,1)S(1)}, u32[]{:S(2)}, u32[]{:S(2)}) collective-permute-start(s16[144,128]{1,0:T(8,128)(2,1)S(1)} %get-tuple-element.17.own), channel_id=1, source_target_pairs={{0,1},{1,3},{2,0},{3,2},{4,5},{5,7},{6,4},{7,6},{8,9},{9,11},{10,8... | collective-permute-start | bytes 110600 | tf_op jit(solution)/shard_map/ppermute | solution.py:351
  15.7 5.8 %collective-permute-start.7 = (s16[144,128]{1,0:T(8,128)(2,1)S(1)}, s16[144,128]{1,0:T(8,128)(2,1)S(1)}, u32[]{:S(2)}, u32[]{:S(2)}) collective-permute-start(s16[144,128]{1,0:T(8,128)(2,1)S(1)} %get-tuple-element.17.own), channel_id=1, source_target_pairs={{0,3},{1,2},{2,1},{3,0},{4,7},{5,6},{6,5},{7,4},{8,11},{9,10},{10,... | collective-permute-start | bytes 110600 | tf_op jit(solution)/shard_map/ppermute | solution.py:351
  18.1 4.0 %collective-permute-start.6 = (s16[144,128]{1,0:T(8,128)(2,1)S(1)}, s16[144,128]{1,0:T(8,128)(2,1)S(1)}, u32[]{:S(2)}, u32[]{:S(2)}) collective-permute-start(s16[144,128]{1,0:T(8,128)(2,1)S(1)} %get-tuple-element.17.own), channel_id=1, source_target_pairs={{0,2},{1,0},{2,3},{3,1},{4,6},{5,4},{6,7},{7,5},{8,10},{9,8},{10,1... | collective-permute-start | bytes 110600 | tf_op jit(solution)/shard_map/ppermute | solution.py:351
  20.1 1.9 %copy-start = (f32[128,128]{1,0:T(8,128)S(1)}, f32[128,128]{1,0:T(8,128)}, u32[]{:S(2)}) copy-start(f32[128,128]{1,0:T(8,128)} %diag_inverse.1) | copy-start | bytes 196612

commit v8 on v5

--- a/solution.py
+++ b/solution.py
@@ -261,14 +261,13 @@
             factor[block(col_index ^ step, local_rows), :] = part[...]
         else:
             greens.append((step, part))
-    total = jnp.zeros(solved.shape, jnp.float32)
-    for step, green in sorted(greens, key=lambda one: one[0]):
-        total = total + lax.dot_general(
-            factor[:, block(row_index ^ step, width)],
-            green[...],
-            (((1,), (1,)), ((), ())),
-            preferred_element_type=jnp.float32,
-        )
+    greens = sorted(greens, key=lambda one: one[0])
+    total = lax.dot_general(
+        jnp.concatenate([factor[:, block(row_index ^ step, width)] for step, _ in greens], axis=1),
+        jnp.concatenate([green[...] for _, green in greens], axis=1),
+        (((1,), (1,)), ((), ())),
+        preferred_element_type=jnp.float32,
+    )
     total = -total
     solved[...] = total
     pieces = []
@@ -277,11 +276,12 @@
         pieces.append(rest.astype(jnp.bfloat16))
         rest = rest - pieces[-1].astype(jnp.float32)
     own = factor[:, block(col_index, rows)]
-    value = 0.0
-    for piece in pieces[::-1]:
-        value = value + lax.dot_general(
-            piece, own, (((1,), (1,)), ((), ())), preferred_element_type=jnp.float32
-        )
+    value = lax.dot_general(
+        jnp.concatenate(pieces[::-1], axis=1),
+        jnp.concatenate([own] * len(pieces), axis=1),
+        (((1,), (1,)), ((), ())),
+        preferred_element_type=jnp.float32,
+    )
     code_of(value, coded)
 
 

time: 22.8 us -> 22.8 us (level)
  no operation moved by 1% of the time
where the time goes in v8:
time: 22.8 us; the launch traced here: 22.7 us
  starting transfers between devices  13.8 us (61%)
  waiting for transfers between devices  4.93 us (22%)
  Pallas kernels  2.44 us (11%)
  other arithmetic  0.73 us (3%)
  between operations  0.68 us (3%)
    ppermute x6, starting transfers between devices, partner(): return lax.ppermute(value, axis, [(a, a ^ step) for a in range(size)])  8.31 us
    ppermute x3, starting transfers between devices, per_device(): lax.ppermute(code, 'col', list(enumerate(moves)))  5.49 us
    ppermute x6, waiting for transfers between devices, partner(): return lax.ppermute(value, axis, [(a, a ^ step) for a in range(size)])  3.78 us
    pallas_call x1, Pallas kernels, pack(): pl.pallas_call(lambda *refs: pack_kernel(row_count, col_count, *refs), ou...  1.18 us
    ppermute x3, waiting for transfers between devices, per_device(): lax.ppermute(code, 'col', list(enumerate(moves)))  1.15 us
    mul x1, other arithmetic, per_device(): mask[p:p + 1] * jnp.tile(solved[:, p * size:(p + 1) * size], (1, group))  0.73 us
    pallas_call x1, Pallas kernels, finish(): pl.pallas_call(finish_kernel, out_shape=jax.ShapeDtypeStruct(diag_inverse...  0.67 us
    pallas_call x1, Pallas kernels, solve(): pl.pallas_call(lambda *refs: solve_kernel(origins, *refs), out_shape=[plt...  0.58 us
  transfers between devices with their start and end apart: 9, of which 4 were waited for; matrix products, arithmetic and copies ran while one was open for 4% of the time, Pallas kernels for 0%

profile of v8, /device:TPU:0, one launch (start us, length us, event | category | flops | bytes accessed | tf_op | source)
XLA Modules:
  0.0 22.7 jit_solution(1978074865640719354)
XLA Ops:
  0.6 1.2 %pack.1 = (bf16[32,1024]{1,0:T(8,128)(2,1)S(1)}, f32[1,512]{1,0:T(1,128)S(1)}, bf16[256,256]{1,0:T(8,128)(2,1)S(1)}, bf16[256,256]{1,0:T(8,128)(2,1)S(1)}, bf16[...) custom-call(s32[4,8]{1,0:T(4,128)} %refs_0_.1, bf16[512,512]{1,0:T(8,128)(2,1)} %refs_1_.1, bf16[32,2048]{1,0:T(8,128)(2,1)} %refs_2_.1), custom_call_target="tpu_custom_call" | custom-call | tf_op jit(solution)/shard_map/pack/pallas_call | solution.py:219
  1.8 4.1 %collective-permute-start.3 = (bf16[32,1024]{1,0:T(8,128)(2,1)S(1)}, bf16[32,1024]{1,0:T(8,128)(2,1)S(1)}, u32[]{:S(2)}, u32[]{:S(2)}) collective-permute-start(bf16[32,1024]{1,0:T(8,128)(2,1)S(1)} %get-tuple-element.11.refs_0_), channel_id=1, source_target_pairs={{0,2},{1,3},{2,0},{3,1},{4,6},{5,7},{6,4},{7,5},{8,10},{9,11},{10,... | collective-permute-start | bytes 196616 | tf_op jit(solution)/shard_map/ppermute | solution.py:18
  5.9 1.5 %collective-permute-start = (bf16[256,256]{1,0:T(8,128)(2,1)S(1)}, bf16[256,256]{1,0:T(8,128)(2,1)S(1)}, u32[]{:S(2)}, u32[]{:S(2)}) collective-permute-start(bf16[256,256]{1,0:T(8,128)(2,1)S(1)} %get-tuple-element.13), channel_id=1, source_target_pairs={{0,8},{4,12},{8,0},{12,4},{1,9},{5,13},{9,1},{13,5},{2,10},{6,14},... | collective-permute-start | bytes 393224 | tf_op jit(solution)/shard_map/ppermute | solution.py:18
  7.4 0.0 collective-permute-start.1
  7.4 0.6 %collective-permute-start.2 = (bf16[256,256]{1,0:T(8,128)(2,1)S(1)}, bf16[256,256]{1,0:T(8,128)(2,1)S(1)}, u32[]{:S(2)}, u32[]{:S(2)}) collective-permute-start(bf16[256,256]{1,0:T(8,128)(2,1)S(1)} %get-tuple-element.15), channel_id=1, source_target_pairs={{0,4},{4,0},{8,12},{12,8},{1,5},{5,1},{9,13},{13,9},{2,6},{6,2},{1... | collective-permute-start | bytes 393224 | tf_op jit(solution)/shard_map/ppermute | solution.py:18
  8.1 1.6 %collective-permute-start.4 = (bf16[32,1024]{1,0:T(8,128)(2,1)S(1)}, bf16[32,1024]{1,0:T(8,128)(2,1)S(1)}, u32[]{:S(2)}, u32[]{:S(2)}) collective-permute-start(bf16[32,1024]{1,0:T(8,128)(2,1)S(1)} %get-tuple-element.11.refs_0_), channel_id=1, source_target_pairs={{0,1},{1,0},{2,3},{3,2},{4,5},{5,4},{6,7},{7,6},{8,9},{9,8},{10,11... | collective-permute-start | bytes 196616 | tf_op jit(solution)/shard_map/ppermute | solution.py:18
  9.6 0.0 collective-permute-done.3.refs_5_
  9.6 0.5 %collective-permute-start.5 = (bf16[32,1024]{1,0:T(8,128)(2,1)S(1)}, bf16[32,1024]{1,0:T(8,128)(2,1)S(1)}, u32[]{:S(2)}, u32[]{:S(2)}) collective-permute-start(bf16[32,1024]{1,0:T(8,128)(2,1)S(1)} %collective-permute-done.3.refs_5_), channel_id=1, source_target_pairs={{0,1},{1,0},{2,3},{3,2},{4,5},{5,4},{6,7},{7,6},{8,9},{9,8},{10,11... | collective-permute-start | bytes 196616 | tf_op jit(solution)/shard_map/ppermute | solution.py:18
  10.1 2.6 %collective-permute-done.4.refs_6_ = bf16[32,1024]{1,0:T(8,128)(2,1)S(1)} collective-permute-done((bf16[32,1024]{1,0:T(8,128)(2,1)S(1)}, bf16[32,1024]{1,0:T(8,128)(2,1)S(1)}, u32[]{:S(2)}, u32[]{:S(2)}) %collective-permute-start.4) | collective-permute-done | bytes 65568 | tf_op jit(solution)/shard_map/ppermute | solution.py:18
  12.7 1.2 %collective-permute-done.5.refs_7_ = bf16[32,1024]{1,0:T(8,128)(2,1)S(1)} collective-permute-done((bf16[32,1024]{1,0:T(8,128)(2,1)S(1)}, bf16[32,1024]{1,0:T(8,128)(2,1)S(1)}, u32[]{:S(2)}, u32[]{:S(2)}) %collective-permute-start.5) | collective-permute-done | bytes 65568 | tf_op jit(solution)/shard_map/ppermute | solution.py:18
  13.9 0.0 collective-permute-done.refs_2_
  13.9 0.0 collective-permute-done.1.refs_3_
  13.9 0.0 collective-permute-done.2.refs_4_
  13.9 0.6 %solve.1 = (f32[128,256]{1,0:T(8,128)S(1)}, s16[144,128]{1,0:T(8,128)(2,1)S(1)}) custom-call(bf16[32,1024]{1,0:T(8,128)(2,1)S(1)} %get-tuple-element.11.refs_0_, bf16[256,256]{1,0:T(8,128)(2,1)S(1)} %get-tuple-element.12.refs_1_, bf16[256,256]{1,0:T(8,128)(2,1)S(1)} %collective-permute-done.refs_2_, bf16[256,256]{1,0:T(8,128)(2,1)S(1)} %collective-permute-done.1.refs_3_, ...), custom_call_target="tpu_custom_call" | custom-call | tf_op jit(solution)/shard_map/solve/pallas_call | solution.py:291
  14.5 1.2 %collective-permute-start.8 = (s16[144,128]{1,0:T(8,128)(2,1)S(1)}, s16[144,128]{1,0:T(8,128)(2,1)S(1)}, u32[]{:S(2)}, u32[]{:S(2)}) collective-permute-start(s16[144,128]{1,0:T(8,128)(2,1)S(1)} %get-tuple-element.17.own), channel_id=1, source_target_pairs={{0,1},{1,3},{2,0},{3,2},{4,5},{5,7},{6,4},{7,6},{8,9},{9,11},{10,8... | collective-permute-start | bytes 110600 | tf_op jit(solution)/shard_map/ppermute | solution.py:351
  15.7 2.4 %collective-permute-start.7 = (s16[144,128]{1,0:T(8,128)(2,1)S(1)}, s16[144,128]{1,0:T(8,128)(2,1)S(1)}, u32[]{:S(2)}, u32[]{:S(2)}) collective-permute-start(s16[144,128]{1,0:T(8,128)(2,1)S(1)} %get-tuple-element.17.own), channel_id=1, source_target_pairs={{0,3},{1,2},{2,1},{3,0},{4,7},{5,6},{6,5},{7,4},{8,11},{9,10},{10,... | collective-permute-start | bytes 110600 | tf_op jit(solution)/shard_map/ppermute | solution.py:351
  18.1 1.9 %collective-permute-start.6 = (s16[144,128]{1,0:T(8,128)(2,1)S(1)}, s16[144,128]{1,0:T(8,128)(2,1)S(1)}, u32[]{:S(2)}, u32[]{:S(2)}) collective-permute-start(s16[144,128]{1,0:T(8,128)(2,1)S(1)} %get-tuple-element.17.own), channel_id=1, source_target_pairs={{0,2},{1,0},{2,3},{3,1},{4,6},{5,4},{6,7},{7,5},{8,10},{9,8},{10,1... | collective-permute-start | bytes 110600 | tf_op jit(solution)/shard_map/ppermute | solution.py:351
  20.0 0.1 tile.4
  20.1 0.0 copy-start
  20.1 0.7 %broadcast_multiply_fusion = f32[128,512]{1,0:T(8,128)} fusion(f32[128,512]{1,0:T(8,128)S(1)} %bitcast.4, f32[512]{0:T(512)S(1)} %bitcast.3), kind=kLoop, calls=%fused_computation | loop fusion | flops 65536 | bytes 526336 | tf_op jit(solution)/shard_map/mul | solution.py:348
  20.9 0.0 collective-permute-done.8.ring
  20.9 0.6 %collective-permute-done.7.across = s16[144,128]{1,0:T(8,128)(2,1)S(1)} collective-permute-done((s16[144,128]{1,0:T(8,128)(2,1)S(1)}, s16[144,128]{1,0:T(8,128)(2,1)S(1)}, u32[]{:S(2)}, u32[]{:S(2)}) %collective-permute-start.7) | collective-permute-done | bytes 36896 | tf_op jit(solution)/shard_map/ppermute | solution.py:351
  21.5 0.6 %collective-permute-done.6.back = s16[144,128]{1,0:T(8,128)(2,1)S(1)} collective-permute-done((s16[144,128]{1,0:T(8,128)(2,1)S(1)}, s16[144,128]{1,0:T(8,128)(2,1)S(1)}, u32[]{:S(2)}, u32[]{:S(2)}) %collective-permute-start.6) | collective-permute-done | bytes 36896 | tf_op jit(solution)/shard_map/ppermute | solution.py:351
  22.0 0.0 copy-done
  22.0 0.7 %finish.1 = f32[128,128]{1,0:T(8,128)} custom-call(f32[128,128]{1,0:T(8,128)S(1)} %copy-done, s16[144,128]{1,0:T(8,128)(2,1)S(1)} %get-tuple-element.17.own, s16[144,128]{1,0:T(8,128)(2,1)S(1)} %collective-permute-done.6.back, s16[144,128]{1,0:T(8,128)(2,1)S(1)} %collective-permute-done.7.across, s16[144,128]{1,0:T(8,128)(2,1)S(1)} %collective-permute-done.8.ring), custom_call_target="tpu_custom_call" | custom-call | tf_op jit(solution)/shard_map/finish/pallas_call | solution.py:311
  (1 shorter events, 0.0 us)
Async XLA Ops:
  1.8 7.8 %collective-permute-start.3 = (bf16[32,1024]{1,0:T(8,128)(2,1)S(1)}, bf16[32,1024]{1,0:T(8,128)(2,1)S(1)}, u32[]{:S(2)}, u32[]{:S(2)}) collective-permute-start(bf16[32,1024]{1,0:T(8,128)(2,1)S(1)} %get-tuple-element.11.refs_0_), channel_id=1, source_target_pairs={{0,2},{1,3},{2,0},{3,1},{4,6},{5,7},{6,4},{7,5},{8,10},{9,11},{10,... | collective-permute-start | bytes 196616 | tf_op jit(solution)/shard_map/ppermute | solution.py:18
  5.9 8.0 %collective-permute-start = (bf16[256,256]{1,0:T(8,128)(2,1)S(1)}, bf16[256,256]{1,0:T(8,128)(2,1)S(1)}, u32[]{:S(2)}, u32[]{:S(2)}) collective-permute-start(bf16[256,256]{1,0:T(8,128)(2,1)S(1)} %get-tuple-element.13), channel_id=1, source_target_pairs={{0,8},{4,12},{8,0},{12,4},{1,9},{5,13},{9,1},{13,5},{2,10},{6,14},... | collective-permute-start | bytes 393224 | tf_op jit(solution)/shard_map/ppermute | solution.py:18
  7.4 6.5 %collective-permute-start.1 = (bf16[256,256]{1,0:T(8,128)(2,1)S(1)}, bf16[256,256]{1,0:T(8,128)(2,1)S(1)}, u32[]{:S(2)}, u32[]{:S(2)}) collective-permute-start(bf16[256,256]{1,0:T(8,128)(2,1)S(1)} %get-tuple-element.14), channel_id=1, source_target_pairs={{0,12},{4,8},{8,4},{12,0},{1,13},{5,9},{9,5},{13,1},{2,14},{6,10},... | collective-permute-start | bytes 393224 | tf_op jit(solution)/shard_map/ppermute | solution.py:18
  7.4 6.5 %collective-permute-start.2 = (bf16[256,256]{1,0:T(8,128)(2,1)S(1)}, bf16[256,256]{1,0:T(8,128)(2,1)S(1)}, u32[]{:S(2)}, u32[]{:S(2)}) collective-permute-start(bf16[256,256]{1,0:T(8,128)(2,1)S(1)} %get-tuple-element.15), channel_id=1, source_target_pairs={{0,4},{4,0},{8,12},{12,8},{1,5},{5,1},{9,13},{13,9},{2,6},{6,2},{1... | collective-permute-start | bytes 393224 | tf_op jit(solution)/shard_map/ppermute | solution.py:18
  8.1 4.6 %collective-permute-start.4 = (bf16[32,1024]{1,0:T(8,128)(2,1)S(1)}, bf16[32,1024]{1,0:T(8,128)(2,1)S(1)}, u32[]{:S(2)}, u32[]{:S(2)}) collective-permute-start(bf16[32,1024]{1,0:T(8,128)(2,1)S(1)} %get-tuple-element.11.refs_0_), channel_id=1, source_target_pairs={{0,1},{1,0},{2,3},{3,2},{4,5},{5,4},{6,7},{7,6},{8,9},{9,8},{10,11... | collective-permute-start | bytes 196616 | tf_op jit(solution)/shard_map/ppermute | solution.py:18
  9.6 4.3 %collective-permute-start.5 = (bf16[32,1024]{1,0:T(8,128)(2,1)S(1)}, bf16[32,1024]{1,0:T(8,128)(2,1)S(1)}, u32[]{:S(2)}, u32[]{:S(2)}) collective-permute-start(bf16[32,1024]{1,0:T(8,128)(2,1)S(1)} %collective-permute-done.3.refs_5_), channel_id=1, source_target_pairs={{0,1},{1,0},{2,3},{3,2},{4,5},{5,4},{6,7},{7,6},{8,9},{9,8},{10,11... | collective-permute-start | bytes 196616 | tf_op jit(solution)/shard_map/ppermute | solution.py:18
  14.5 6.4 %collective-permute-start.8 = (s16[144,128]{1,0:T(8,128)(2,1)S(1)}, s16[144,128]{1,0:T(8,128)(2,1)S(1)}, u32[]{:S(2)}, u32[]{:S(2)}) collective-permute-start(s16[144,128]{1,0:T(8,128)(2,1)S(1)} %get-tuple-element.17.own), channel_id=1, source_target_pairs={{0,1},{1,3},{2,0},{3,2},{4,5},{5,7},{6,4},{7,6},{8,9},{9,11},{10,8... | collective-permute-start | bytes 110600 | tf_op jit(solution)/shard_map/ppermute | solution.py:351
  15.7 5.8 %collective-permute-start.7 = (s16[144,128]{1,0:T(8,128)(2,1)S(1)}, s16[144,128]{1,0:T(8,128)(2,1)S(1)}, u32[]{:S(2)}, u32[]{:S(2)}) collective-permute-start(s16[144,128]{1,0:T(8,128)(2,1)S(1)} %get-tuple-element.17.own), channel_id=1, source_target_pairs={{0,3},{1,2},{2,1},{3,0},{4,7},{5,6},{6,5},{7,4},{8,11},{9,10},{10,... | collective-permute-start | bytes 110600 | tf_op jit(solution)/shard_map/ppermute | solution.py:351
  18.1 4.0 %collective-permute-start.6 = (s16[144,128]{1,0:T(8,128)(2,1)S(1)}, s16[144,128]{1,0:T(8,128)(2,1)S(1)}, u32[]{:S(2)}, u32[]{:S(2)}) collective-permute-start(s16[144,128]{1,0:T(8,128)(2,1)S(1)} %get-tuple-element.17.own), channel_id=1, source_target_pairs={{0,2},{1,0},{2,3},{3,1},{4,6},{5,4},{6,7},{7,5},{8,10},{9,8},{10,1... | collective-permute-start | bytes 110600 | tf_op jit(solution)/shard_map/ppermute | solution.py:351
  20.1 1.9 %copy-start = (f32[128,128]{1,0:T(8,128)S(1)}, f32[128,128]{1,0:T(8,128)}, u32[]{:S(2)}) copy-start(f32[128,128]{1,0:T(8,128)} %diag_inverse.1) | copy-start | bytes 196612

commit v9 on v4

--- a/solution.py
+++ b/solution.py
@@ -7,7 +7,16 @@
 
 
 EXPONENT_ROWS = 16
-OPERANDS = (0, 4, 6, 7, 2, 1, 5, 3)
+ROW_MOVES = ((0, 1, 2, 3), (3, 2, 0, 1), (1, 0, 3, 2), (2, 3, 1, 0))
+
+
+def looked_up(table, index):
+    return sum(jnp.where(index == a, b, 0) for a, b in enumerate(table))
+
+
+def sources(table):
+    return [table.index(a) for a in range(len(table))]
+OPERANDS = (0, 4, 5, 6, 7, 1, 2, 3)
 
 
 def partner(value, axis, step):
@@ -173,8 +182,8 @@
     copies[0].wait()
     chosen = [
         (
-            places(fill, row_index ^ s, col_index * group, group, half),
-            places(fill, row_index ^ s, row_index * chunk, chunk, kept),
+            places(fill, looked_up(ROW_MOVES[s], row_index), col_index * group, group, half),
+            places(fill, looked_up(ROW_MOVES[s], row_index), row_index * chunk, chunk, kept),
         )
         for s in range(row_count)
     ]
@@ -243,12 +252,14 @@
     col_index = lax.axis_index("col")
     local_rows = factors[0].shape[0]
     rows, width = greens[0].shape
-    for t in range(col_count):
-        factor[block(col_index ^ t, local_rows), :] = factors[t][...]
+    origins = [(0, 1, 2, 3)] + [(2, 3, 0, 1), (1, 0, 3, 2), (3, 2, 1, 0)]
+    for origin, part in zip(origins, factors):
+        place = sum(jnp.where(col_index == a, o, 0) for a, o in enumerate(origin))
+        factor[block(place, local_rows), :] = part[...]
     total = jnp.zeros(solved.shape, jnp.float32)
     for s in range(row_count):
         total = total + lax.dot_general(
-            factor[:, block(row_index ^ s, width)],
+            factor[:, block(looked_up(sources(ROW_MOVES[s]), row_index), width)],
             greens[s][...],
             (((1,), (1,)), ((), ())),
             preferred_element_type=jnp.float32,
@@ -301,10 +312,8 @@
     for code in codes:
         exponent = code[count:, :].astype(jnp.int32).astype(jnp.float32)[:1]
         sums.append(code[:count, :].astype(jnp.int32).astype(jnp.float32) * jnp.exp2(exponent - 14.0))
-    sums = [sums[n] for n in [0, 1, 3, 2]]
-    while len(sums) > 1:
-        sums = [a + b for a, b in zip(sums[::2], sums[1::2])]
-    out[...] = diag_inverse[...] - sums[0]
+    total = (sums[0] + sums[2]) + (sums[3] + sums[1])
+    out[...] = diag_inverse[...] - total
 
 
 def finish(diag_inverse, codes):
@@ -330,23 +339,34 @@
     size = factor_cols.shape[1] // blocks
 
     own_factor, mask, *greens = pack(green_top, factor_cols, fill_blocks)
-    far, cross = partner(greens[2], "row", 2), partner(greens[3], "row", 3)
-    near = partner(greens[1], "row", 1)
-    parts = {"c": near, "x": far, "xc": cross}
-    parts["z2"] = partner(own_factor, "col", 2)
-    parts["z1"] = partner(own_factor, "col", 1)
-    held = []
-    passed, *rest = lax.optimization_barrier((parts["z2"], *[parts[n] for n in held]))
-    parts.update(zip(held, rest))
-    parts["z3"] = partner(passed, "col", 1)
+    moves = {
+        "b+": (1, 3, 0, 2),
+        "b-": (2, 0, 3, 1),
+        "z1": (1, 0, 3, 2),
+        "z2": (2, 3, 0, 1),
+        "z3": (3, 2, 1, 0),
+    }
+
+    def moved(value, name):
+        return lax.ppermute(value, "col", list(enumerate(moves[name])))
+
+    def crossed(value, m):
+        return lax.ppermute(value, "row", list(enumerate(ROW_MOVES[m])))
+
+    parts = {n: crossed(greens[m], m) for m, n in ((1, "c"), (2, "x"), (3, "xc"))}
+    parts["z1"] = moved(own_factor, "z1")
+    parts["z2"] = moved(own_factor, "z2")
+    passed, *rest = lax.optimization_barrier((parts["z2"], *[parts[n] for n in []]))
+    parts.update(zip([], rest))
+    parts["fw"] = moved(passed, "z1")
     greens = [greens[0], parts["c"], parts["x"], parts["xc"]]
-    factors = [own_factor] + [parts["z%d" % t] for t in range(1, col_count)]
+    factors = [own_factor] + [parts[n] for n in ['z2', 'z1', 'fw']]
     solved, code = solve(factors, greens)
     green_cols = None
     for p in range(half):
         term = mask[p : p + 1] * jnp.tile(solved[:, p * size : (p + 1) * size], (1, group))
         green_cols = term if green_cols is None else green_cols + term
-    codes = [code] + [partner(code, "col", t) for t in [1, 3, 2]]
+    codes = [code] + [moved(code, name) for name in ['b-', 'z3', 'b+']]
     return (green_cols, finish(diag_inverse, codes))
 
 

time: 23.3 us -> 22.8 us (0.979)
  waiting for transfers between devices: 6.79 us -> 4.9 us
  starting transfers between devices: 12.4 us -> 13.8 us
    ppermute x9, waiting for transfers between devices: 6.79 us -> 4.9 us  [the longest x6 4.89 us: moved(): return lax.ppermute(value, 'col', list(enumerate(moves[name])))]
    ppermute x9, starting transfers between devices: 12.4 us -> 13.8 us  [the longest x6 11.8 us: moved(): return lax.ppermute(value, 'col', list(enumerate(moves[name])))]
where the time goes in v9:
time: 22.8 us; the launch traced here: 22.7 us
  starting transfers between devices  13.8 us (61%)
  waiting for transfers between devices  4.9 us (21%)
  Pallas kernels  2.44 us (11%)
  other arithmetic  0.73 us (3%)
  between operations  0.68 us (3%)
    ppermute x6, starting transfers between devices, moved(): return lax.ppermute(value, 'col', list(enumerate(moves[name])))  11.8 us
    ppermute x6, waiting for transfers between devices, moved(): return lax.ppermute(value, 'col', list(enumerate(moves[name])))  4.89 us
    ppermute x3, starting transfers between devices, crossed(): return lax.ppermute(value, 'row', list(enumerate(ROW_MOVES[m])))  2.03 us
    pallas_call x1, Pallas kernels, pack(): pl.pallas_call(lambda *refs: pack_kernel(row_count, col_count, *refs), ou...  1.18 us
    mul x1, other arithmetic, per_device(): mask[p:p + 1] * jnp.tile(solved[:, p * size:(p + 1) * size], (1, group))  0.73 us
    pallas_call x1, Pallas kernels, finish(): pl.pallas_call(finish_kernel, out_shape=jax.ShapeDtypeStruct(diag_inverse...  0.67 us
    pallas_call x1, Pallas kernels, solve(): pl.pallas_call(lambda *refs: solve_kernel(row_count, col_count, *refs), o...  0.58 us
  transfers between devices with their start and end apart: 9, of which 4 were waited for; matrix products, arithmetic and copies ran while one was open for 4% of the time, Pallas kernels for 0%

profile of v9, /device:TPU:0, one launch (start us, length us, event | category | flops | bytes accessed | tf_op | source)
XLA Modules:
  0.0 22.7 jit_solution(1619780066910426129)
XLA Ops:
  0.6 1.2 %pack.1 = (bf16[32,1024]{1,0:T(8,128)(2,1)S(1)}, f32[1,512]{1,0:T(1,128)S(1)}, bf16[256,256]{1,0:T(8,128)(2,1)S(1)}, bf16[256,256]{1,0:T(8,128)(2,1)S(1)}, bf16[...) custom-call(s32[4,8]{1,0:T(4,128)} %refs_0_.1, bf16[512,512]{1,0:T(8,128)(2,1)} %refs_1_.1, bf16[32,2048]{1,0:T(8,128)(2,1)} %refs_2_.1), custom_call_target="tpu_custom_call" | custom-call | tf_op jit(solution)/shard_map/pack/pallas_call | solution.py:225
  1.8 4.1 %collective-permute-start.3 = (bf16[32,1024]{1,0:T(8,128)(2,1)S(1)}, bf16[32,1024]{1,0:T(8,128)(2,1)S(1)}, u32[]{:S(2)}, u32[]{:S(2)}) collective-permute-start(bf16[32,1024]{1,0:T(8,128)(2,1)S(1)} %get-tuple-element.11.refs_0_), channel_id=1, source_target_pairs={{0,2},{1,3},{2,0},{3,1},{4,6},{5,7},{6,4},{7,5},{8,10},{9,11},{10,... | collective-permute-start | bytes 196616 | tf_op jit(solution)/shard_map/ppermute | solution.py:351
  5.9 0.7 %collective-permute-start = (bf16[256,256]{1,0:T(8,128)(2,1)S(1)}, bf16[256,256]{1,0:T(8,128)(2,1)S(1)}, u32[]{:S(2)}, u32[]{:S(2)}) collective-permute-start(bf16[256,256]{1,0:T(8,128)(2,1)S(1)} %get-tuple-element.13), channel_id=1, source_target_pairs={{0,12},{4,8},{8,0},{12,4},{1,13},{5,9},{9,1},{13,5},{2,14},{6,10},... | collective-permute-start | bytes 393224 | tf_op jit(solution)/shard_map/ppermute | solution.py:354
  6.6 1.0 %collective-permute-start.1 = (bf16[256,256]{1,0:T(8,128)(2,1)S(1)}, bf16[256,256]{1,0:T(8,128)(2,1)S(1)}, u32[]{:S(2)}, u32[]{:S(2)}) collective-permute-start(bf16[256,256]{1,0:T(8,128)(2,1)S(1)} %get-tuple-element.14), channel_id=1, source_target_pairs={{0,4},{4,0},{8,12},{12,8},{1,5},{5,1},{9,13},{13,9},{2,6},{6,2},{1... | collective-permute-start | bytes 393224 | tf_op jit(solution)/shard_map/ppermute | solution.py:354
  7.5 0.4 %collective-permute-start.2 = (bf16[256,256]{1,0:T(8,128)(2,1)S(1)}, bf16[256,256]{1,0:T(8,128)(2,1)S(1)}, u32[]{:S(2)}, u32[]{:S(2)}) collective-permute-start(bf16[256,256]{1,0:T(8,128)(2,1)S(1)} %get-tuple-element.15), channel_id=1, source_target_pairs={{0,8},{4,12},{8,4},{12,0},{1,9},{5,13},{9,5},{13,1},{2,10},{6,14},... | collective-permute-start | bytes 393224 | tf_op jit(solution)/shard_map/ppermute | solution.py:354
  8.0 1.6 %collective-permute-start.4 = (bf16[32,1024]{1,0:T(8,128)(2,1)S(1)}, bf16[32,1024]{1,0:T(8,128)(2,1)S(1)}, u32[]{:S(2)}, u32[]{:S(2)}) collective-permute-start(bf16[32,1024]{1,0:T(8,128)(2,1)S(1)} %get-tuple-element.11.refs_0_), channel_id=1, source_target_pairs={{0,1},{1,0},{2,3},{3,2},{4,5},{5,4},{6,7},{7,6},{8,9},{9,8},{10,11... | collective-permute-start | bytes 196616 | tf_op jit(solution)/shard_map/ppermute | solution.py:351
  9.5 0.0 collective-permute-done.3.refs_5_
  9.6 0.6 %collective-permute-start.5 = (bf16[32,1024]{1,0:T(8,128)(2,1)S(1)}, bf16[32,1024]{1,0:T(8,128)(2,1)S(1)}, u32[]{:S(2)}, u32[]{:S(2)}) collective-permute-start(bf16[32,1024]{1,0:T(8,128)(2,1)S(1)} %collective-permute-done.3.refs_5_), channel_id=1, source_target_pairs={{0,1},{1,0},{2,3},{3,2},{4,5},{5,4},{6,7},{7,6},{8,9},{9,8},{10,11... | collective-permute-start | bytes 196616 | tf_op jit(solution)/shard_map/ppermute | solution.py:351
  10.1 2.3 %collective-permute-done.4.refs_6_ = bf16[32,1024]{1,0:T(8,128)(2,1)S(1)} collective-permute-done((bf16[32,1024]{1,0:T(8,128)(2,1)S(1)}, bf16[32,1024]{1,0:T(8,128)(2,1)S(1)}, u32[]{:S(2)}, u32[]{:S(2)}) %collective-permute-start.4) | collective-permute-done | bytes 65568 | tf_op jit(solution)/shard_map/ppermute | solution.py:351
  12.4 1.4 %collective-permute-done.5.refs_7_ = bf16[32,1024]{1,0:T(8,128)(2,1)S(1)} collective-permute-done((bf16[32,1024]{1,0:T(8,128)(2,1)S(1)}, bf16[32,1024]{1,0:T(8,128)(2,1)S(1)}, u32[]{:S(2)}, u32[]{:S(2)}) %collective-permute-start.5) | collective-permute-done | bytes 65568 | tf_op jit(solution)/shard_map/ppermute | solution.py:351
  13.8 0.0 collective-permute-done.refs_2_
  13.8 0.0 collective-permute-done.1.refs_3_
  13.8 0.0 collective-permute-done.2.refs_4_
  13.9 0.6 %solve.1 = (f32[128,256]{1,0:T(8,128)S(1)}, s16[144,128]{1,0:T(8,128)(2,1)S(1)}) custom-call(bf16[32,1024]{1,0:T(8,128)(2,1)S(1)} %get-tuple-element.11.refs_0_, bf16[256,256]{1,0:T(8,128)(2,1)S(1)} %get-tuple-element.12.refs_1_, bf16[256,256]{1,0:T(8,128)(2,1)S(1)} %collective-permute-done.refs_2_, bf16[256,256]{1,0:T(8,128)(2,1)S(1)} %collective-permute-done.1.refs_3_, ...), custom_call_target="tpu_custom_call" | custom-call | tf_op jit(solution)/shard_map/solve/pallas_call | solution.py:294
  14.4 1.4 %collective-permute-start.8 = (s16[144,128]{1,0:T(8,128)(2,1)S(1)}, s16[144,128]{1,0:T(8,128)(2,1)S(1)}, u32[]{:S(2)}, u32[]{:S(2)}) collective-permute-start(s16[144,128]{1,0:T(8,128)(2,1)S(1)} %get-tuple-element.17.refs_0_), channel_id=1, source_target_pairs={{0,1},{1,3},{2,0},{3,2},{4,5},{5,7},{6,4},{7,6},{8,9},{9,11},{10,8... | collective-permute-start | bytes 110600 | tf_op jit(solution)/shard_map/ppermute | solution.py:351
  15.8 2.2 %collective-permute-start.7 = (s16[144,128]{1,0:T(8,128)(2,1)S(1)}, s16[144,128]{1,0:T(8,128)(2,1)S(1)}, u32[]{:S(2)}, u32[]{:S(2)}) collective-permute-start(s16[144,128]{1,0:T(8,128)(2,1)S(1)} %get-tuple-element.17.refs_0_), channel_id=1, source_target_pairs={{0,3},{1,2},{2,1},{3,0},{4,7},{5,6},{6,5},{7,4},{8,11},{9,10},{10,... | collective-permute-start | bytes 110600 | tf_op jit(solution)/shard_map/ppermute | solution.py:351
  18.0 1.9 %collective-permute-start.6 = (s16[144,128]{1,0:T(8,128)(2,1)S(1)}, s16[144,128]{1,0:T(8,128)(2,1)S(1)}, u32[]{:S(2)}, u32[]{:S(2)}) collective-permute-start(s16[144,128]{1,0:T(8,128)(2,1)S(1)} %get-tuple-element.17.refs_0_), channel_id=1, source_target_pairs={{0,2},{1,0},{2,3},{3,1},{4,6},{5,4},{6,7},{7,5},{8,10},{9,8},{10,1... | collective-permute-start | bytes 110600 | tf_op jit(solution)/shard_map/ppermute | solution.py:351
  20.0 0.1 tile.4
  20.1 0.0 copy-start
  20.1 0.7 %broadcast_multiply_fusion = f32[128,512]{1,0:T(8,128)} fusion(f32[128,512]{1,0:T(8,128)S(1)} %bitcast.4, f32[512]{0:T(512)S(1)} %bitcast.3), kind=kLoop, calls=%fused_computation | loop fusion | flops 65536 | bytes 526336 | tf_op jit(solution)/shard_map/mul | solution.py:367
  20.9 0.0 collective-permute-done.8.refs_3_
  20.9 0.7 %collective-permute-done.7.refs_2_ = s16[144,128]{1,0:T(8,128)(2,1)S(1)} collective-permute-done((s16[144,128]{1,0:T(8,128)(2,1)S(1)}, s16[144,128]{1,0:T(8,128)(2,1)S(1)}, u32[]{:S(2)}, u32[]{:S(2)}) %collective-permute-start.7) | collective-permute-done | bytes 36896 | tf_op jit(solution)/shard_map/ppermute | solution.py:351
  21.6 0.4 %collective-permute-done.6.refs_1_ = s16[144,128]{1,0:T(8,128)(2,1)S(1)} collective-permute-done((s16[144,128]{1,0:T(8,128)(2,1)S(1)}, s16[144,128]{1,0:T(8,128)(2,1)S(1)}, u32[]{:S(2)}, u32[]{:S(2)}) %collective-permute-start.6) | collective-permute-done | bytes 36896 | tf_op jit(solution)/shard_map/ppermute | solution.py:351
  22.0 0.0 copy-done
  22.0 0.7 %finish.1 = f32[128,128]{1,0:T(8,128)} custom-call(f32[128,128]{1,0:T(8,128)S(1)} %copy-done, s16[144,128]{1,0:T(8,128)(2,1)S(1)} %get-tuple-element.17.refs_0_, s16[144,128]{1,0:T(8,128)(2,1)S(1)} %collective-permute-done.6.refs_1_, s16[144,128]{1,0:T(8,128)(2,1)S(1)} %collective-permute-done.7.refs_2_, s16[144,128]{1,0:T(8,128)(2,1)S(1)} %collective-permute-done.8.refs_3_), custom_call_target="tpu_custom_call" | custom-call | tf_op jit(solution)/shard_map/finish/pallas_call | solution.py:320
  (1 shorter events, 0.0 us)
Async XLA Ops:
  1.8 7.8 %collective-permute-start.3 = (bf16[32,1024]{1,0:T(8,128)(2,1)S(1)}, bf16[32,1024]{1,0:T(8,128)(2,1)S(1)}, u32[]{:S(2)}, u32[]{:S(2)}) collective-permute-start(bf16[32,1024]{1,0:T(8,128)(2,1)S(1)} %get-tuple-element.11.refs_0_), channel_id=1, source_target_pairs={{0,2},{1,3},{2,0},{3,1},{4,6},{5,7},{6,4},{7,5},{8,10},{9,11},{10,... | collective-permute-start | bytes 196616 | tf_op jit(solution)/shard_map/ppermute | solution.py:351
  5.9 7.9 %collective-permute-start = (bf16[256,256]{1,0:T(8,128)(2,1)S(1)}, bf16[256,256]{1,0:T(8,128)(2,1)S(1)}, u32[]{:S(2)}, u32[]{:S(2)}) collective-permute-start(bf16[256,256]{1,0:T(8,128)(2,1)S(1)} %get-tuple-element.13), channel_id=1, source_target_pairs={{0,12},{4,8},{8,0},{12,4},{1,13},{5,9},{9,1},{13,5},{2,14},{6,10},... | collective-permute-start | bytes 393224 | tf_op jit(solution)/shard_map/ppermute | solution.py:354
  6.6 7.3 %collective-permute-start.1 = (bf16[256,256]{1,0:T(8,128)(2,1)S(1)}, bf16[256,256]{1,0:T(8,128)(2,1)S(1)}, u32[]{:S(2)}, u32[]{:S(2)}) collective-permute-start(bf16[256,256]{1,0:T(8,128)(2,1)S(1)} %get-tuple-element.14), channel_id=1, source_target_pairs={{0,4},{4,0},{8,12},{12,8},{1,5},{5,1},{9,13},{13,9},{2,6},{6,2},{1... | collective-permute-start | bytes 393224 | tf_op jit(solution)/shard_map/ppermute | solution.py:354
  7.5 6.3 %collective-permute-start.2 = (bf16[256,256]{1,0:T(8,128)(2,1)S(1)}, bf16[256,256]{1,0:T(8,128)(2,1)S(1)}, u32[]{:S(2)}, u32[]{:S(2)}) collective-permute-start(bf16[256,256]{1,0:T(8,128)(2,1)S(1)} %get-tuple-element.15), channel_id=1, source_target_pairs={{0,8},{4,12},{8,4},{12,0},{1,9},{5,13},{9,5},{13,1},{2,10},{6,14},... | collective-permute-start | bytes 393224 | tf_op jit(solution)/shard_map/ppermute | solution.py:354
  8.0 4.5 %collective-permute-start.4 = (bf16[32,1024]{1,0:T(8,128)(2,1)S(1)}, bf16[32,1024]{1,0:T(8,128)(2,1)S(1)}, u32[]{:S(2)}, u32[]{:S(2)}) collective-permute-start(bf16[32,1024]{1,0:T(8,128)(2,1)S(1)} %get-tuple-element.11.refs_0_), channel_id=1, source_target_pairs={{0,1},{1,0},{2,3},{3,2},{4,5},{5,4},{6,7},{7,6},{8,9},{9,8},{10,11... | collective-permute-start | bytes 196616 | tf_op jit(solution)/shard_map/ppermute | solution.py:351
  9.6 4.3 %collective-permute-start.5 = (bf16[32,1024]{1,0:T(8,128)(2,1)S(1)}, bf16[32,1024]{1,0:T(8,128)(2,1)S(1)}, u32[]{:S(2)}, u32[]{:S(2)}) collective-permute-start(bf16[32,1024]{1,0:T(8,128)(2,1)S(1)} %collective-permute-done.3.refs_5_), channel_id=1, source_target_pairs={{0,1},{1,0},{2,3},{3,2},{4,5},{5,4},{6,7},{7,6},{8,9},{9,8},{10,11... | collective-permute-start | bytes 196616 | tf_op jit(solution)/shard_map/ppermute | solution.py:351
  14.4 6.4 %collective-permute-start.8 = (s16[144,128]{1,0:T(8,128)(2,1)S(1)}, s16[144,128]{1,0:T(8,128)(2,1)S(1)}, u32[]{:S(2)}, u32[]{:S(2)}) collective-permute-start(s16[144,128]{1,0:T(8,128)(2,1)S(1)} %get-tuple-element.17.refs_0_), channel_id=1, source_target_pairs={{0,1},{1,3},{2,0},{3,2},{4,5},{5,7},{6,4},{7,6},{8,9},{9,11},{10,8... | collective-permute-start | bytes 110600 | tf_op jit(solution)/shard_map/ppermute | solution.py:351
  15.8 5.8 %collective-permute-start.7 = (s16[144,128]{1,0:T(8,128)(2,1)S(1)}, s16[144,128]{1,0:T(8,128)(2,1)S(1)}, u32[]{:S(2)}, u32[]{:S(2)}) collective-permute-start(s16[144,128]{1,0:T(8,128)(2,1)S(1)} %get-tuple-element.17.refs_0_), channel_id=1, source_target_pairs={{0,3},{1,2},{2,1},{3,0},{4,7},{5,6},{6,5},{7,4},{8,11},{9,10},{10,... | collective-permute-start | bytes 110600 | tf_op jit(solution)/shard_map/ppermute | solution.py:351
  18.0 4.0 %collective-permute-start.6 = (s16[144,128]{1,0:T(8,128)(2,1)S(1)}, s16[144,128]{1,0:T(8,128)(2,1)S(1)}, u32[]{:S(2)}, u32[]{:S(2)}) collective-permute-start(s16[144,128]{1,0:T(8,128)(2,1)S(1)} %get-tuple-element.17.refs_0_), channel_id=1, source_target_pairs={{0,2},{1,0},{2,3},{3,1},{4,6},{5,4},{6,7},{7,5},{8,10},{9,8},{10,1... | collective-permute-start | bytes 110600 | tf_op jit(solution)/shard_map/ppermute | solution.py:351
  20.1 1.9 %copy-start = (f32[128,128]{1,0:T(8,128)S(1)}, f32[128,128]{1,0:T(8,128)}, u32[]{:S(2)}) copy-start(f32[128,128]{1,0:T(8,128)} %diag_inverse.1) | copy-start | bytes 196612

commit v10 on v9

--- a/solution.py
+++ b/solution.py
@@ -272,11 +272,12 @@
         pieces.append(rest.astype(jnp.bfloat16))
         rest = rest - pieces[-1].astype(jnp.float32)
     own = factor[:, block(col_index, rows)]
-    value = 0.0
-    for piece in pieces[::-1]:
-        value = value + lax.dot_general(
-            piece, own, (((1,), (1,)), ((), ())), preferred_element_type=jnp.float32
-        )
+    value = lax.dot_general(
+        jnp.concatenate(pieces[::-1], axis=1),
+        jnp.concatenate([own] * len(pieces), axis=1),
+        (((1,), (1,)), ((), ())),
+        preferred_element_type=jnp.float32,
+    )
     largest = jnp.max(jnp.abs(value), axis=0, keepdims=True)
     exponent = jnp.floor(jnp.log2(jnp.maximum(largest, 2.0**-100)))
     scaled = jnp.round(value * jnp.exp2(14.0 - exponent))

time: 22.8 us -> 22.8 us (level)
  no operation moved by 1% of the time
where the time goes in v10:
time: 22.8 us; the launch traced here: 22.7 us
  starting transfers between devices  13.8 us (61%)
  waiting for transfers between devices  4.9 us (21%)
  Pallas kernels  2.45 us (11%)
  other arithmetic  0.73 us (3%)
  between operations  0.68 us (3%)
    ppermute x6, starting transfers between devices, moved(): return lax.ppermute(value, 'col', list(enumerate(moves[name])))  11.8 us
    ppermute x6, waiting for transfers between devices, moved(): return lax.ppermute(value, 'col', list(enumerate(moves[name])))  4.89 us
    ppermute x3, starting transfers between devices, crossed(): return lax.ppermute(value, 'row', list(enumerate(ROW_MOVES[m])))  2.03 us
    pallas_call x1, Pallas kernels, pack(): pl.pallas_call(lambda *refs: pack_kernel(row_count, col_count, *refs), ou...  1.18 us
    mul x1, other arithmetic, per_device(): mask[p:p + 1] * jnp.tile(solved[:, p * size:(p + 1) * size], (1, group))  0.73 us
    pallas_call x1, Pallas kernels, finish(): pl.pallas_call(finish_kernel, out_shape=jax.ShapeDtypeStruct(diag_inverse...  0.67 us
    pallas_call x1, Pallas kernels, solve(): pl.pallas_call(lambda *refs: solve_kernel(row_count, col_count, *refs), o...  0.59 us
  transfers between devices with their start and end apart: 9, of which 4 were waited for; matrix products, arithmetic and copies ran while one was open for 4% of the time, Pallas kernels for 0%

profile of v10, /device:TPU:0, one launch (start us, length us, event | category | flops | bytes accessed | tf_op | source)
XLA Modules:
  0.0 22.7 jit_solution(5643601584551584638)
XLA Ops:
  0.6 1.2 %pack.1 = (bf16[32,1024]{1,0:T(8,128)(2,1)S(1)}, f32[1,512]{1,0:T(1,128)S(1)}, bf16[256,256]{1,0:T(8,128)(2,1)S(1)}, bf16[256,256]{1,0:T(8,128)(2,1)S(1)}, bf16[...) custom-call(s32[4,8]{1,0:T(4,128)} %refs_0_.1, bf16[512,512]{1,0:T(8,128)(2,1)} %refs_1_.1, bf16[32,2048]{1,0:T(8,128)(2,1)} %refs_2_.1), custom_call_target="tpu_custom_call" | custom-call | tf_op jit(solution)/shard_map/pack/pallas_call | solution.py:225
  1.8 4.1 %collective-permute-start.3 = (bf16[32,1024]{1,0:T(8,128)(2,1)S(1)}, bf16[32,1024]{1,0:T(8,128)(2,1)S(1)}, u32[]{:S(2)}, u32[]{:S(2)}) collective-permute-start(bf16[32,1024]{1,0:T(8,128)(2,1)S(1)} %get-tuple-element.11.refs_0_), channel_id=1, source_target_pairs={{0,2},{1,3},{2,0},{3,1},{4,6},{5,7},{6,4},{7,5},{8,10},{9,11},{10,... | collective-permute-start | bytes 196616 | tf_op jit(solution)/shard_map/ppermute | solution.py:352
  5.9 0.7 %collective-permute-start = (bf16[256,256]{1,0:T(8,128)(2,1)S(1)}, bf16[256,256]{1,0:T(8,128)(2,1)S(1)}, u32[]{:S(2)}, u32[]{:S(2)}) collective-permute-start(bf16[256,256]{1,0:T(8,128)(2,1)S(1)} %get-tuple-element.13), channel_id=1, source_target_pairs={{0,12},{4,8},{8,0},{12,4},{1,13},{5,9},{9,1},{13,5},{2,14},{6,10},... | collective-permute-start | bytes 393224 | tf_op jit(solution)/shard_map/ppermute | solution.py:355
  6.6 1.0 %collective-permute-start.1 = (bf16[256,256]{1,0:T(8,128)(2,1)S(1)}, bf16[256,256]{1,0:T(8,128)(2,1)S(1)}, u32[]{:S(2)}, u32[]{:S(2)}) collective-permute-start(bf16[256,256]{1,0:T(8,128)(2,1)S(1)} %get-tuple-element.14), channel_id=1, source_target_pairs={{0,4},{4,0},{8,12},{12,8},{1,5},{5,1},{9,13},{13,9},{2,6},{6,2},{1... | collective-permute-start | bytes 393224 | tf_op jit(solution)/shard_map/ppermute | solution.py:355
  7.5 0.4 %collective-permute-start.2 = (bf16[256,256]{1,0:T(8,128)(2,1)S(1)}, bf16[256,256]{1,0:T(8,128)(2,1)S(1)}, u32[]{:S(2)}, u32[]{:S(2)}) collective-permute-start(bf16[256,256]{1,0:T(8,128)(2,1)S(1)} %get-tuple-element.15), channel_id=1, source_target_pairs={{0,8},{4,12},{8,4},{12,0},{1,9},{5,13},{9,5},{13,1},{2,10},{6,14},... | collective-permute-start | bytes 393224 | tf_op jit(solution)/shard_map/ppermute | solution.py:355
  8.0 1.6 %collective-permute-start.4 = (bf16[32,1024]{1,0:T(8,128)(2,1)S(1)}, bf16[32,1024]{1,0:T(8,128)(2,1)S(1)}, u32[]{:S(2)}, u32[]{:S(2)}) collective-permute-start(bf16[32,1024]{1,0:T(8,128)(2,1)S(1)} %get-tuple-element.11.refs_0_), channel_id=1, source_target_pairs={{0,1},{1,0},{2,3},{3,2},{4,5},{5,4},{6,7},{7,6},{8,9},{9,8},{10,11... | collective-permute-start | bytes 196616 | tf_op jit(solution)/shard_map/ppermute | solution.py:352
  9.5 0.0 collective-permute-done.3.refs_5_
  9.6 0.6 %collective-permute-start.5 = (bf16[32,1024]{1,0:T(8,128)(2,1)S(1)}, bf16[32,1024]{1,0:T(8,128)(2,1)S(1)}, u32[]{:S(2)}, u32[]{:S(2)}) collective-permute-start(bf16[32,1024]{1,0:T(8,128)(2,1)S(1)} %collective-permute-done.3.refs_5_), channel_id=1, source_target_pairs={{0,1},{1,0},{2,3},{3,2},{4,5},{5,4},{6,7},{7,6},{8,9},{9,8},{10,11... | collective-permute-start | bytes 196616 | tf_op jit(solution)/shard_map/ppermute | solution.py:352
  10.1 2.3 %collective-permute-done.4.refs_6_ = bf16[32,1024]{1,0:T(8,128)(2,1)S(1)} collective-permute-done((bf16[32,1024]{1,0:T(8,128)(2,1)S(1)}, bf16[32,1024]{1,0:T(8,128)(2,1)S(1)}, u32[]{:S(2)}, u32[]{:S(2)}) %collective-permute-start.4) | collective-permute-done | bytes 65568 | tf_op jit(solution)/shard_map/ppermute | solution.py:352
  12.4 1.4 %collective-permute-done.5.refs_7_ = bf16[32,1024]{1,0:T(8,128)(2,1)S(1)} collective-permute-done((bf16[32,1024]{1,0:T(8,128)(2,1)S(1)}, bf16[32,1024]{1,0:T(8,128)(2,1)S(1)}, u32[]{:S(2)}, u32[]{:S(2)}) %collective-permute-start.5) | collective-permute-done | bytes 65568 | tf_op jit(solution)/shard_map/ppermute | solution.py:352
  13.8 0.0 collective-permute-done.refs_2_
  13.8 0.0 collective-permute-done.1.refs_3_
  13.8 0.0 collective-permute-done.2.refs_4_
  13.9 0.6 %solve.1 = (f32[128,256]{1,0:T(8,128)S(1)}, s16[144,128]{1,0:T(8,128)(2,1)S(1)}) custom-call(bf16[32,1024]{1,0:T(8,128)(2,1)S(1)} %get-tuple-element.11.refs_0_, bf16[256,256]{1,0:T(8,128)(2,1)S(1)} %get-tuple-element.12.refs_1_, bf16[256,256]{1,0:T(8,128)(2,1)S(1)} %collective-permute-done.refs_2_, bf16[256,256]{1,0:T(8,128)(2,1)S(1)} %collective-permute-done.1.refs_3_, ...), custom_call_target="tpu_custom_call" | custom-call | tf_op jit(solution)/shard_map/solve/pallas_call | solution.py:295
  14.4 1.4 %collective-permute-start.8 = (s16[144,128]{1,0:T(8,128)(2,1)S(1)}, s16[144,128]{1,0:T(8,128)(2,1)S(1)}, u32[]{:S(2)}, u32[]{:S(2)}) collective-permute-start(s16[144,128]{1,0:T(8,128)(2,1)S(1)} %get-tuple-element.17.refs_0_), channel_id=1, source_target_pairs={{0,1},{1,3},{2,0},{3,2},{4,5},{5,7},{6,4},{7,6},{8,9},{9,11},{10,8... | collective-permute-start | bytes 110600 | tf_op jit(solution)/shard_map/ppermute | solution.py:352
  15.8 2.2 %collective-permute-start.7 = (s16[144,128]{1,0:T(8,128)(2,1)S(1)}, s16[144,128]{1,0:T(8,128)(2,1)S(1)}, u32[]{:S(2)}, u32[]{:S(2)}) collective-permute-start(s16[144,128]{1,0:T(8,128)(2,1)S(1)} %get-tuple-element.17.refs_0_), channel_id=1, source_target_pairs={{0,3},{1,2},{2,1},{3,0},{4,7},{5,6},{6,5},{7,4},{8,11},{9,10},{10,... | collective-permute-start | bytes 110600 | tf_op jit(solution)/shard_map/ppermute | solution.py:352
  18.1 1.9 %collective-permute-start.6 = (s16[144,128]{1,0:T(8,128)(2,1)S(1)}, s16[144,128]{1,0:T(8,128)(2,1)S(1)}, u32[]{:S(2)}, u32[]{:S(2)}) collective-permute-start(s16[144,128]{1,0:T(8,128)(2,1)S(1)} %get-tuple-element.17.refs_0_), channel_id=1, source_target_pairs={{0,2},{1,0},{2,3},{3,1},{4,6},{5,4},{6,7},{7,5},{8,10},{9,8},{10,1... | collective-permute-start | bytes 110600 | tf_op jit(solution)/shard_map/ppermute | solution.py:352
  20.0 0.1 tile.4
  20.1 0.0 copy-start
  20.1 0.7 %broadcast_multiply_fusion = f32[128,512]{1,0:T(8,128)} fusion(f32[128,512]{1,0:T(8,128)S(1)} %bitcast.4, f32[512]{0:T(512)S(1)} %bitcast.3), kind=kLoop, calls=%fused_computation | loop fusion | flops 65536 | bytes 526336 | tf_op jit(solution)/shard_map/mul | solution.py:368
  20.9 0.0 collective-permute-done.8.refs_3_
  20.9 0.7 %collective-permute-done.7.refs_2_ = s16[144,128]{1,0:T(8,128)(2,1)S(1)} collective-permute-done((s16[144,128]{1,0:T(8,128)(2,1)S(1)}, s16[144,128]{1,0:T(8,128)(2,1)S(1)}, u32[]{:S(2)}, u32[]{:S(2)}) %collective-permute-start.7) | collective-permute-done | bytes 36896 | tf_op jit(solution)/shard_map/ppermute | solution.py:352
  21.6 0.4 %collective-permute-done.6.refs_1_ = s16[144,128]{1,0:T(8,128)(2,1)S(1)} collective-permute-done((s16[144,128]{1,0:T(8,128)(2,1)S(1)}, s16[144,128]{1,0:T(8,128)(2,1)S(1)}, u32[]{:S(2)}, u32[]{:S(2)}) %collective-permute-start.6) | collective-permute-done | bytes 36896 | tf_op jit(solution)/shard_map/ppermute | solution.py:352
  22.0 0.0 copy-done
  22.0 0.7 %finish.1 = f32[128,128]{1,0:T(8,128)} custom-call(f32[128,128]{1,0:T(8,128)S(1)} %copy-done, s16[144,128]{1,0:T(8,128)(2,1)S(1)} %get-tuple-element.17.refs_0_, s16[144,128]{1,0:T(8,128)(2,1)S(1)} %collective-permute-done.6.refs_1_, s16[144,128]{1,0:T(8,128)(2,1)S(1)} %collective-permute-done.7.refs_2_, s16[144,128]{1,0:T(8,128)(2,1)S(1)} %collective-permute-done.8.refs_3_), custom_call_target="tpu_custom_call" | custom-call | tf_op jit(solution)/shard_map/finish/pallas_call | solution.py:321
  (1 shorter events, 0.0 us)
Async XLA Ops:
  1.8 7.8 %collective-permute-start.3 = (bf16[32,1024]{1,0:T(8,128)(2,1)S(1)}, bf16[32,1024]{1,0:T(8,128)(2,1)S(1)}, u32[]{:S(2)}, u32[]{:S(2)}) collective-permute-start(bf16[32,1024]{1,0:T(8,128)(2,1)S(1)} %get-tuple-element.11.refs_0_), channel_id=1, source_target_pairs={{0,2},{1,3},{2,0},{3,1},{4,6},{5,7},{6,4},{7,5},{8,10},{9,11},{10,... | collective-permute-start | bytes 196616 | tf_op jit(solution)/shard_map/ppermute | solution.py:352
  5.9 7.9 %collective-permute-start = (bf16[256,256]{1,0:T(8,128)(2,1)S(1)}, bf16[256,256]{1,0:T(8,128)(2,1)S(1)}, u32[]{:S(2)}, u32[]{:S(2)}) collective-permute-start(bf16[256,256]{1,0:T(8,128)(2,1)S(1)} %get-tuple-element.13), channel_id=1, source_target_pairs={{0,12},{4,8},{8,0},{12,4},{1,13},{5,9},{9,1},{13,5},{2,14},{6,10},... | collective-permute-start | bytes 393224 | tf_op jit(solution)/shard_map/ppermute | solution.py:355
  6.6 7.3 %collective-permute-start.1 = (bf16[256,256]{1,0:T(8,128)(2,1)S(1)}, bf16[256,256]{1,0:T(8,128)(2,1)S(1)}, u32[]{:S(2)}, u32[]{:S(2)}) collective-permute-start(bf16[256,256]{1,0:T(8,128)(2,1)S(1)} %get-tuple-element.14), channel_id=1, source_target_pairs={{0,4},{4,0},{8,12},{12,8},{1,5},{5,1},{9,13},{13,9},{2,6},{6,2},{1... | collective-permute-start | bytes 393224 | tf_op jit(solution)/shard_map/ppermute | solution.py:355
  7.5 6.3 %collective-permute-start.2 = (bf16[256,256]{1,0:T(8,128)(2,1)S(1)}, bf16[256,256]{1,0:T(8,128)(2,1)S(1)}, u32[]{:S(2)}, u32[]{:S(2)}) collective-permute-start(bf16[256,256]{1,0:T(8,128)(2,1)S(1)} %get-tuple-element.15), channel_id=1, source_target_pairs={{0,8},{4,12},{8,4},{12,0},{1,9},{5,13},{9,5},{13,1},{2,10},{6,14},... | collective-permute-start | bytes 393224 | tf_op jit(solution)/shard_map/ppermute | solution.py:355
  8.0 4.5 %collective-permute-start.4 = (bf16[32,1024]{1,0:T(8,128)(2,1)S(1)}, bf16[32,1024]{1,0:T(8,128)(2,1)S(1)}, u32[]{:S(2)}, u32[]{:S(2)}) collective-permute-start(bf16[32,1024]{1,0:T(8,128)(2,1)S(1)} %get-tuple-element.11.refs_0_), channel_id=1, source_target_pairs={{0,1},{1,0},{2,3},{3,2},{4,5},{5,4},{6,7},{7,6},{8,9},{9,8},{10,11... | collective-permute-start | bytes 196616 | tf_op jit(solution)/shard_map/ppermute | solution.py:352
  9.6 4.3 %collective-permute-start.5 = (bf16[32,1024]{1,0:T(8,128)(2,1)S(1)}, bf16[32,1024]{1,0:T(8,128)(2,1)S(1)}, u32[]{:S(2)}, u32[]{:S(2)}) collective-permute-start(bf16[32,1024]{1,0:T(8,128)(2,1)S(1)} %collective-permute-done.3.refs_5_), channel_id=1, source_target_pairs={{0,1},{1,0},{2,3},{3,2},{4,5},{5,4},{6,7},{7,6},{8,9},{9,8},{10,11... | collective-permute-start | bytes 196616 | tf_op jit(solution)/shard_map/ppermute | solution.py:352
  14.4 6.4 %collective-permute-start.8 = (s16[144,128]{1,0:T(8,128)(2,1)S(1)}, s16[144,128]{1,0:T(8,128)(2,1)S(1)}, u32[]{:S(2)}, u32[]{:S(2)}) collective-permute-start(s16[144,128]{1,0:T(8,128)(2,1)S(1)} %get-tuple-element.17.refs_0_), channel_id=1, source_target_pairs={{0,1},{1,3},{2,0},{3,2},{4,5},{5,7},{6,4},{7,6},{8,9},{9,11},{10,8... | collective-permute-start | bytes 110600 | tf_op jit(solution)/shard_map/ppermute | solution.py:352
  15.8 5.8 %collective-permute-start.7 = (s16[144,128]{1,0:T(8,128)(2,1)S(1)}, s16[144,128]{1,0:T(8,128)(2,1)S(1)}, u32[]{:S(2)}, u32[]{:S(2)}) collective-permute-start(s16[144,128]{1,0:T(8,128)(2,1)S(1)} %get-tuple-element.17.refs_0_), channel_id=1, source_target_pairs={{0,3},{1,2},{2,1},{3,0},{4,7},{5,6},{6,5},{7,4},{8,11},{9,10},{10,... | collective-permute-start | bytes 110600 | tf_op jit(solution)/shard_map/ppermute | solution.py:352
  18.1 4.0 %collective-permute-start.6 = (s16[144,128]{1,0:T(8,128)(2,1)S(1)}, s16[144,128]{1,0:T(8,128)(2,1)S(1)}, u32[]{:S(2)}, u32[]{:S(2)}) collective-permute-start(s16[144,128]{1,0:T(8,128)(2,1)S(1)} %get-tuple-element.17.refs_0_), channel_id=1, source_target_pairs={{0,2},{1,0},{2,3},{3,1},{4,6},{5,4},{6,7},{7,5},{8,10},{9,8},{10,1... | collective-permute-start | bytes 110600 | tf_op jit(solution)/shard_map/ppermute | solution.py:352
  20.1 1.9 %copy-start = (f32[128,128]{1,0:T(8,128)S(1)}, f32[128,128]{1,0:T(8,128)}, u32[]{:S(2)}) copy-start(f32[128,128]{1,0:T(8,128)} %diag_inverse.1) | copy-start | bytes 196612
